TPU v7x, 128 devices: a whole 4x4x4 slice. The times are simulated.
128 devices in a mesh: res: 32 (over x, y, core), head: 4 (over z).
Axes of the slice: x: 4, y: 4, z: 4, core: 2. Of those that a mesh axis runs over, the one named last changes fastest.
Arguments:
- queries: bfloat16 [8192, 3072], P(('res', 'head'))
- keys: bfloat16 [8192, 3072], P(('res', 'head'))
- values: bfloat16 [8192, 3072], P(('res', 'head')), may hold values from -6 to 6
- out_grad: bfloat16 [8192, 3072], P('res', 'head'), may hold values from -6 to 6
- chain_bias: float32 [24], P('head'), may hold values from -2 to 1
- chain_of_block: int32 [64], P('res'), may hold values from 0 to 15, never falling along the last dimension, each value on 1 to 8 neighbouring positions
- key_valid: int32 [8192], P('res'), may hold values from 0 to 1, as said below
- neighbours: int32 [64, 16], P('res'), may hold values from 0 to 63, as said below
Outputs:
- attended: bfloat16 [8192, 3072], P('res', 'head')
- query_grad: bfloat16 [8192, 3072], P(('res', 'head'))
- key_grad: bfloat16 [8192, 3072], P(('res', 'head'))
- value_grad: bfloat16 [8192, 3072], P(('res', 'head'))
Inputs may be any that keep to these rules, and one draw needn't show every extreme that they name: `neighbours`: each row b lists 16 distinct blocks, b itself among them. Over the 2 blocks of one group, the distinct blocks listed from any one other group number at most 1, and exactly 1 for some pair of groups in every draw. `key_valid`: residues 0 and 1 of every block hold 1.
All inputs are finite; a program needn't handle non-finite values.
Results may differ from a plain program's by a relative error of at most 0.012.
The roundings to bfloat16 on the way count: a program that leaves them out, or rounds other values in their place, can miss the bound.
Values may be sent and summed in bfloat16 or wider, within the bound.
No kernel may reach another device: no remote copies, remote signals or barrier semaphores. Data moves between devices by JAX's collectives and lax.ppermute only.
A program may use at most 192 MiB of HBM per device.

v0:
```python
import math

import jax
import jax.numpy as jnp
from jax import lax
from jax.sharding import PartitionSpec as P

HD = 128
NBR = 16


def slot_table(neighbours, own_group, n_res, blocks_here, capacity):
    owners = neighbours // blocks_here
    local_id = neighbours % blocks_here
    remote = owners != own_group
    flat_owner = owners.reshape(-1)
    flat_local = local_id.reshape(-1)
    flat_remote = remote.reshape(-1)
    by_owner = flat_owner[:, None] == jnp.arange(n_res, dtype=jnp.int32)[None, :]
    by_local = flat_local[:, None] == jnp.arange(blocks_here, dtype=jnp.int32)[None, :]
    present = jnp.any(
        by_owner[:, :, None] & by_local[:, None, :] & flat_remote[:, None, None], axis=0
    )
    ranks = jnp.cumsum(present.astype(jnp.int32), axis=1) - 1
    slots = jnp.arange(capacity, dtype=jnp.int32)
    placed = present[:, :, None] & (ranks[:, :, None] == slots[None, None, :])
    labels = jnp.arange(blocks_here, dtype=jnp.int32)[None, :, None] + 1
    requests = jnp.sum(jnp.where(placed, labels, 0), axis=1) - 1
    entry_rank = ranks[owners, local_id]
    table_index = jnp.where(remote, blocks_here + owners * capacity + entry_rank, local_id)
    return (requests, table_index)


def fetch_blocks(requests_in, key_blocks, value_blocks, key_codes, table_index, n_res, capacity):
    blocks_here, rows_block, width = key_blocks.shape
    picked = jnp.clip(requests_in, 0, blocks_here - 1)
    live = requests_in >= 0
    key_send = jnp.where(live[:, :, None, None], jnp.take(key_blocks, picked, axis=0), 0)
    value_send = jnp.where(live[:, :, None, None], jnp.take(value_blocks, picked, axis=0), 0)
    code_send = jnp.where(live[:, :, None], jnp.take(key_codes, picked, axis=0), -1)
    key_recv, value_recv, code_recv = (
        lax.all_to_all(key_send, "res", split_axis=0, concat_axis=0, tiled=True),
        lax.all_to_all(value_send, "res", split_axis=0, concat_axis=0, tiled=True),
        lax.all_to_all(code_send, "res", split_axis=0, concat_axis=0, tiled=True),
    )
    key_table = jnp.concatenate(
        [key_blocks, key_recv.reshape(n_res * capacity, rows_block, width)], axis=0
    )
    value_table = jnp.concatenate(
        [value_blocks, value_recv.reshape(n_res * capacity, rows_block, width)], axis=0
    )
    code_table = jnp.concatenate(
        [key_codes, code_recv.reshape(n_res * capacity, rows_block)], axis=0
    )
    flat = table_index.reshape(-1)
    key_near = jnp.take(key_table, flat, axis=0).reshape(blocks_here, -1, width)
    value_near = jnp.take(value_table, flat, axis=0).reshape(blocks_here, -1, width)
    code_near = jnp.take(code_table, flat, axis=0).reshape(blocks_here, -1).astype(jnp.float32)
    return (key_near, value_near, code_near)


def head_weights(query_head, key_head, bias_value, cross, valid):
    scale = 1.0 / math.sqrt(HD)
    scores = (
        jnp.einsum("jqd,jkd->jqk", query_head, key_head, preferred_element_type=jnp.float32) * scale
    )
    scores = scores + bias_value * cross[:, None, :]
    scores = jnp.where(valid[:, None, :], scores, -jnp.inf)
    peak = jnp.max(scores, axis=-1, keepdims=True)
    weights = jnp.exp(scores - peak)
    total = jnp.sum(weights, axis=-1, keepdims=True)
    return (weights, total)


def forward_heads(query_blocks, near, chain_bias, query_chain, heads_here):
    key_near, value_near, code_near = near
    valid = code_near >= 0
    cross = (code_near != query_chain[:, None]).astype(jnp.float32)

    def one_head(head_index, output):
        start = head_index * HD
        query_head = lax.dynamic_slice_in_dim(query_blocks, start, HD, 2)
        key_head = lax.dynamic_slice_in_dim(key_near, start, HD, 2)
        value_head = lax.dynamic_slice_in_dim(value_near, start, HD, 2)
        weights, total = head_weights(query_head, key_head, chain_bias[head_index], cross, valid)
        rounded = weights.astype(jnp.bfloat16)
        mixed = (
            jnp.einsum("jqk,jkd->jqd", rounded, value_head, preferred_element_type=jnp.float32)
            / total
        )
        return lax.dynamic_update_slice_in_dim(output, mixed.astype(jnp.bfloat16), start, 2)

    return lax.fori_loop(0, heads_here, one_head, jnp.zeros(query_blocks.shape, jnp.bfloat16))


def head_backward(
    query_blocks,
    grad_blocks,
    attended,
    key_near,
    value_near,
    bias_value,
    cross,
    valid,
    start,
    entries,
    table_rows,
):
    rows_block = query_blocks.shape[1]
    scale = 1.0 / math.sqrt(HD)
    query_head = query_blocks[:, :, start : start + HD]
    key_head = key_near[:, :, start : start + HD]
    value_head = value_near[:, :, start : start + HD]
    grad_head = grad_blocks[:, :, start : start + HD]
    output_head = attended[:, :, start : start + HD]
    weights, total = head_weights(query_head, key_head, bias_value, cross, valid)
    probs = weights / total
    delta = jnp.sum(
        grad_head.astype(jnp.float32) * output_head.astype(jnp.float32), axis=-1, keepdims=True
    )
    dprob = jnp.einsum("jqd,jkd->jqk", grad_head, value_head, preferred_element_type=jnp.float32)
    dscore = (probs * (dprob - delta)).astype(jnp.bfloat16)
    probs_round = probs.astype(jnp.bfloat16)
    query_part = (
        jnp.einsum("jqk,jkd->jqd", dscore, key_head, preferred_element_type=jnp.float32) * scale
    )
    key_entries = (
        jnp.einsum("jqk,jqd->jkd", dscore, query_head, preferred_element_type=jnp.float32) * scale
    )
    value_entries = jnp.einsum(
        "jqk,jqd->jkd", probs_round, grad_head, preferred_element_type=jnp.float32
    )
    blank_slab = jnp.zeros((table_rows, rows_block, HD), jnp.float32)
    key_slab = blank_slab.at[entries].add(key_entries.reshape(-1, rows_block, HD))
    value_slab = blank_slab.at[entries].add(value_entries.reshape(-1, rows_block, HD))
    return (query_part.astype(jnp.bfloat16), key_slab, value_slab)


def fold_back(receiving, arrived):
    rows_block = arrived.shape[2]
    features = arrived.shape[3]
    return jnp.einsum(
        "sl,sbf->lbf",
        receiving,
        arrived.reshape(-1, rows_block, features),
        preferred_element_type=jnp.float32,
    )


def body(queries, keys, values, out_grad, chain_bias, chain_of_block, key_valid, neighbours):
    n_res = lax.axis_size("res")
    own_group = lax.axis_index("res")
    blocks_here = chain_of_block.shape[0]
    rows_block = key_valid.shape[0] // blocks_here
    capacity = (NBR - blocks_here + n_res - 2) // (n_res - 1)
    table_rows = blocks_here + n_res * capacity
    query_rows, key_rows, value_rows = (
        lax.all_to_all(queries, "head", split_axis=1, concat_axis=0, tiled=True),
        lax.all_to_all(keys, "head", split_axis=1, concat_axis=0, tiled=True),
        lax.all_to_all(values, "head", split_axis=1, concat_axis=0, tiled=True),
    )
    width = query_rows.shape[1]
    heads_here = width // HD
    query_blocks = query_rows.reshape(blocks_here, rows_block, width)
    key_blocks = key_rows.reshape(blocks_here, rows_block, width)
    value_blocks = value_rows.reshape(blocks_here, rows_block, width)
    grad_blocks = out_grad.reshape(blocks_here, rows_block, width)
    key_codes = jnp.where(
        key_valid.reshape(blocks_here, rows_block) == 1, chain_of_block[:, None], -1
    )
    key_codes = key_codes.astype(jnp.float32).astype(jnp.bfloat16)
    query_chain = chain_of_block.astype(jnp.float32)
    requests, table_index = slot_table(neighbours, own_group, n_res, blocks_here, capacity)
    requests_in = lax.all_to_all(requests, "res", split_axis=0, concat_axis=0, tiled=True)
    near = fetch_blocks(
        requests_in, key_blocks, value_blocks, key_codes, table_index, n_res, capacity
    )
    attended = forward_heads(query_blocks, near, chain_bias, query_chain, heads_here)
    key_near, value_near, code_near = near
    valid = code_near >= 0
    cross = (code_near != query_chain[:, None]).astype(jnp.float32)
    entries = table_index.reshape(-1)
    receiving = (
        requests_in.reshape(-1)[:, None] == jnp.arange(blocks_here, dtype=jnp.int32)[None, :]
    ).astype(jnp.bfloat16)
    query_pieces = []
    key_pieces = []
    value_pieces = []
    for head_index in range(heads_here):
        start = head_index * HD
        query_part, key_slab, value_slab = head_backward(
            query_blocks,
            grad_blocks,
            attended,
            key_near,
            value_near,
            chain_bias[head_index],
            cross,
            valid,
            start,
            entries,
            table_rows,
        )
        query_pieces.append(query_part)
        key_pieces.append(key_slab)
        value_pieces.append(value_slab)
    query_grad = jnp.concatenate(query_pieces, axis=2)
    key_table = jnp.concatenate(key_pieces, axis=2)
    value_table = jnp.concatenate(value_pieces, axis=2)
    key_remote = (
        key_table[blocks_here:].reshape(n_res, capacity, rows_block, width).astype(jnp.bfloat16)
    )
    value_remote = (
        value_table[blocks_here:].reshape(n_res, capacity, rows_block, width).astype(jnp.bfloat16)
    )
    key_arrived, value_arrived = (
        lax.all_to_all(key_remote, "res", split_axis=0, concat_axis=0, tiled=True),
        lax.all_to_all(value_remote, "res", split_axis=0, concat_axis=0, tiled=True),
    )
    key_total = key_table[:blocks_here] + fold_back(receiving, key_arrived)
    value_total = value_table[:blocks_here] + fold_back(receiving, value_arrived)
    key_grad = key_total.astype(jnp.bfloat16).reshape(-1, width)
    value_grad = value_total.astype(jnp.bfloat16).reshape(-1, width)
    query_out, key_out, value_out = (
        lax.all_to_all(
            query_grad.reshape(-1, width), "head", split_axis=0, concat_axis=1, tiled=True
        ),
        lax.all_to_all(key_grad, "head", split_axis=0, concat_axis=1, tiled=True),
        lax.all_to_all(value_grad, "head", split_axis=0, concat_axis=1, tiled=True),
    )
    return (attended.reshape(-1, width), query_out, key_out, value_out)


def solution(mesh):
    return jax.shard_map(
        body,
        mesh=mesh,
        in_specs=(
            P(("res", "head"), None),
            P(("res", "head"), None),
            P(("res", "head"), None),
            P("res", "head"),
            P("head"),
            P("res"),
            P("res"),
            P("res", None),
        ),
        out_specs=(
            P("res", "head"),
            P(("res", "head"), None),
            P(("res", "head"), None),
            P(("res", "head"), None),
        ),
        check_vma=False,
    )
```

profile of v0, /device:TPU:8, one launch (start us, length us, event | category | flops | bytes accessed | tf_op | source)
XLA Modules:
  0.0 652.4 jit_solution(12655064570032550017)
XLA Ops:
  2.6 7.5 %all-to-all-start = ((s32[32,1,1]{2,1,0:T(1,128)}), s32[32,1,1]{2,1,0:T(1,128)S(1)}, u32[]{:S(2)}, u32[]{:S(2)}) async-start(s32[32,1,1]{2,1,0:T(1,128)} %copy.174), calls=%async_computation | async-start | bytes 32768 | tf_op jit(solution)/shard_map/all_to_all | solution.py:174
  16.2 5.3 all-to-all-start.5
  40.5 5.9 all-to-all-start.1
  50.0 10.7 %fusion.26 = (bf16[32,1,128,768]{3,2,1,0:T(8,128)(2,1)}, bf16[32,1,128,768]{3,2,1,0:T(8,128)(2,1)}) fusion(bf16[32,128,768]{2,1,0:T(8,128)(2,1)} %gather_fusion.5, pred[32]{0:T(512)(128)(4,1)S(1)} %and_bitcast_fusion, pred[32]{0:T(512)(128)(4,1)S(1)} %broadcast_compare_fusion.3, bf16[32,128,768]{2,1,0:T(8,128)(2,1)} %gather_fusion.3), kind=kLoop, calls=%fused_computation.53 | loop fusion | flops 12582912 | bytes 25165888 | tf_op jit(solution)/shard_map/jit(_where)/select_n | solution.py:39
  60.7 79.2 %all_to_all.139 = bf16[32,1,128,768]{3,2,1,0:T(8,128)(2,1)} all-to-all(bf16[32,1,128,768]{3,2,1,0:T(8,128)(2,1)} %get-tuple-element.187), channel_id=1, replica_groups=mesh['res'=32,'head'=4] {'res'}, dimensions={0} | all-to-all | bytes 12582912 | tf_op jit(solution)/shard_map/all_to_all | solution.py:43
  139.9 6.1 all-to-all-start.4
  153.3 6.1 pad_maximum_fusion.1
  159.4 73.7 %all-to-all-done.4 = bf16[32,1,128,768]{3,2,1,0:T(8,128)(2,1)} async-done(((bf16[32,1,128,768]{3,2,1,0:T(8,128)(2,1)}), bf16[32,1,128,768]{3,2,1,0:T(8,128)(2,1)}, u32[]{:S(2)}, u32[]{:S(2)}) %all-to-all-start.4) | async-done | bytes 6291488 | tf_op jit(solution)/shard_map/all_to_all | solution.py:42
  236.8 6.1 pad_maximum_fusion
  242.9 6.4 gather_fusion.6
  249.4 6.5 gather_fusion.4
  255.9 10.7 %broadcast_select_fusion = (bf16[32,128,768]{2,1,0:T(8,128)(2,1)}, bf16[32,128,768]{2,1,0:T(8,128)(2,1)}) fusion(bf16[32,128,768]{2,1,0:T(8,128)(2,1)} %gather_fusion.6, pred[32]{0:T(512)(128)(4,1)S(1)} %compare_and_fusion, bf16[32,128,768]{2,1,0:T(8,128)(2,1)} %gather_fusion.4), kind=kLoop, calls=%fused_computation.59 | loop fusion | flops 6291456 | bytes 25165856 | tf_op jit(solution)/shard_map/jit(_take)/select_n | solution.py:57
  266.6 31.7 %while.13 = (s32[]{:T(128)}, bf16[2,128,768]{2,1,0:T(8,128)(2,1)S(1)}, pred[2,2048]{1,0:T(4,128)(4,1)S(1)}, bf16[2,128,768]{2,1,0:T(8,128)(2,1)S(1)}, bf16[2,204...) while((s32[]{:T(128)}, ...), condition=%wide.region_6.9_spmd, body=%wide.region_3.8_spmd.sunk | while | flops 272698880 | bytes 8584379 | solution.py:93
  385.6 4.9 scatter_fusion.4
  401.3 10.2 %fusion.19 = bf16[32,1,128,768]{3,0,2,1:T(8,128)(2,1)} fusion(f32[34,128,768]{2,0,1:T(8,128)} %copy_dynamic-update-slice_fusion.6), kind=kLoop, calls=%fused_computation.45 | loop fusion | bytes 12582912 | tf_op jit(solution)/shard_map/convert_element_type | solution.py:211
  411.5 8.9 %copy.201 = bf16[32,1,128,768]{3,2,1,0:T(8,128)(2,1)} copy(bf16[32,1,128,768]{3,0,2,1:T(8,128)(2,1)} %fusion.19) | data formatting | bytes 12582912 | tf_op jit(solution)/shard_map/convert_element_type | solution.py:211
  420.4 5.1 all-to-all-start.8
  430.3 6.2 scatter_fusion.6
  441.3 6.3 scatter_fusion.7
  452.3 6.2 scatter_fusion.8
  463.3 6.2 scatter_fusion.9
  474.3 6.3 scatter_fusion.10
  486.6 7.3 %scatter_fusion.11 = f32[34,128,128]{2,1,0:T(8,128)} fusion(f32[34,128,128]{2,1,0:T(8,128)} %broadcast.480.clone.11, s32[32]{0:T(128)S(1)} %fusion.282, f32[32,128,128]{2,1,0:T(8,128)} %bitcast.275), kind=kCustom, calls=%fused_computation.18 | custom fusion | flops 524288 | bytes 6291584 | tf_op jit(solution)/shard_map/scatter-add | solution.py:135
  511.7 10.1 %fusion.20 = bf16[32,1,128,768]{3,0,2,1:T(8,128)(2,1)} fusion(f32[34,128,768]{2,0,1:T(8,128)} %copy_dynamic-update-slice_fusion), kind=kLoop, calls=%fused_computation.46 | loop fusion | bytes 12582912 | tf_op jit(solution)/shard_map/convert_element_type | solution.py:214
  521.8 9.1 %copy.211 = bf16[32,1,128,768]{3,2,1,0:T(8,128)(2,1)} copy(bf16[32,1,128,768]{3,0,2,1:T(8,128)(2,1)} %fusion.20) | data formatting | bytes 12582912 | tf_op jit(solution)/shard_map/convert_element_type | solution.py:214
  530.9 6.4 all-to-all-start.10
  537.4 8.4 %fusion.94 = bf16[2,128,768]{2,0,1:T(2,128)(2,1)S(1)} fusion(bf16[32,1,128,768]{3,2,1,0:T(8,128)(2,1)} %all-to-all-done.8, f32[34,128,768]{2,0,1:T(8,128)} %copy_dynamic-update-slice_fusion.6, s32[32]{0:T(128)S(1)} %copy-done.13), kind=kOutput, calls=%fused_computation.158 | convolution fusion | flops 12976192 | bytes 7471232 | tf_op jit(solution)/shard_map/sl,sbf->lbf/dot_general | solution.py:142
  546.6 78.4 %all-to-all-done.10 = bf16[32,1,128,768]{3,2,1,0:T(8,128)(2,1)} async-done(((bf16[32,1,128,768]{3,2,1,0:T(8,128)(2,1)}), bf16[32,1,128,768]{3,2,1,0:T(8,128)(2,1)}, u32[]{:S(2)}, u32[]{:S(2)}) %all-to-all-start.10) | async-done | bytes 6291488 | tf_op jit(solution)/shard_map/all_to_all | solution.py:218
  624.9 5.1 all-to-all-start.9
  630.0 8.4 %fusion.100 = bf16[2,128,768]{2,0,1:T(2,128)(2,1)S(1)} fusion(bf16[32,1,128,768]{3,2,1,0:T(8,128)(2,1)} %all-to-all-done.10, f32[34,128,768]{2,0,1:T(8,128)} %copy_dynamic-update-slice_fusion, s32[32]{0:T(128)S(1)} %copy-done.13), kind=kOutput, calls=%fused_computation.160 | convolution fusion | flops 12976192 | bytes 7471232 | tf_op jit(solution)/shard_map/sl,sbf->lbf/dot_general | solution.py:142
  639.2 4.8 all-to-all-start.11
  645.5 5.8 all-to-all-done.11
  (192 shorter events, 222.2 us)
Async XLA Ops:
  2.6 13.6 %all-to-all-start = ((s32[32,1,1]{2,1,0:T(1,128)}), s32[32,1,1]{2,1,0:T(1,128)S(1)}, u32[]{:S(2)}, u32[]{:S(2)}) async-start(s32[32,1,1]{2,1,0:T(1,128)} %copy.174), calls=%async_computation | async-start | bytes 32768 | tf_op jit(solution)/shard_map/all_to_all | solution.py:174
  16.2 13.4 %all-to-all-start.5 = ((bf16[64,4,768]{2,0,1:T(8,128)(2,1)}), bf16[64,4,768]{2,0,1:T(8,128)(2,1)S(1)}, u32[]{:S(2)}, u32[]{:S(2)}) async-start(bf16[64,4,768]{2,0,1:T(8,128)(2,1)} %bitcast.255), calls=%async_computation.5 | async-start | bytes 786432 | tf_op jit(solution)/shard_map/all_to_all | solution.py:160
  25.4 11.4 %copy-start.12 = (s32[32]{0:T(128)}, s32[32]{0:T(128)S(1)}, u32[]{:S(2)}) copy-start(s32[32]{0:T(128)S(1)} %get-tuple-element.152) | copy-start | bytes 388
  29.6 10.8 %all-to-all-start.3 = ((bf16[64,4,768]{2,0,1:T(8,128)(2,1)}), bf16[64,4,768]{2,0,1:T(8,128)(2,1)S(1)}, u32[]{:S(2)}, u32[]{:S(2)}) async-start(bf16[64,4,768]{2,0,1:T(8,128)(2,1)} %bitcast.256), calls=%async_computation.3 | async-start | bytes 786432 | tf_op jit(solution)/shard_map/all_to_all | solution.py:159
  40.5 20.3 %all-to-all-start.1 = ((bf16[32,1,128]{2,1,0:T(2,128)(2,1)}), bf16[32,1,128]{2,1,0:T(2,128)(2,1)S(1)}, u32[]{:S(2)}, u32[]{:S(2)}) async-start(bf16[32,1,128]{2,1,0:T(2,128)(2,1)} %copy.175), calls=%async_computation.1 | async-start | bytes 32768 | tf_op jit(solution)/shard_map/all_to_all | solution.py:44
  139.9 7.3 %copy-start.14 = (s32[2]{0:T(128)S(1)}, s32[2]{0:T(128)}, u32[]{:S(2)}) copy-start(s32[2]{0:T(128)} %param.19) | copy-start | bytes 28
  139.9 7.3 %copy-start.8 = (bf16[64,3072]{1,0:T(8,128)(2,1)S(1)}, bf16[64,3072]{1,0:T(8,128)(2,1)}, u32[]{:S(2)}) copy-start(bf16[64,3072]{1,0:T(8,128)(2,1)} %param.14) | copy-start | bytes 1179652
  139.9 8.1 %copy-start.11 = (f32[6]{0:T(128)S(1)}, f32[6]{0:T(128)}, u32[]{:S(2)}) copy-start(f32[6]{0:T(128)} %param.18) | copy-start | bytes 76
  139.9 93.2 %all-to-all-start.4 = ((bf16[32,1,128,768]{3,2,1,0:T(8,128)(2,1)}), bf16[32,1,128,768]{3,2,1,0:T(8,128)(2,1)}, u32[]{:S(2)}, u32[]{:S(2)}) async-start(bf16[32,1,128,768]{3,2,1,0:T(8,128)(2,1)} %get-tuple-element.188), calls=%async_computation.4 | async-start | bytes 12582912 | tf_op jit(solution)/shard_map/all_to_all | solution.py:42
  233.1 33.4 %all-to-all-start.2 = ((bf16[64,4,768]{2,0,1:T(8,128)(2,1)}), bf16[64,4,768]{2,0,1:T(8,128)(2,1)S(1)}, u32[]{:S(2)}, u32[]{:S(2)}) async-start(bf16[64,4,768]{2,0,1:T(8,128)(2,1)} %bitcast.257), calls=%async_computation.2 | async-start | bytes 786432 | tf_op jit(solution)/shard_map/all_to_all | solution.py:158
  298.3 3.2 copy-start.7
  298.3 41.5 %copy-start.10 = (pred[2,2048]{1,0:T(4,128)(4,1)}, pred[2,2048]{1,0:T(4,128)(4,1)S(1)}, u32[]{:S(2)}) copy-start(pred[2,2048]{1,0:T(4,128)(4,1)S(1)} %get-tuple-element.313) | copy-start | bytes 12292
  298.3 46.1 %copy-start.6 = (bf16[2,128,768]{2,1,0:T(8,128)(2,1)}, bf16[2,128,768]{2,1,0:T(8,128)(2,1)S(1)}, u32[]{:S(2)}) copy-start(bf16[2,128,768]{2,1,0:T(8,128)(2,1)S(1)} %get-tuple-element.309) | copy-start | bytes 1179652
  298.3 3.2 copy-start.9
  348.9 71.6 %all-to-all-start.7 = ((bf16[4,64,768]{2,1,0:T(8,128)(2,1)}), bf16[4,64,768]{2,1,0:T(8,128)(2,1)S(1)}, u32[]{:S(2)}, u32[]{:S(2)}) async-start(bf16[4,64,768]{2,1,0:T(8,128)(2,1)} %bitcast.47), calls=%async_computation.7 | async-start | bytes 786432 | tf_op jit(solution)/shard_map/all_to_all | solution.py:225
  420.4 110.5 %all-to-all-start.8 = ((bf16[32,1,128,768]{3,2,1,0:T(8,128)(2,1)}), bf16[32,1,128,768]{3,2,1,0:T(8,128)(2,1)}, u32[]{:S(2)}, u32[]{:S(2)}) async-start(bf16[32,1,128,768]{3,2,1,0:T(8,128)(2,1)} %copy.201), calls=%async_computation.8 | async-start | bytes 12582912 | tf_op jit(solution)/shard_map/all_to_all | solution.py:217
  486.6 7.3 %copy-start.1 = (f32[34,128,128]{2,1,0:T(8,128)S(1)}, f32[34,128,128]{2,1,0:T(8,128)}, u32[]{:S(2)}) copy-start(f32[34,128,128]{2,1,0:T(8,128)} %scatter_fusion.6) | copy-start | bytes 6684676
  494.0 2.9 copy-start.2
  496.9 2.9 copy-start.3
  499.8 3.0 copy-start.4
  502.8 3.0 copy-start.5
  505.8 3.0 copy-start
  530.9 6.5 copy-start.13
  530.9 94.0 %all-to-all-start.10 = ((bf16[32,1,128,768]{3,2,1,0:T(8,128)(2,1)}), bf16[32,1,128,768]{3,2,1,0:T(8,128)(2,1)}, u32[]{:S(2)}, u32[]{:S(2)}) async-start(bf16[32,1,128,768]{3,2,1,0:T(8,128)(2,1)} %copy.211), calls=%async_computation.10 | async-start | bytes 12582912 | tf_op jit(solution)/shard_map/all_to_all | solution.py:218
  624.9 14.3 %all-to-all-start.9 = ((bf16[4,64,768]{2,1,0:T(8,128)(2,1)}), bf16[4,64,768]{2,1,0:T(8,128)(2,1)S(1)}, u32[]{:S(2)}, u32[]{:S(2)}) async-start(bf16[4,64,768]{2,1,0:T(8,128)(2,1)} %bitcast.58), calls=%async_computation.9 | async-start | bytes 786432 | tf_op jit(solution)/shard_map/all_to_all | solution.py:228
  639.2 12.2 %all-to-all-start.11 = ((bf16[4,64,768]{2,1,0:T(8,128)(2,1)}), bf16[4,64,768]{2,1,0:T(8,128)(2,1)S(1)}, u32[]{:S(2)}, u32[]{:S(2)}) async-start(bf16[4,64,768]{2,1,0:T(8,128)(2,1)} %bitcast.68), calls=%async_computation.11 | async-start | bytes 786432 | tf_op jit(solution)/shard_map/all_to_all | solution.py:229
where the time goes:
time: 662 us; the launch traced here: 652 us
  waiting for transfers between devices  167 us (25%)
  local copies, waits for them, and re-layouts  123 us (19%)
  other arithmetic  116 us (18%)
  matrix products  108 us (16%)
  blocking collectives  79.2 us (12%)
  starting transfers between devices  58.1 us (9%)
    all_to_all x1, blocking collectives, fetch_blocks(): lax.all_to_all(value_send, 'res', split_axis=0, concat_axis=0, tiled=True)  79.2 us
    all_to_all x1, waiting for transfers between devices, body(): lax.all_to_all(value_remote, 'res', split_axis=0, concat_axis=0, tiled=True)  78.4 us
    all_to_all x1, waiting for transfers between devices, fetch_blocks(): lax.all_to_all(key_send, 'res', split_axis=0, concat_axis=0, tiled=True)  73.7 us
    scatter-add x6, other arithmetic, head_backward(): blank_slab.at[entries].add(value_entries.reshape(-1, rows_block, HD))  38.5 us
    unnamed x42, local copies, waits for them, and re-layouts  29.8 us
    scatter-add x6, other arithmetic, head_backward(): blank_slab.at[entries].add(key_entries.reshape(-1, rows_block, HD))  28.2 us
    dot_general x6, matrix products, head_backward(): jnp.einsum('jqk,jqd->jkd', probs_round, grad_head, preferred_element_type...  20.2 us
    convert_element_type x2, local copies, waits for them, and re-layouts, body(): value_table[blocks_here:].reshape(n_res, capacity, rows_block, width)  19.2 us
  transfers between devices with their start and end apart: 11, of which 6 were waited for; matrix products, arithmetic and copies ran while one was open for 40% of the time, Pallas kernels for 0%

commit v1 on v0

v1 whole, which is shorter than its diff:
```python
import functools
import math

import jax
import jax.numpy as jnp
from jax import lax
from jax.experimental import pallas as pl
from jax.experimental.pallas import tpu as pltpu
from jax.sharding import Mesh, PartitionSpec as P

HD = 128
BS = 128
NBR = 16
HALF = 64
NX, NYH, NYL, NC, NZ = 4, 2, 2, 2, 4
SLOTS = 6
META = 16
ROWS = 3 * 64 + META
NB = 64
QB = 16
SCALE = 1.0 / math.sqrt(HD)
LOG2E = math.log2(math.e)
CHIPS = ("x", "yh", "yl", "z")
VMEM = pl.BlockSpec(memory_space=pltpu.VMEM)
SMEM = pl.BlockSpec(memory_space=pltpu.SMEM)
PARAMS = pltpu.CompilerParams(vmem_limit_bytes=56 * 1024 * 1024)
F32 = jnp.float32
BF16 = jnp.bfloat16


def chip_index(x, yh, yl, z):
    return ((x * NYH + yh) * NYL + yl) * NZ + z


def working_chips():
    for x in range(SLOTS // NYH):
        for yh in range(NYH):
            for z in range(NZ):
                yield x, yh, z, z * SLOTS + x * NYH + yh


def pack_kernel(q_ref, k_ref, v_ref, lists_ref, rows_ref):
    x = pl.program_id(0)

    @pl.when(x < SLOTS // NYH)
    def _():
        for yh in range(NYH):
            for z in range(NZ):
                start = pl.multiple_of((z * SLOTS + x * NYH + yh) * HD, HD)
                for t, ref in enumerate((q_ref, k_ref, v_ref)):
                    piece = ref[:, pl.ds(start, HD)]
                    for yl in range(NYL):
                        dest = chip_index(0, yh, yl, z)
                        rows_ref[dest, t * HALF : (t + 1) * HALF] = piece

    @pl.when(x >= SLOTS // NYH)
    def _():
        rows_ref[:, : 3 * HALF] = jnp.zeros((NB // NX, 3 * HALF, HD), BF16)

    lists = lists_ref[...]
    for dest in range(NB // NX):
        rows_ref[dest, 3 * HALF :] = lists


def pack_grad_kernel(g_ref, grad_ref):
    for s in range(SLOTS):
        grad_ref[s] = g_ref[:, s * HD : (s + 1) * HD]
    grad_ref[SLOTS:] = jnp.zeros((NX * NYH - SLOTS, 2 * BS, HD), BF16)


def dot(a, b):
    return jnp.dot(a, b, preferred_element_type=F32)


def attention_kernel(
    info_ref,
    lists_ref,
    bias_ref,
    rows_ref,
    other_ref,
    grad_ref,
    att_ref,
    dq_ref,
    own_ref,
    far_ref,
    kv,
    kt,
    vt,
    mask,
    work,
    wide,
    dkv,
):
    core = info_ref[0]
    low = info_ref[1]
    bias = bias_ref[info_ref[2]] * LOG2E

    def fill(quad, _):
        for base, ref, at in ((0, rows_ref, HALF), (NB // 2, other_ref, 0)):
            lines = ref[quad * 4, at + 2 * HALF :].astype(F32)
            for half in range(2):
                src = quad * 4 + half * 2
                slot = base + quad * 2 + half
                k_block = jnp.concatenate(
                    [ref[src, at : at + HALF], ref[src + 1, at : at + HALF]], axis=0
                )
                v_at = at + HALF
                v_block = jnp.concatenate(
                    [ref[src, v_at : v_at + HALF], ref[src + 1, v_at : v_at + HALF]], axis=0
                )
                kv[slot] = jnp.concatenate([k_block, v_block], axis=1)
                kt[slot] = k_block.T
                vt[slot] = v_block.T
                dkv[slot] = jnp.zeros((BS, 2 * HD), F32)
                shown = jnp.where(lines[half : half + 1] == 1.0, 0.0, -jnp.inf)
                mask[slot] = jnp.broadcast_to(shown, (BS, BS)).T
        return 0

    lax.fori_loop(0, NB // 4, fill, 0)

    def diagonal(a, b):
        zero = jnp.zeros((HD, HD), BF16)
        return jnp.concatenate(
            [jnp.concatenate([a, zero], axis=1), jnp.concatenate([zero, b], axis=1)], axis=0
        )

    def one_block(i, _):
        pair = i // 2
        half = i % 2
        quad = pair * 2 + low
        src = quad * 4 + half * 2
        q = jnp.concatenate([rows_ref[src, :HALF], rows_ref[src + 1, :HALF]], axis=0)
        g = grad_ref[i]
        gt = g.T
        into = diagonal(q.T, gt)
        out_of = diagonal(q, g)
        line = quad * 4 + 2 + half
        chain = lists_ref[line, NBR]
        slots = []
        shifts = []
        for j in range(NBR):
            n = lists_ref[line, j]
            far = ((n // 2) % 2 != core).astype(jnp.int32)
            other_line = far * NB + (n // 4) * 4 + 2 + n % 2
            slots.append(far * (NB // 2) + (n // 4) * 2 + n % 2)
            shifts.append(jnp.where(lists_ref[other_line, NBR] != chain, bias, 0.0))
        peak = jnp.full((8, BS), -jnp.inf, F32)
        for j in range(NBR):
            both = dot(kv[slots[j]], into)
            score = both[:, :BS] * (SCALE * LOG2E) + (mask[slots[j]] + shifts[j])
            work[j] = score
            wide[j] = both[:, BS:]
            peak = jnp.maximum(peak, jnp.max(score.reshape(BS // 8, 8, BS), axis=0))
        peak = jnp.max(peak, axis=0, keepdims=True)
        total = jnp.zeros((8, BS), F32)
        mixed = jnp.zeros((HD, BS), F32)
        for j in range(0, NBR, 2):
            pair_weights = []
            for u in (j, j + 1):
                weights = jnp.exp2(work[u] - peak)
                work[u] = weights
                total = total + jnp.sum(weights.reshape(BS // 8, 8, BS), axis=0)
                pair_weights.append(weights.astype(BF16))
            vt_pair = jnp.concatenate([vt[slots[j]], vt[slots[j + 1]]], axis=1)
            mixed = mixed + dot(vt_pair, jnp.concatenate(pair_weights, axis=0))
        total = jnp.sum(total, axis=0, keepdims=True)
        attended = (mixed / total).astype(BF16)
        att_ref[i] = attended.T
        delta = jnp.sum(gt.astype(F32) * attended.astype(F32), axis=0, keepdims=True)
        inverse = 1.0 / total
        dqt = jnp.zeros((HD, BS), F32)
        for j in range(0, NBR, 2):
            pair_scores = []
            for u in (j, j + 1):
                probs = work[u] * inverse
                dscore = (probs * (wide[u] - delta)).astype(BF16)
                pair_scores.append(dscore)
                dkv[slots[u]] += dot(
                    jnp.concatenate([dscore, probs.astype(BF16)], axis=1), out_of
                )
            kt_pair = jnp.concatenate([kt[slots[j]], kt[slots[j + 1]]], axis=1)
            dqt = dqt + dot(kt_pair, jnp.concatenate(pair_scores, axis=0))
        dq = (dqt * SCALE).astype(BF16).T
        for yl in range(NYL):
            dest = (pair * 2 + yl) * 4 + half * 2
            dq_ref[dest] = dq[:HALF]
            dq_ref[dest + 1] = dq[HALF:]
        return 0

    lax.fori_loop(0, QB, one_block, 0)

    def drain(b, _):
        src = b * 2
        for t, scale in enumerate((SCALE, 1.0)):
            near = dkv[b, :, t * HD : (t + 1) * HD] * scale
            far = (dkv[NB // 2 + b, :, t * HD : (t + 1) * HD] * scale).astype(BF16)
            for h in range(2):
                own_ref[src + h, t] = near[h * HALF : (h + 1) * HALF]
                far_ref[src + h, t] = far[h * HALF : (h + 1) * HALF]
        return 0

    lax.fori_loop(0, NB // 2, drain, 0)


def merge_kernel(dq_ref, own_ref, came_ref, out_ref):
    out_ref[:, :HALF] = dq_ref[...]
    for t in range(2):
        both = own_ref[:, t] + came_ref[:, t].astype(F32)
        out_ref[:, (t + 1) * HALF : (t + 2) * HALF] = both.astype(BF16)


def unpack_kernel(info_ref, rows_ref, dq_ref, dk_ref, dv_ref):
    low = info_ref[1]
    for x, yh, z, head in working_chips():
        lane = slice(head * HD, (head + 1) * HD)
        zero = chip_index(x, yh, 0, z)
        one = chip_index(x, yh, 1, z)
        dq_ref[:, lane] = rows_ref[zero + low * NZ, :HALF]
        for t, ref in ((1, dk_ref), (2, dv_ref)):
            part = slice(t * HALF, (t + 1) * HALF)
            both = rows_ref[zero, part].astype(F32) + rows_ref[one, part].astype(F32)
            ref[:, lane] = both.astype(BF16)


def join_kernel(att_ref, out_ref):
    for s in range(SLOTS):
        out_ref[:, s * HD : (s + 1) * HD] = att_ref[s]


def shape(dims, dtype):
    return jax.ShapeDtypeStruct(dims, dtype)


def body(queries, keys, values, out_grad, chain_bias, chain_of_block, key_valid, neighbours):
    swap = [(0, 1), (1, 0)]
    core = lax.axis_index("c")
    low = lax.axis_index("yl")
    slot = jnp.minimum(lax.axis_index("x") * NYH + lax.axis_index("yh"), SLOTS - 1)
    info = jnp.stack([core, low, slot, slot]).astype(jnp.int32)

    lists = jnp.concatenate([neighbours, chain_of_block[:, None]], axis=1)
    lists = jnp.concatenate([key_valid.reshape(2, BS), jnp.pad(lists, ((0, 0), (0, BS - 1 - NBR)))])
    lists = jnp.pad(lists, ((0, META - 4), (0, 0))).astype(BF16)

    whole = pl.BlockSpec((HALF, NZ * SLOTS * HD), lambda x: (0, 0))
    rows = pl.pallas_call(
        pack_kernel,
        grid=(NX,),
        out_shape=shape((NB, ROWS, HD), BF16),
        in_specs=[whole, whole, whole, pl.BlockSpec((META, BS), lambda x: (0, 0))],
        out_specs=pl.BlockSpec((NB // NX, ROWS, HD), lambda x: (x, 0, 0)),
        compiler_params=PARAMS,
        name="pack",
    )(queries, keys, values, lists)
    grads = pl.pallas_call(
        pack_grad_kernel,
        out_shape=shape((NX * NYH, 2 * BS, HD), BF16),
        in_specs=[VMEM],
        out_specs=VMEM,
        compiler_params=PARAMS,
        name="pack_grad",
    )(out_grad)

    rows = lax.all_to_all(rows, CHIPS, split_axis=0, concat_axis=0, tiled=True)
    other = lax.ppermute(rows[:, HALF:], "c", swap)
    grads = lax.all_to_all(grads, ("x", "yh"), split_axis=0, concat_axis=0, tiled=True)
    lists = jnp.stack(
        [
            rows.reshape(NB // NZ, NZ, ROWS, HD)[:, 0, 3 * HALF : 3 * HALF + 4],
            other.reshape(NB // NZ, NZ, ROWS - HALF, HD)[:, 0, 2 * HALF : 2 * HALF + 4],
        ]
    )
    lists = lists.astype(jnp.int32).reshape(2 * NB, HD)

    table = pltpu.VMEM((NB, BS, HD), BF16)
    att, dq, own, far = pl.pallas_call(
        attention_kernel,
        out_shape=(
            shape((QB, BS, HD), BF16),
            shape((NB, HALF, HD), BF16),
            shape((NB, 2, HALF, HD), F32),
            shape((NB, 2, HALF, HD), BF16),
        ),
        in_specs=[SMEM, SMEM, SMEM, VMEM, VMEM, VMEM],
        out_specs=(VMEM,) * 4,
        scratch_shapes=[
            pltpu.VMEM((NB, BS, 2 * HD), BF16),
            table,
            table,
            pltpu.VMEM((NB, BS, BS), F32),
            pltpu.VMEM((NBR, BS, BS), F32),
            pltpu.VMEM((NBR, BS, BS), F32),
            pltpu.VMEM((NB, BS, 2 * HD), F32),
        ],
        compiler_params=PARAMS,
        name="attention",
    )(info, lists, chain_bias, rows, other, grads.reshape(QB, BS, HD))

    came = lax.ppermute(far, "c", swap)
    att = lax.all_to_all(
        att.reshape(NX * NYH, 2 * BS, HD), ("x", "yh"), split_axis=0, concat_axis=0, tiled=True
    )
    attended = pl.pallas_call(
        join_kernel,
        out_shape=shape((2 * BS, SLOTS * HD), BF16),
        in_specs=[VMEM],
        out_specs=VMEM,
        compiler_params=PARAMS,
        name="join",
    )(att)
    steps = 8
    each = NB // steps
    split = pl.BlockSpec((each, 2, HALF, HD), lambda i: (i, 0, 0, 0))
    back = pl.pallas_call(
        merge_kernel,
        grid=(steps,),
        out_shape=shape((NB, 3 * HALF, HD), BF16),
        in_specs=[pl.BlockSpec((each, HALF, HD), lambda i: (i, 0, 0)), split, split],
        out_specs=pl.BlockSpec((each, 3 * HALF, HD), lambda i: (i, 0, 0)),
        compiler_params=PARAMS,
        name="merge",
    )(dq, own, came)
    back = lax.all_to_all(back, CHIPS, split_axis=0, concat_axis=0, tiled=True)
    flat = shape((HALF, NZ * SLOTS * HD), BF16)
    dq, dk, dv = pl.pallas_call(
        unpack_kernel,
        out_shape=(flat, flat, flat),
        in_specs=[SMEM, VMEM],
        out_specs=(VMEM,) * 3,
        compiler_params=PARAMS,
        name="unpack",
    )(info, back)
    return attended, dq, dk, dv


def solution(mesh):
    grid = Mesh(mesh.devices.reshape(NX, NYH, NYL, NC, NZ), ("x", "yh", "yl", "c", "z"))
    res = ("x", "yh", "yl", "c")
    both = P(res + ("z",), None)
    return jax.shard_map(
        body,
        mesh=grid,
        in_specs=(both, both, both, P(res, "z"), P("z"), P(res), P(res), P(res, None)),
        out_specs=(P(res, "z"), both, both, both),
        check_vma=False,
    )
```

time: 662 us -> 187 us (0.28); the launches traced: 652 us -> 185 us
  local copies, waits for them, and re-layouts: 123 us -> 6.4 us
  waiting for transfers between devices: 167 us -> 50.4 us
  other arithmetic: 116 us -> 3.96 us
  matrix products: 108 us -> 0 us
  Pallas kernels: 0 us -> 54.6 us
  starting transfers between devices: 58.1 us -> 14.7 us
  blocking collectives: 79.2 us -> 54.3 us
    all_to_all x11 -> x3, waiting for transfers between devices: 167 us -> 49.6 us  [the longest x1 38.1 us: body(): back = lax.all_to_all(back, CHIPS, split_axis=0, concat_axis=0, tiled=True)]
    dot_general x38 -> x0, matrix products: 89.5 us -> none  [the longest x6 20.2 us: head_backward(): jnp.einsum('jqk,jqd->jkd', probs_round, grad_head, preferred_element_type...]
    scatter-add x12 -> x0, other arithmetic: 66.8 us -> none  [the longest x6 38.5 us: head_backward(): blank_slab.at[entries].add(value_entries.reshape(-1, rows_block, HD))]
    pallas_call x0 -> x6, Pallas kernels: none -> 54.6 us  [the longest x1 37 us: body(): pl.pallas_call(attention_kernel, out_shape=(shape((QB, BS, HD), BF16), sh...]
    all_to_all x11 -> x3, starting transfers between devices: 58.1 us -> 14.7 us  [the longest x1 6.98 us: body(): back = lax.all_to_all(back, CHIPS, split_axis=0, concat_axis=0, tiled=True)]
    convert_element_type x6 -> x0, local copies, waits for them, and re-layouts: 39.9 us -> none  [the longest x2 19.2 us: body(): value_table[blocks_here:].reshape(n_res, capacity, rows_block, width)]
    unnamed x42 -> x8, local copies, waits for them, and re-layouts: 29.8 us -> 3.84 us
    all_to_all x1, blocking collectives: 79.2 us -> 54.3 us  [body(): rows = lax.all_to_all(rows, CHIPS, split_axis=0, concat_axis=0, tiled=True)]
  transfers between devices with their start and end apart: 11 -> 5, of which waited for: 6 -> 4; matrix products, arithmetic and copies ran while one was open for 40% -> 1% of each run, Pallas kernels for 0% -> 6%
where the time goes in v1:
time: 187 us; the launch traced here: 185 us
  Pallas kernels  54.6 us (29%)
  blocking collectives  54.3 us (29%)
  waiting for transfers between devices  50.4 us (27%)
  starting transfers between devices  14.7 us (8%)
  local copies, waits for them, and re-layouts  6.4 us (3%)
  other arithmetic  3.96 us (2%)
    all_to_all x1, blocking collectives, body(): rows = lax.all_to_all(rows, CHIPS, split_axis=0, concat_axis=0, tiled=True)  54.3 us
    all_to_all x1, waiting for transfers between devices, body(): back = lax.all_to_all(back, CHIPS, split_axis=0, concat_axis=0, tiled=True)  38.1 us
    pallas_call x1, Pallas kernels, body(): pl.pallas_call(attention_kernel, out_shape=(shape((QB, BS, HD), BF16), sh...  37 us
    all_to_all x1, waiting for transfers between devices, body(): lax.all_to_all(grads, ('x', 'yh'), split_axis=0, concat_axis=0, tiled=True)  9.22 us
    all_to_all x1, starting transfers between devices, body(): back = lax.all_to_all(back, CHIPS, split_axis=0, concat_axis=0, tiled=True)  6.98 us
    pallas_call x1, Pallas kernels, body(): pl.pallas_call(merge_kernel, grid=(steps,), out_shape=shape((NB, 3 * HALF...  6.93 us
    all_to_all x1, starting transfers between devices, body(): lax.all_to_all(grads, ('x', 'yh'), split_axis=0, concat_axis=0, tiled=True)  4.14 us
    unnamed x8, local copies, waits for them, and re-layouts  3.84 us
  transfers between devices with their start and end apart: 5, of which 4 were waited for; matrix products, arithmetic and copies ran while one was open for 1% of the time, Pallas kernels for 6%

profile of v1, /device:TPU:8, one launch (start us, length us, event | category | flops | bytes accessed | tf_op | source)
XLA Modules:
  0.0 185.1 jit_solution(15535963568666654132)
XLA Ops:
  0.6 0.7 convert_bitcast_fusion
  1.3 0.1 copy.12
  1.4 0.7 convert_bitcast_fusion.1
  2.1 0.7 convert.18
  2.8 0.1 fusion.5
  2.8 0.6 fusion.2.lists_ref
  3.4 3.6 %pack.1 = bf16[64,208,128]{2,1,0:T(8,128)(2,1)} custom-call(bf16[64,3072]{1,0:T(8,128)(2,1)} %q_ref.1, bf16[64,3072]{1,0:T(8,128)(2,1)} %k_ref.1, bf16[64,3072]{1,0:T(8,128)(2,1)} %v_ref.1, bf16[16,128]{1,0:T(8,128)(2,1)} %fusion.2.lists_ref), custom_call_target="tpu_custom_call" | custom-call | tf_op jit(solution)/shard_map/pack/pallas_call | solution.py:246
  7.0 54.3 %all_to_all.20.rows_ref = bf16[64,208,128]{2,1,0:T(8,128)(2,1)S(1)} all-to-all(bf16[64,208,128]{2,1,0:T(8,128)(2,1)} %pack.1), channel_id=1, replica_groups=mesh['x'=4,'yh'=2,'yl'=2,'c'=2,'z'=4] {'x','yh','yl','z'}, dimensions={0} | all-to-all | bytes 6815744 | tf_op jit(solution)/shard_map/all_to_all | solution.py:264
  61.4 0.0 copy-start
  61.4 1.7 slice.13
  63.0 0.0 collective-permute-start
  63.0 2.1 %pack_grad.1 = bf16[8,256,128]{2,1,0:T(8,128)(2,1)} custom-call(bf16[256,768]{1,0:T(8,128)(2,1)} %g_ref.1), custom_call_target="tpu_custom_call" | custom-call | tf_op jit(solution)/shard_map/pack_grad/pallas_call | solution.py:255
  65.2 4.1 %all-to-all-start.1 = ((bf16[8,256,128]{2,1,0:T(8,128)(2,1)}), bf16[8,256,128]{2,1,0:T(8,128)(2,1)}, u32[]{:S(2)}, u32[]{:S(2)}) async-start(bf16[8,256,128]{2,1,0:T(8,128)(2,1)} %pack_grad.1), calls=%async_computation.1 | async-start | bytes 1048576 | tf_op jit(solution)/shard_map/all_to_all | solution.py:266
  69.3 0.6 pad_add_fusion.info_ref
  69.9 0.0 copy-done
  70.0 0.0 collective-permute-done.other_ref
  70.0 0.8 slice_bitcast_fusion
  70.8 0.6 convert.20.lists_ref
  71.4 9.2 %all-to-all-done.1 = bf16[8,256,128]{2,1,0:T(8,128)(2,1)} async-done(((bf16[8,256,128]{2,1,0:T(8,128)(2,1)}), bf16[8,256,128]{2,1,0:T(8,128)(2,1)}, u32[]{:S(2)}, u32[]{:S(2)}) %all-to-all-start.1) | async-done | bytes 524320 | tf_op jit(solution)/shard_map/all_to_all | solution.py:266
  80.6 37.0 %attention.1 = (bf16[16,128,128]{2,1,0:T(8,128)(2,1)}, bf16[64,64,128]{2,1,0:T(8,128)(2,1)}, f32[64,2,64,128]{3,2,1,0:T(8,128)}, bf16[64,2,64,128]{3,2,1,0:T(8,128)(2,1)}) custom-call(s32[4]{0:T(128)} %pad_add_fusion.info_ref, s32[128,128]{1,0:T(8,128)} %convert.20.lists_ref, f32[6]{0:T(128)} %bias_ref.1, bf16[64,208,128]{2,1,0:T(8,128)(2,1)} %copy-done, ...), custom_call_target="tpu_custom_call" | custom-call | tf_op jit(solution)/shard_map/attention/pallas_call | solution.py:276
  117.7 0.0 collective-permute-start.1
  117.7 3.6 %all-to-all-start.2 = ((bf16[8,256,128]{2,1,0:T(8,128)(2,1)}), bf16[8,256,128]{2,1,0:T(8,128)(2,1)S(1)}, u32[]{:S(2)}, u32[]{:S(2)}) async-start(bf16[8,256,128]{2,1,0:T(8,128)(2,1)} %bitcast.20), calls=%async_computation.2 | async-start | bytes 1048576 | tf_op jit(solution)/shard_map/all_to_all | solution.py:300
  121.3 0.8 collective-permute-done.1.came_ref
  122.0 1.4 copy-done.2
  123.4 6.9 %merge.1 = bf16[64,192,128]{2,1,0:T(8,128)(2,1)} custom-call(bf16[64,64,128]{2,1,0:T(8,128)(2,1)} %get-tuple-element.12.dq_ref, f32[64,2,64,128]{3,2,1,0:T(8,128)} %get-tuple-element.13.own_ref, bf16[64,2,64,128]{3,2,1,0:T(8,128)(2,1)} %copy-done.2), custom_call_target="tpu_custom_call" | custom-call | tf_op jit(solution)/shard_map/merge/pallas_call | solution.py:314
  130.4 2.2 %all-to-all-done.2.att_ref = bf16[8,256,128]{2,1,0:T(8,128)(2,1)S(1)} async-done(((bf16[8,256,128]{2,1,0:T(8,128)(2,1)}), bf16[8,256,128]{2,1,0:T(8,128)(2,1)S(1)}, u32[]{:S(2)}, u32[]{:S(2)}) %all-to-all-start.2) | async-done | bytes 524320 | tf_op jit(solution)/shard_map/all_to_all | solution.py:300
  132.6 0.8 copy-done.3
  133.4 7.0 %all-to-all-start.3 = ((bf16[64,192,128]{2,1,0:T(8,128)(2,1)}), bf16[64,192,128]{2,1,0:T(8,128)(2,1)S(1)}, u32[]{:S(2)}, u32[]{:S(2)}) async-start(bf16[64,192,128]{2,1,0:T(8,128)(2,1)} %merge.1), calls=%async_computation.3 | async-start | bytes 6291456 | tf_op jit(solution)/shard_map/all_to_all | solution.py:323
  140.4 1.9 %join.1 = bf16[256,768]{1,0:T(8,128)(2,1)} custom-call(bf16[8,256,128]{2,1,0:T(8,128)(2,1)} %copy-done.3), custom_call_target="tpu_custom_call" | custom-call | tf_op jit(solution)/shard_map/join/pallas_call | solution.py:303
  142.3 38.1 %all-to-all-done.3.rows_ref = bf16[64,192,128]{2,1,0:T(8,128)(2,1)S(1)} async-done(((bf16[64,192,128]{2,1,0:T(8,128)(2,1)}), bf16[64,192,128]{2,1,0:T(8,128)(2,1)S(1)}, u32[]{:S(2)}, u32[]{:S(2)}) %all-to-all-start.3) | async-done | bytes 3145760 | tf_op jit(solution)/shard_map/all_to_all | solution.py:323
  180.4 1.6 copy-done.1
  182.0 3.1 %unpack.1 = (bf16[64,3072]{1,0:T(8,128)(2,1)}, bf16[64,3072]{1,0:T(8,128)(2,1)}, bf16[64,3072]{1,0:T(8,128)(2,1)}) custom-call(s32[4]{0:T(128)} %pad_add_fusion.info_ref, bf16[64,192,128]{2,1,0:T(8,128)(2,1)} %copy-done.1), custom_call_target="tpu_custom_call" | custom-call | tf_op jit(solution)/shard_map/unpack/pallas_call | solution.py:325
  (5 shorter events, 0.0 us)
Async XLA Ops:
  61.4 8.6 %copy-start = (bf16[64,208,128]{2,1,0:T(8,128)(2,1)}, bf16[64,208,128]{2,1,0:T(8,128)(2,1)S(1)}, u32[]{:S(2)}) copy-start(bf16[64,208,128]{2,1,0:T(8,128)(2,1)S(1)} %all_to_all.20.rows_ref) | copy-start | bytes 10223620
  63.0 6.9 %collective-permute-start = (bf16[64,144,128]{2,1,0:T(8,128)(2,1)}, bf16[64,144,128]{2,1,0:T(8,128)(2,1)}, u32[]{:S(2)}, u32[]{:S(2)}) collective-permute-start(bf16[64,144,128]{2,1,0:T(8,128)(2,1)} %slice.13), channel_id=1, source_target_pairs={{0,4},{4,0},{1,5},{5,1},{2,6},{6,2},{3,7},{7,3},{8,12},{12,8},{9,1... | collective-permute-start | bytes 7077896 | tf_op jit(solution)/shard_map/ppermute | solution.py:265
  65.2 15.4 %all-to-all-start.1 = ((bf16[8,256,128]{2,1,0:T(8,128)(2,1)}), bf16[8,256,128]{2,1,0:T(8,128)(2,1)}, u32[]{:S(2)}, u32[]{:S(2)}) async-start(bf16[8,256,128]{2,1,0:T(8,128)(2,1)} %pack_grad.1), calls=%async_computation.1 | async-start | bytes 1048576 | tf_op jit(solution)/shard_map/all_to_all | solution.py:266
  117.7 4.4 %collective-permute-start.1 = (bf16[64,2,64,128]{3,2,1,0:T(8,128)(2,1)}, bf16[64,2,64,128]{3,2,1,0:T(8,128)(2,1)S(1)}, u32[]{:S(2)}, u32[]{:S(2)}) collective-permute-start(bf16[64,2,64,128]{3,2,1,0:T(8,128)(2,1)} %get-tuple-element.14), channel_id=1, source_target_pairs={{0,4},{4,0},{1,5},{5,1},{2,6},{6,2},{3,7},{7,3},{8,12},{12,8},{9,1... | collective-permute-start | bytes 6291464 | tf_op jit(solution)/shard_map/ppermute | solution.py:299
  117.7 14.9 %all-to-all-start.2 = ((bf16[8,256,128]{2,1,0:T(8,128)(2,1)}), bf16[8,256,128]{2,1,0:T(8,128)(2,1)S(1)}, u32[]{:S(2)}, u32[]{:S(2)}) async-start(bf16[8,256,128]{2,1,0:T(8,128)(2,1)} %bitcast.20), calls=%async_computation.2 | async-start | bytes 1048576 | tf_op jit(solution)/shard_map/all_to_all | solution.py:300
  122.0 1.4 copy-start.2
  132.6 0.8 copy-start.3
  133.4 47.0 %all-to-all-start.3 = ((bf16[64,192,128]{2,1,0:T(8,128)(2,1)}), bf16[64,192,128]{2,1,0:T(8,128)(2,1)S(1)}, u32[]{:S(2)}, u32[]{:S(2)}) async-start(bf16[64,192,128]{2,1,0:T(8,128)(2,1)} %merge.1), calls=%async_computation.3 | async-start | bytes 6291456 | tf_op jit(solution)/shard_map/all_to_all | solution.py:323
  180.4 1.6 copy-start.1

commit v2 on v1

v2 whole, which is shorter than its diff:
```python
import functools
import math

import jax
import jax.numpy as jnp
from jax import lax
from jax.experimental import pallas as pl
from jax.experimental.pallas import tpu as pltpu
from jax.sharding import Mesh, PartitionSpec as P

HD = 128
BS = 128
NBR = 16
HALF = 64
QUARTER = 32
NX, NYH, NYL, NC, NZ = 4, 2, 2, 2, 4
SLOTS = 6
META = 16
SIDES = NX * NYH
Q_AT = 2 * HALF + META
ROWS = Q_AT + QUARTER
BACK = 2 * HALF + QUARTER
NB = 64
QB = 16
SCALE = 1.0 / math.sqrt(HD)
LOG2E = math.log2(math.e)
CHIPS = ("x", "yh", "yl", "z")
PARTS = 4
ANY = pl.BlockSpec(memory_space=pl.ANY)
VMEM = pl.BlockSpec(memory_space=pltpu.VMEM)
SMEM = pl.BlockSpec(memory_space=pltpu.SMEM)
PARAMS = pltpu.CompilerParams(vmem_limit_bytes=50 * 1024 * 1024)
FULL = pltpu.CompilerParams(vmem_limit_bytes=62 * 1024 * 1024)
F32 = jnp.float32
BF16 = jnp.bfloat16


def chip_index(x, yh, yl, z):
    return ((x * NYH + yh) * NYL + yl) * NZ + z


def pack_kernel(info_ref, chain_ref, q_ref, k_ref, v_ref, valid_ref, near_ref, rows_ref, lists):
    x = pl.program_id(0)
    low = info_ref[1]

    @pl.when(x == 0)
    def _():
        lane = lax.broadcasted_iota(jnp.int32, (1, BS), 1)
        lists[...] = jnp.zeros((META, BS), F32)
        lists[0:2] = valid_ref[...].astype(F32)
        lists[2:4, 0:NBR] = near_ref[...].astype(F32)
        for half in range(2):
            line = lists[2 + half : 3 + half]
            chain = jnp.full((1, BS), chain_ref[half], jnp.int32).astype(F32)
            lists[2 + half : 3 + half] = jnp.where(lane == NBR, chain, line)

    @pl.when(x < SLOTS // NYH)
    def _():
        for yh in range(NYH):
            for z in range(NZ):
                start = pl.multiple_of((z * SLOTS + x * NYH + yh) * HD, HD)
                first, second = chip_index(0, yh, 0, z), chip_index(0, yh, 1, z)
                for t, ref in enumerate((k_ref, v_ref)):
                    piece = ref[:, pl.ds(start, HD)]
                    for dest in (first, second):
                        rows_ref[dest, t * HALF : (t + 1) * HALF] = piece
                query = q_ref[:, pl.ds(start, HD)]
                upper, lower = query[:QUARTER], query[QUARTER:]
                rows_ref[first, Q_AT:] = jnp.where(low == 0, upper, lower)
                rows_ref[second, Q_AT:] = jnp.where(low == 0, lower, upper)

    @pl.when(x >= SLOTS // NYH)
    def _():
        rows_ref[...] = jnp.zeros((NB // NX, ROWS, HD), BF16)

    held = lists[...].astype(BF16)
    for dest in range(NB // NX):
        rows_ref[dest, 2 * HALF : Q_AT] = held


def pack_grad_kernel(info_ref, g_ref, keep_ref, swap_ref):
    x, yh = info_ref[2], info_ref[3]
    for d in range(NX):
        first = jnp.minimum(x ^ d, SLOTS // NYH - 1) * NYH
        for ref, side in ((keep_ref, yh), (swap_ref, 1 - yh)):
            start = pl.multiple_of((first + side) * HD, HD)
            ref[d] = g_ref[:, pl.ds(start, HD)]


def dot(a, b):
    return jnp.dot(a, b, preferred_element_type=F32)


def attention_kernel(
    info_ref,
    lists_ref,
    bias_ref,
    rows_hbm,
    other_hbm,
    lower_hbm,
    grad_keep_hbm,
    grad_came_hbm,
    grad_1_hbm,
    grad_2_hbm,
    grad_3_hbm,
    att_keep_hbm,
    att_swap_hbm,
    back_hbm,
    far_hbm,
    lower_out_hbm,
    *refs,
):
    (
        rows_ref,
        other_ref,
        lower_ref,
        lower_out_ref,
        grad_ref,
        att_ref,
        kv,
        kt,
        vt,
        mask,
        scores,
        weights,
        dprob_even,
        dprob_odd,
        stats,
        dkv,
        back_ref,
        far_ref,
        rows_sem,
        other_sem,
        lower_sem,
        grad_sem,
        att_sem,
        back_sem,
        far_sem,
    ) = refs
    core = info_ref[0]
    low = info_ref[1]
    x, yh = info_ref[2], info_ref[3]
    slot_here = x * NYH + yh
    dprob = (dprob_even, dprob_odd)
    bias = bias_ref[jnp.minimum(slot_here, SLOTS - 1)] * LOG2E
    part = NB // PARTS

    def chunk(k):
        return pl.ds(k * part, part)

    def copies(source, target, sems, lines):
        return [
            pltpu.make_async_copy(
                source.at[chunk(k), pl.ds(0, lines)], target.at[chunk(k)], sems.at[k]
            )
            for k in range(PARTS)
        ]

    rows_in = copies(rows_hbm, rows_ref, rows_sem, ROWS)
    other_in = copies(other_hbm, other_ref, other_sem, Q_AT)
    grad_pieces = [(grad_keep_hbm.at[0], grad_came_hbm.at[0])]
    for ref in (grad_1_hbm, grad_2_hbm, grad_3_hbm):
        grad_pieces.append((ref.at[0], ref.at[1]))
    grads_in = []
    att_out = []
    for d, pieces in enumerate(grad_pieces):
        for n, (piece, side, att_hbm) in enumerate(
            ((pieces[0], yh, att_keep_hbm), (pieces[1], 1 - yh, att_swap_hbm))
        ):
            pair = (x ^ d) * NYH + side
            at = d * 2 + n
            grads_in.append(pltpu.make_async_copy(piece, grad_ref.at[pair], grad_sem.at[at]))
            att_out.append(pltpu.make_async_copy(att_ref.at[pair], att_hbm.at[d], att_sem.at[at]))
    lower_in = pltpu.make_async_copy(lower_hbm, lower_ref, lower_sem.at[0])
    lower_out = pltpu.make_async_copy(lower_out_ref, lower_out_hbm, lower_sem.at[1])
    for copy in rows_in + other_in + [lower_in] + grads_in:
        copy.start()

    def grad_block(i):
        start = pl.multiple_of((i % 2) * BS, BS)
        return grad_ref[i // 2, pl.ds(start, BS)]

    def fill(quad, base, ref):
        lines = ref[quad * 4, 2 * HALF : Q_AT].astype(F32)
        for half in range(2):
            src = quad * 4 + half * 2
            slot = base + quad * 2 + half
            k_block = jnp.concatenate([ref[src, :HALF], ref[src + 1, :HALF]], axis=0)
            v_block = jnp.concatenate(
                [ref[src, HALF : 2 * HALF], ref[src + 1, HALF : 2 * HALF]], axis=0
            )
            kv[slot] = jnp.concatenate([k_block, v_block], axis=1)
            kt[slot] = k_block.T
            vt[slot] = v_block.T
            dkv[slot] = jnp.zeros((BS, 2 * HD), F32)
            shown = jnp.where(lines[half : half + 1] == 1.0, 0.0, -jnp.inf)
            mask[slot] = jnp.broadcast_to(shown, (BS, BS)).T

    for base, ref, waits in ((0, rows_ref, rows_in), (NB // 2, other_ref, other_in)):
        for k, copy in enumerate(waits):
            copy.wait()

            def fill_one(m, _, base=base, ref=ref, k=k):
                fill(k * (part // 4) + m, base, ref)
                return 0

            lax.fori_loop(0, part // 4, fill_one, 0)
    lower_in.wait()
    for copy in grads_in:
        copy.wait()

    def diagonal(a, b):
        zero = jnp.zeros((HD, HD), BF16)
        return jnp.concatenate(
            [jnp.concatenate([a, zero], axis=1), jnp.concatenate([zero, b], axis=1)], axis=0
        )

    def place(i):
        pair = i // 2
        half = i % 2
        quad = pair * 2 + low
        return pair, half, quad

    def query_block(i):
        pair, half, quad = place(i)
        src = quad * 4 + half * 2
        low_src = pair * 4 + half * 2
        pieces = []
        for h in range(2):
            pieces += [rows_ref[src + h, Q_AT:], lower_ref[low_src + h]]
        return jnp.concatenate(pieces, axis=0)

    def listed(i, j):
        _, half, quad = place(i)
        n = lists_ref[quad * 4 + 2 + half, j]
        far = ((n // 2) % 2 != core).astype(jnp.int32)
        line = far * NB + (n // 4) * 4 + 2 + n % 2
        return far * (NB // 2) + (n // 4) * 2 + n % 2, line

    class Scores:
        def __init__(self, i, parity):
            _, half, quad = place(i)
            self.i = i
            self.chain = lists_ref[quad * 4 + 2 + half, NBR]
            self.into = diagonal(query_block(i).T, grad_block(i).T)
            self.dprob = dprob[parity]
            self.peak = jnp.full((8, BS), -jnp.inf, F32)

        def step(self, j):
            slot, line = listed(self.i, j)
            shift = jnp.where(lists_ref[line, NBR] != self.chain, bias, 0.0)
            both = dot(kv[slot], self.into)
            score = both[:, :BS] * (SCALE * LOG2E) + (mask[slot] + shift)
            scores[j] = score
            self.dprob[j] = both[:, BS:]
            self.peak = jnp.maximum(self.peak, jnp.max(score.reshape(BS // 8, 8, BS), axis=0))

        def end(self):
            stats[0:1] = jnp.max(self.peak, axis=0, keepdims=True)

    class Mix:
        def __init__(self, i):
            self.i = i
            self.peak = stats[0:1]
            self.total = jnp.zeros((8, BS), F32)
            self.mixed = jnp.zeros((HD, BS), F32)
            self.held = []

        def step(self, j):
            row = jnp.exp2(scores[j] - self.peak)
            weights[j] = row
            self.total = self.total + jnp.sum(row.reshape(BS // 8, 8, BS), axis=0)
            self.held.append((row.astype(BF16), vt[listed(self.i, j)[0]]))
            if j % 2:
                (r0, v0), (r1, v1) = self.held
                self.held = []
                self.mixed = self.mixed + dot(
                    jnp.concatenate([v0, v1], axis=1), jnp.concatenate([r0, r1], axis=0)
                )

        def end(self):
            total = jnp.sum(self.total, axis=0, keepdims=True)
            attended = (self.mixed / total).astype(BF16)
            pair, half, _ = place(self.i)
            att_ref[pair, pl.ds(pl.multiple_of(half * BS, BS), BS)] = attended.T
            grad = grad_block(self.i).T.astype(F32)
            stats[1:2] = jnp.sum(grad * attended.astype(F32), axis=0, keepdims=True)
            stats[2:3] = 1.0 / total

    class Back:
        def __init__(self, i, parity):
            self.i = i
            self.dprob = dprob[parity]
            self.delta = stats[1:2]
            self.inverse = stats[2:3]
            self.out_of = diagonal(query_block(i), grad_block(i))
            self.dqt = jnp.zeros((HD, BS), F32)
            self.held = []

        def step(self, j):
            slot, _ = listed(self.i, j)
            probs = weights[j] * self.inverse
            dscore = (probs * (self.dprob[j] - self.delta)).astype(BF16)
            both = jnp.concatenate([dscore, probs.astype(BF16)], axis=1)
            dkv[slot] += dot(both, self.out_of)
            self.held.append((dscore, kt[slot]))
            if j % 2:
                (s0, k0), (s1, k1) = self.held
                self.held = []
                self.dqt = self.dqt + dot(
                    jnp.concatenate([k0, k1], axis=1), jnp.concatenate([s0, s1], axis=0)
                )

        def end(self):
            pair, half, quad = place(self.i)
            dq = (self.dqt * SCALE).astype(BF16).T
            for h in range(2):
                at = h * HALF
                back_ref[quad * 4 + half * 2 + h, 2 * HALF :] = dq[at : at + QUARTER]
                lower_out_ref[pair * 4 + half * 2 + h] = dq[at + QUARTER : at + HALF]

    def together(*stages):
        for j in range(NBR):
            for stage in stages:
                stage.step(j)
        for stage in stages:
            stage.end()

    together(Scores(0, 0))
    together(Mix(0), Scores(1, 1))

    def rounds(r, _):
        for parity in range(2):
            i = r * 2 + parity
            together(Back(i, parity), Mix(i + 1), Scores(i + 2, parity))
        return 0

    lax.fori_loop(0, QB // 2 - 1, rounds, 0)
    together(Back(QB - 2, 0), Mix(QB - 1))
    together(Back(QB - 1, 1))

    for copy in att_out + [lower_out]:
        copy.start()
    far_out = copies(far_ref, far_hbm, far_sem, 2 * HALF)
    back_out = copies(back_ref, back_hbm, back_sem, BACK)

    def drain(b, base, target):
        for t, scale in enumerate((SCALE, 1.0)):
            block = (dkv[base + b, :, t * HD : (t + 1) * HD] * scale).astype(BF16)
            rows = slice(t * HALF, (t + 1) * HALF)
            for h in range(2):
                target[b * 2 + h, rows] = block[h * HALF : (h + 1) * HALF]

    for base, target, outs in ((NB // 2, far_ref, far_out), (0, back_ref, back_out)):
        for k, copy in enumerate(outs):

            def drain_one(m, _, base=base, target=target, k=k):
                drain(k * (part // 2) + m, base, target)
                return 0

            lax.fori_loop(0, part // 2, drain_one, 0)
            copy.start()
    for copy in att_out + [lower_out] + far_out + back_out:
        copy.wait()


def merge_kernel(
    info_ref,
    back_hbm,
    came_hbm,
    lower_hbm,
    out_hbm,
    back_ref,
    came_ref,
    back_sem,
    came_sem,
    out_sem,
    lower_sem,
):
    other = 1 - info_ref[1]
    each = NB // PARTS
    near = slice(0, 2 * HALF)
    copies = []
    for k in range(PARTS):
        part = pl.ds(k * each, each)
        copies.append(
            (
                pltpu.make_async_copy(
                    back_hbm.at[part, near], back_ref.at[part], back_sem.at[k]
                ),
                pltpu.make_async_copy(came_hbm.at[part], came_ref.at[part], came_sem.at[k]),
                pltpu.make_async_copy(back_ref.at[part], out_hbm.at[part, near], out_sem.at[k]),
            )
        )
    lower = []
    for n in range(SIDES):
        target = out_hbm.at[pl.ds((n * 2 + other) * NZ, NZ), slice(2 * HALF, BACK)]
        source = lower_hbm.at[pl.ds(n * NZ, NZ)]
        lower.append(pltpu.make_async_copy(source, target, lower_sem.at[n]))
    for mine, came, _ in copies:
        mine.start()
        came.start()
    for copy in lower:
        copy.start()
    for k, (mine, came, out) in enumerate(copies):
        mine.wait()
        came.wait()

        def add(m, _, k=k):
            n = k * each + m
            back_ref[n] = (back_ref[n].astype(F32) + came_ref[n].astype(F32)).astype(BF16)
            return 0

        lax.fori_loop(0, each, add, 0, unroll=4)
        out.start()
    for _, _, out in copies:
        out.wait()
    for copy in lower:
        copy.wait()


def unpack_kernel(info_ref, rows_hbm, dq_ref, dk_ref, dv_ref, rows_ref, sems):
    low = info_ref[1]
    each = NB // NX
    copies = [
        pltpu.make_async_copy(
            rows_hbm.at[pl.ds(x * each, each)], rows_ref.at[pl.ds(x * each, each)], sems.at[x]
        )
        for x in range(SLOTS // NYH)
    ]
    for copy in copies:
        copy.start()
    for x, copy in enumerate(copies):
        copy.wait()
        for yh in range(NYH):
            for z in range(NZ):
                head = z * SLOTS + x * NYH + yh
                lane = slice(head * HD, (head + 1) * HD)
                zero = chip_index(x, yh, 0, z)
                one = chip_index(x, yh, 1, z)
                dq_ref[:QUARTER, lane] = rows_ref[zero + low * NZ, 2 * HALF :]
                dq_ref[QUARTER:, lane] = rows_ref[zero + (1 - low) * NZ, 2 * HALF :]
                for t, ref in enumerate((dk_ref, dv_ref)):
                    part = slice(t * HALF, (t + 1) * HALF)
                    both = rows_ref[zero, part].astype(F32) + rows_ref[one, part].astype(F32)
                    ref[:, lane] = both.astype(BF16)


def join_kernel(info_ref, keep_hbm, came_hbm, one_hbm, two_hbm, three_hbm, out_hbm, sems):
    x, yh = info_ref[2], info_ref[3]
    pieces = [(keep_hbm.at[0], came_hbm.at[0])]
    for ref in (one_hbm, two_hbm, three_hbm):
        pieces.append((ref.at[0], ref.at[1]))

    def each(act):
        for d, pair in enumerate(pieces):
            first = (x ^ d) * NYH

            @pl.when(first < SLOTS)
            def _(d=d, pair=pair, first=first):
                for n, side in enumerate((yh, 1 - yh)):
                    lane = pl.ds(pl.multiple_of((first + side) * HD, HD), HD)
                    act(pltpu.make_async_copy(pair[n], out_hbm.at[:, lane], sems.at[d * 2 + n]))

    each(lambda copy: copy.start())
    each(lambda copy: copy.wait())


def shape(dims, dtype):
    return jax.ShapeDtypeStruct(dims, dtype)


def attend(*operands):
    four = shape((NX, 2 * BS, HD), BF16)
    table = pltpu.VMEM((NB, BS, HD), BF16)
    near = pltpu.VMEM((NBR, BS, BS), F32)
    sems = pltpu.SemaphoreType.DMA((PARTS,))
    return pl.pallas_call(
        attention_kernel,
        out_shape=(
            four,
            four,
            shape((NB, BACK, HD), BF16),
            shape((NB, 2 * HALF, HD), BF16),
            shape((SIDES * NZ, QUARTER, HD), BF16),
        ),
        in_specs=[SMEM, SMEM, SMEM] + [ANY] * 8,
        out_specs=(ANY,) * 5,
        scratch_shapes=[
            pltpu.VMEM((NB, ROWS, HD), BF16),
            pltpu.VMEM((NB, Q_AT, HD), BF16),
            pltpu.VMEM((SIDES * NZ, QUARTER, HD), BF16),
            pltpu.VMEM((SIDES * NZ, QUARTER, HD), BF16),
            pltpu.VMEM((SIDES, 2 * BS, HD), BF16),
            pltpu.VMEM((SIDES, 2 * BS, HD), BF16),
            pltpu.VMEM((NB, BS, 2 * HD), BF16),
            table,
            table,
            pltpu.VMEM((NB, BS, BS), F32),
            near,
            near,
            near,
            near,
            pltpu.VMEM((8, BS), F32),
            pltpu.VMEM((NB, BS, 2 * HD), F32),
            pltpu.VMEM((NB, BACK, HD), BF16),
            pltpu.VMEM((NB, 2 * HALF, HD), BF16),
            sems,
            sems,
            pltpu.SemaphoreType.DMA((2,)),
            pltpu.SemaphoreType.DMA((SIDES,)),
            pltpu.SemaphoreType.DMA((SIDES,)),
            sems,
            sems,
        ],
        compiler_params=PARAMS,
        name="attention",
    )(*operands)


def body(queries, keys, values, out_grad, chain_bias, chain_of_block, key_valid, neighbours):
    swap = [(0, 1), (1, 0)]
    info = jnp.stack([lax.axis_index(name) for name in ("c", "yl", "x", "yh")]).astype(jnp.int32)

    whole = pl.BlockSpec((HALF, NZ * SLOTS * HD), lambda x: (0, 0))
    packed = pl.pallas_call(
        pack_kernel,
        grid=(NX,),
        out_shape=shape((NB, ROWS, HD), BF16),
        in_specs=[
            SMEM,
            SMEM,
            whole,
            whole,
            whole,
            pl.BlockSpec((2, BS), lambda x: (0, 0)),
            pl.BlockSpec((2, NBR), lambda x: (0, 0)),
        ],
        out_specs=pl.BlockSpec((NB // NX, ROWS, HD), lambda x: (x, 0, 0)),
        scratch_shapes=[pltpu.VMEM((META, BS), F32)],
        compiler_params=FULL,
        name="pack",
    )(info, chain_of_block, queries, keys, values, key_valid.reshape(2, BS), neighbours)
    four = shape((NX, 2 * BS, HD), BF16)
    keep, sent = pl.pallas_call(
        pack_grad_kernel,
        out_shape=(four, four),
        in_specs=[SMEM, VMEM],
        out_specs=(VMEM, VMEM),
        compiler_params=FULL,
        name="pack_grad",
    )(info, out_grad)

    def along_x(kept, came, onward):
        moved = []
        for d in range(1, NX):
            pairs = [(i, i ^ d) for i in range(NX) if (i ^ d if onward else i) < SLOTS // NYH]
            moved.append(lax.ppermute(jnp.stack([kept[d], came[d]]), "x", pairs))
        return moved

    came = lax.ppermute(sent, "yh", swap)
    packed, keep, came = lax.optimization_barrier((packed, keep, came))
    rows = lax.all_to_all(packed, CHIPS, split_axis=0, concat_axis=0, tiled=True)
    grads = along_x(keep, came, True)
    rows, grads = lax.optimization_barrier((rows, grads))
    grads = [keep, came] + grads
    other = lax.ppermute(rows, "c", swap)
    theirs = lax.dynamic_index_in_dim(
        rows.reshape(SIDES, NYL, NZ, ROWS, HD)[:, :, :, Q_AT:],
        1 - lax.axis_index("yl"),
        axis=1,
        keepdims=False,
    )
    lower = lax.ppermute(theirs.reshape(SIDES * NZ, QUARTER, HD), "yl", swap)
    lists = jnp.stack(
        [
            rows.reshape(NB // NZ, NZ, ROWS, HD)[:, 0, 2 * HALF : 2 * HALF + 4],
            other.reshape(NB // NZ, NZ, ROWS, HD)[:, 0, 2 * HALF : 2 * HALF + 4],
        ]
    )
    lists = lists.astype(jnp.int32).reshape(2 * NB, HD)

    att_keep, att_swap, back, far, lower = attend(info, lists, chain_bias, rows, other, lower, *grads)

    came = lax.ppermute(far, "c", swap)
    lower_came = lax.ppermute(lower, "yl", swap)
    att_came = lax.ppermute(att_swap, "yh", swap)
    sems = pltpu.SemaphoreType.DMA((PARTS,))
    back = pl.pallas_call(
        merge_kernel,
        out_shape=shape((NB, BACK, HD), BF16),
        in_specs=[SMEM, ANY, ANY, ANY],
        out_specs=ANY,
        scratch_shapes=[
            pltpu.VMEM((NB, 2 * HALF, HD), BF16),
            pltpu.VMEM((NB, 2 * HALF, HD), BF16),
            sems,
            sems,
            sems,
            pltpu.SemaphoreType.DMA((SIDES,)),
        ],
        input_output_aliases={1: 0},
        compiler_params=PARAMS,
        name="merge",
    )(info, back, came, lower_came)
    back, att_keep, att_came = lax.optimization_barrier((back, att_keep, att_came))
    back = lax.all_to_all(back, CHIPS, split_axis=0, concat_axis=0, tiled=True)
    moved = along_x(att_keep, att_came, False)
    attended = pl.pallas_call(
        join_kernel,
        out_shape=shape((2 * BS, SLOTS * HD), BF16),
        in_specs=[SMEM] + [ANY] * 5,
        out_specs=ANY,
        scratch_shapes=[pltpu.SemaphoreType.DMA((SIDES,))],
        compiler_params=PARAMS,
        name="join",
    )(info, att_keep, att_came, *moved)
    flat = shape((HALF, NZ * SLOTS * HD), BF16)
    dq, dk, dv = pl.pallas_call(
        unpack_kernel,
        out_shape=(flat, flat, flat),
        in_specs=[SMEM, ANY],
        out_specs=(VMEM,) * 3,
        scratch_shapes=[
            pltpu.VMEM((NB, BACK, HD), BF16),
            pltpu.SemaphoreType.DMA((SLOTS // NYH,)),
        ],
        compiler_params=PARAMS,
        name="unpack",
    )(info, back)
    return attended, dq, dk, dv


def solution(mesh):
    grid = Mesh(mesh.devices.reshape(NX, NYH, NYL, NC, NZ), ("x", "yh", "yl", "c", "z"))
    res = ("x", "yh", "yl", "c")
    both = P(res + ("z",), None)
    return jax.shard_map(
        body,
        mesh=grid,
        in_specs=(both, both, both, P(res, "z"), P("z"), P(res), P(res), P(res, None)),
        out_specs=(P(res, "z"), both, both, both),
        check_vma=False,
    )
```

time: 187 us -> 170 us (0.909)
  blocking collectives: 54.3 us -> 0 us
  waiting for transfers between devices: 50.4 us -> 80 us
  starting transfers between devices: 14.7 us -> 39.6 us
  Pallas kernels: 54.6 us -> 45 us
  local copies, waits for them, and re-layouts: 6.4 us -> 2.72 us
  other arithmetic: 3.96 us -> 0.74 us
    ppermute x1 -> x11, waiting for transfers between devices: 0.01 us -> 77.5 us  [the longest x6 57.5 us: along_x(): moved.append(lax.ppermute(jnp.stack([kept[d], came[d]]), 'x', pairs))]
    all_to_all x1 -> x0, blocking collectives: 54.3 us -> none  [body(): rows = lax.all_to_all(rows, CHIPS, split_axis=0, concat_axis=0, tiled=True)]
    all_to_all x1, waiting for transfers between devices: 38.1 us -> 0.01 us  [body(): back = lax.all_to_all(back, CHIPS, split_axis=0, concat_axis=0, tiled=True)]
    ppermute x1 -> x11, starting transfers between devices: 0.01 us -> 20.1 us  [the longest x6 17.1 us: along_x(): moved.append(lax.ppermute(jnp.stack([kept[d], came[d]]), 'x', pairs))]
    all_to_all x2 -> x1, waiting for transfers between devices: 11.5 us -> 2.48 us  [body(): lax.all_to_all(packed, CHIPS, split_axis=0, concat_axis=0, tiled=True)]
    pallas_call x3, Pallas kernels: 46.1 us -> 37.8 us  [the longest x1 32.5 us: attend(): pl.pallas_call(attention_kernel, out_shape=(four, four, shape((NB, BACK,...]
    all_to_all x2 -> x1, starting transfers between devices: 7.75 us -> 11.7 us  [body(): lax.all_to_all(packed, CHIPS, split_axis=0, concat_axis=0, tiled=True)]
    unnamed x8 -> x6, local copies, waits for them, and re-layouts: 3.84 us -> 0.01 us
  transfers between devices with their start and end apart: 5 -> 14, of which waited for: 4 -> 11; matrix products, arithmetic and copies ran while one was open for 1% -> 2% of each run, Pallas kernels for 6% -> 5%
where the time goes in v2:
time: 170 us; the launch traced here: 169 us
  waiting for transfers between devices  80 us (47%)
  Pallas kernels  45 us (26%)
  starting transfers between devices  39.6 us (23%)
  local copies, waits for them, and re-layouts  2.72 us (2%)
    ppermute x6, waiting for transfers between devices, along_x(): moved.append(lax.ppermute(jnp.stack([kept[d], came[d]]), 'x', pairs))  57.5 us
    pallas_call x1, Pallas kernels, attend(): pl.pallas_call(attention_kernel, out_shape=(four, four, shape((NB, BACK,...  32.5 us
    ppermute x6, starting transfers between devices, along_x(): moved.append(lax.ppermute(jnp.stack([kept[d], came[d]]), 'x', pairs))  17.1 us
    all_to_all x1, starting transfers between devices, body(): lax.all_to_all(packed, CHIPS, split_axis=0, concat_axis=0, tiled=True)  11.7 us
    ppermute x1, waiting for transfers between devices, body(): lower_came = lax.ppermute(lower, 'yl', swap)  8.54 us
    all_to_all x1, starting transfers between devices, body(): back = lax.all_to_all(back, CHIPS, split_axis=0, concat_axis=0, tiled=True)  7.72 us
    ppermute x1, waiting for transfers between devices, body(): came = lax.ppermute(sent, 'yh', swap)  3.96 us
    ppermute x1, waiting for transfers between devices, body(): other = lax.ppermute(rows, 'c', swap)  3.64 us
  transfers between devices with their start and end apart: 14, of which 11 were waited for; matrix products, arithmetic and copies ran while one was open for 2% of the time, Pallas kernels for 5%

profile of v2, /device:TPU:8, one launch (start us, length us, event | category | flops | bytes accessed | tf_op | source)
XLA Modules:
  0.0 168.9 jit_solution(10085432651851163346)
XLA Ops:
  0.6 0.6 pad_add_fusion.info_ref
  1.2 1.9 %pack_grad.1 = (bf16[4,256,128]{2,1,0:T(8,128)(2,1)}, bf16[4,256,128]{2,1,0:T(8,128)(2,1)}) custom-call(s32[4]{0:T(128)} %pad_add_fusion.info_ref, bf16[256,768]{1,0:T(8,128)(2,1)} %g_ref.1), custom_call_target="tpu_custom_call" | custom-call | tf_op jit(solution)/shard_map/pack_grad/pallas_call | solution.py:545
  3.1 2.3 %collective-permute-start = (bf16[4,256,128]{2,1,0:T(8,128)(2,1)}, bf16[4,256,128]{2,1,0:T(8,128)(2,1)S(1)}, u32[]{:S(2)}, u32[]{:S(2)}) collective-permute-start(bf16[4,256,128]{2,1,0:T(8,128)(2,1)} %get-tuple-element.25), channel_id=1, source_target_pairs={{0,16},{16,0},{1,17},{17,1},{2,18},{18,2},{3,19},{19,3},{4,20},{20... | collective-permute-start | bytes 786440 | tf_op jit(solution)/shard_map/ppermute | solution.py:561
  5.4 3.5 %pack.1 = bf16[64,176,128]{2,1,0:T(8,128)(2,1)} custom-call(s32[4]{0:T(128)} %pad_add_fusion.info_ref, s32[2]{0:T(128)} %chain_ref.1, bf16[64,3072]{1,0:T(8,128)(2,1)} %q_ref.1, bf16[64,3072]{1,0:T(8,128)(2,1)} %k_ref.1, bf16[64,3072]{1,0:T(8,128)(2,1)} %v_ref.1, s32[2,128]{1,0:T(2,128)} %bitcast.21, s32[2,16]{1,0:T(2,128)} %near_ref.1), custom_call_target="tpu_custom_call" | custom-call | tf_op jit(solution)/shard_map/pack/pallas_call | solution.py:526
  8.9 4.0 %collective-permute-done.grad_came_hbm = bf16[4,256,128]{2,1,0:T(8,128)(2,1)S(1)} collective-permute-done((bf16[4,256,128]{2,1,0:T(8,128)(2,1)}, bf16[4,256,128]{2,1,0:T(8,128)(2,1)S(1)}, u32[]{:S(2)}, u32[]{:S(2)}) %collective-permute-start) | collective-permute-done | bytes 262176 | tf_op jit(solution)/shard_map/ppermute | solution.py:561
  12.9 11.7 %all-to-all-start = ((bf16[64,176,128]{2,1,0:T(8,128)(2,1)}), bf16[64,176,128]{2,1,0:T(8,128)(2,1)}, u32[]{:S(2)}, u32[]{:S(2)}) async-start(bf16[64,176,128]{2,1,0:T(8,128)(2,1)} %pack.1), calls=%async_computation | async-start | bytes 5767168 | tf_op jit(solution)/shard_map/all_to_all | solution.py:563
  24.7 3.4 %collective-permute-start.1 = (bf16[2,256,128]{2,1,0:T(8,128)(2,1)S(1)}, bf16[2,256,128]{2,1,0:T(8,128)(2,1)S(1)}, u32[]{:S(2)}, u32[]{:S(2)}) collective-permute-start(bf16[2,256,128]{2,1,0:T(8,128)(2,1)S(1)} %pad_maximum_fusion), channel_id=1, source_target_pairs={{0,32},{32,0},{96,64},{1,33},{33,1},{97,65},{2,34},{34,2},{98,66},... | collective-permute-start | bytes 393224 | tf_op jit(solution)/shard_map/ppermute | solution.py:558
  28.1 2.9 %collective-permute-start.2 = (bf16[2,256,128]{2,1,0:T(8,128)(2,1)S(1)}, bf16[2,256,128]{2,1,0:T(8,128)(2,1)S(1)}, u32[]{:S(2)}, u32[]{:S(2)}) collective-permute-start(bf16[2,256,128]{2,1,0:T(8,128)(2,1)S(1)} %pad_maximum_fusion.1), channel_id=1, source_target_pairs={{0,64},{64,0},{96,32},{1,65},{65,1},{97,33},{2,66},{66,2},{98,34},... | collective-permute-start | bytes 393224 | tf_op jit(solution)/shard_map/ppermute | solution.py:558
  31.1 1.3 collective-permute-start.3
  32.4 26.4 %collective-permute-done.1.grad_1_hbm = bf16[2,256,128]{2,1,0:T(8,128)(2,1)S(1)} collective-permute-done((bf16[2,256,128]{2,1,0:T(8,128)(2,1)S(1)}, bf16[2,256,128]{2,1,0:T(8,128)(2,1)S(1)}, u32[]{:S(2)}, u32[]{:S(2)}) %collective-permute-start.1) | collective-permute-done | bytes 131104 | tf_op jit(solution)/shard_map/ppermute | solution.py:558
  58.7 1.6 collective-permute-done.2.grad_2_hbm
  60.4 2.6 %collective-permute-done.3.grad_3_hbm = bf16[2,256,128]{2,1,0:T(8,128)(2,1)S(1)} collective-permute-done((bf16[2,256,128]{2,1,0:T(8,128)(2,1)S(1)}, bf16[2,256,128]{2,1,0:T(8,128)(2,1)S(1)}, u32[]{:S(2)}, u32[]{:S(2)}) %collective-permute-start.3) | collective-permute-done | bytes 131104 | tf_op jit(solution)/shard_map/ppermute | solution.py:558
  63.0 2.5 %all-to-all-done.rows_hbm = bf16[64,176,128]{2,1,0:T(8,128)(2,1)} async-done(((bf16[64,176,128]{2,1,0:T(8,128)(2,1)}), bf16[64,176,128]{2,1,0:T(8,128)(2,1)}, u32[]{:S(2)}, u32[]{:S(2)}) %all-to-all-start) | async-done | bytes 2883616 | tf_op jit(solution)/shard_map/all_to_all | solution.py:563
  65.5 1.1 slice.62
  66.7 0.8 slice_bitcast_fusion.1
  67.4 3.6 %collective-permute-done.4.other_hbm = bf16[64,176,128]{2,1,0:T(8,128)(2,1)} collective-permute-done((bf16[64,176,128]{2,1,0:T(8,128)(2,1)}, bf16[64,176,128]{2,1,0:T(8,128)(2,1)}, u32[]{:S(2)}, u32[]{:S(2)}) %collective-permute-start.4) | collective-permute-done | bytes 2883616 | tf_op jit(solution)/shard_map/ppermute | solution.py:567
  71.1 0.8 slice_bitcast_fusion
  71.9 3.5 %collective-permute-done.5.lower_hbm = bf16[32,32,128]{2,1,0:T(8,128)(2,1)S(1)} collective-permute-done((bf16[32,32,128]{2,1,0:T(8,128)(2,1)S(1)}, bf16[32,32,128]{2,1,0:T(8,128)(2,1)S(1)}, u32[]{:S(2)}, u32[]{:S(2)}) %collective-permute-start.5) | collective-permute-done | bytes 262176 | tf_op jit(solution)/shard_map/ppermute | solution.py:574
  75.4 32.5 %attention.1 = (bf16[4,256,128]{2,1,0:T(8,128)(2,1)S(1)}, bf16[4,256,128]{2,1,0:T(8,128)(2,1)S(1)}, bf16[64,160,128]{2,1,0:T(8,128)(2,1)}, bf16[64,128,128]{2,1,0:T(8,128)(2,1)}, bf16[32,32,128]{2,1,0:T(8,128)(2,1)S(1)}) custom-call(s32[4]{0:T(128)S(1)} %copy-done.1, s32[128,128]{1,0:T(8,128)S(1)} %convert.1.lists_ref, f32[6]{0:T(128)S(1)} %copy-done.2, ...), custom_call_target="tpu_custom_call" | custom-call | tf_op jit(solution)/shard_map/attention/pallas_call | solution.py:478
  108.0 0.4 collective-permute-start.7
  108.3 0.3 collective-permute-start.8
  108.6 8.5 %collective-permute-done.7.lower_hbm = bf16[32,32,128]{2,1,0:T(8,128)(2,1)S(1)} collective-permute-done((bf16[32,32,128]{2,1,0:T(8,128)(2,1)S(1)}, bf16[32,32,128]{2,1,0:T(8,128)(2,1)S(1)}, u32[]{:S(2)}, u32[]{:S(2)}) %collective-permute-start.7) | collective-permute-done | bytes 262176 | tf_op jit(solution)/shard_map/ppermute | solution.py:586
  117.2 3.4 %merge.1 = bf16[64,160,128]{2,1,0:T(8,128)(2,1)} custom-call(s32[4]{0:T(128)S(1)} %copy-done.1, bf16[64,160,128]{2,1,0:T(8,128)(2,1)} %get-tuple-element.33.back_hbm, bf16[64,128,128]{2,1,0:T(8,128)(2,1)S(1)} %collective-permute-done.6.came_hbm, bf16[32,32,128]{2,1,0:T(8,128)(2,1)S(1)} %collective-permute-done.7.lower_hbm), custom_call_target="tpu_custom_call", output_to_operand_aliasing={{}: (1, {})} | custom-call | tf_op jit(solution)/shard_map/merge/pallas_call | solution.py:589
  120.6 0.3 collective-permute-done.8.came_hbm
  120.8 7.7 %all-to-all-start.1 = ((bf16[64,160,128]{2,1,0:T(8,128)(2,1)}), bf16[64,160,128]{2,1,0:T(8,128)(2,1)S(1)}, u32[]{:S(2)}, u32[]{:S(2)}) async-start(bf16[64,160,128]{2,1,0:T(8,128)(2,1)} %merge.1), calls=%async_computation.1 | async-start | bytes 5242880 | tf_op jit(solution)/shard_map/all_to_all | solution.py:607
  128.6 3.4 %collective-permute-start.9 = (bf16[2,256,128]{2,1,0:T(8,128)(2,1)S(1)}, bf16[2,256,128]{2,1,0:T(8,128)(2,1)S(1)}, u32[]{:S(2)}, u32[]{:S(2)}) collective-permute-start(bf16[2,256,128]{2,1,0:T(8,128)(2,1)S(1)} %pad_maximum_fusion.3), channel_id=1, source_target_pairs={{0,32},{32,0},{64,96},{1,33},{33,1},{65,97},{2,34},{34,2},{66,98},... | collective-permute-start | bytes 393224 | tf_op jit(solution)/shard_map/ppermute | solution.py:558
  132.1 4.8 %collective-permute-start.10 = (bf16[2,256,128]{2,1,0:T(8,128)(2,1)S(1)}, bf16[2,256,128]{2,1,0:T(8,128)(2,1)S(1)}, u32[]{:S(2)}, u32[]{:S(2)}) collective-permute-start(bf16[2,256,128]{2,1,0:T(8,128)(2,1)S(1)} %pad_maximum_fusion.4), channel_id=1, source_target_pairs={{0,64},{32,96},{64,0},{1,65},{33,97},{65,1},{2,66},{34,98},{66,2},... | collective-permute-start | bytes 393224 | tf_op jit(solution)/shard_map/ppermute | solution.py:558
  136.9 1.3 collective-permute-start.11
  138.2 23.9 %collective-permute-done.9.one_hbm = bf16[2,256,128]{2,1,0:T(8,128)(2,1)S(1)} collective-permute-done((bf16[2,256,128]{2,1,0:T(8,128)(2,1)S(1)}, bf16[2,256,128]{2,1,0:T(8,128)(2,1)S(1)}, u32[]{:S(2)}, u32[]{:S(2)}) %collective-permute-start.9) | collective-permute-done | bytes 131104 | tf_op jit(solution)/shard_map/ppermute | solution.py:558
  162.1 3.0 %collective-permute-done.10.two_hbm = bf16[2,256,128]{2,1,0:T(8,128)(2,1)S(1)} collective-permute-done((bf16[2,256,128]{2,1,0:T(8,128)(2,1)S(1)}, bf16[2,256,128]{2,1,0:T(8,128)(2,1)S(1)}, u32[]{:S(2)}, u32[]{:S(2)}) %collective-permute-start.10) | collective-permute-done | bytes 131104 | tf_op jit(solution)/shard_map/ppermute | solution.py:558
  165.1 1.4 join.1
  166.5 2.4 %unpack.1 = (bf16[64,3072]{1,0:T(8,128)(2,1)}, bf16[64,3072]{1,0:T(8,128)(2,1)}, bf16[64,3072]{1,0:T(8,128)(2,1)}) custom-call(s32[4]{0:T(128)S(1)} %copy-done.1, bf16[64,160,128]{2,1,0:T(8,128)(2,1)S(1)} %all-to-all-done.1.rows_hbm), custom_call_target="tpu_custom_call" | custom-call | tf_op jit(solution)/shard_map/unpack/pallas_call | solution.py:619
  (24 shorter events, 0.4 us)
Async XLA Ops:
  3.1 9.8 %collective-permute-start = (bf16[4,256,128]{2,1,0:T(8,128)(2,1)}, bf16[4,256,128]{2,1,0:T(8,128)(2,1)S(1)}, u32[]{:S(2)}, u32[]{:S(2)}) collective-permute-start(bf16[4,256,128]{2,1,0:T(8,128)(2,1)} %get-tuple-element.25), channel_id=1, source_target_pairs={{0,16},{16,0},{1,17},{17,1},{2,18},{18,2},{3,19},{19,3},{4,20},{20... | collective-permute-start | bytes 786440 | tf_op jit(solution)/shard_map/ppermute | solution.py:561
  12.9 11.7 %copy-start = (bf16[4,256,128]{2,1,0:T(8,128)(2,1)S(1)}, bf16[4,256,128]{2,1,0:T(8,128)(2,1)}, u32[]{:S(2)}) copy-start(bf16[4,256,128]{2,1,0:T(8,128)(2,1)} %get-tuple-element.27.grad_keep_hbm) | copy-start | bytes 786436
  12.9 52.6 %all-to-all-start = ((bf16[64,176,128]{2,1,0:T(8,128)(2,1)}), bf16[64,176,128]{2,1,0:T(8,128)(2,1)}, u32[]{:S(2)}, u32[]{:S(2)}) async-start(bf16[64,176,128]{2,1,0:T(8,128)(2,1)} %pack.1), calls=%async_computation | async-start | bytes 5767168 | tf_op jit(solution)/shard_map/all_to_all | solution.py:563
  24.6 50.8 %copy-start.1 = (s32[4]{0:T(128)S(1)}, s32[4]{0:T(128)}, u32[]{:S(2)}) copy-start(s32[4]{0:T(128)} %pad_add_fusion.info_ref) | copy-start | bytes 52
  24.6 50.7 %copy-start.2 = (f32[6]{0:T(128)S(1)}, f32[6]{0:T(128)}, u32[]{:S(2)}) copy-start(f32[6]{0:T(128)} %bias_ref.1) | copy-start | bytes 76
  24.7 34.0 %collective-permute-start.1 = (bf16[2,256,128]{2,1,0:T(8,128)(2,1)S(1)}, bf16[2,256,128]{2,1,0:T(8,128)(2,1)S(1)}, u32[]{:S(2)}, u32[]{:S(2)}) collective-permute-start(bf16[2,256,128]{2,1,0:T(8,128)(2,1)S(1)} %pad_maximum_fusion), channel_id=1, source_target_pairs={{0,32},{32,0},{96,64},{1,33},{33,1},{97,65},{2,34},{34,2},{98,66},... | collective-permute-start | bytes 393224 | tf_op jit(solution)/shard_map/ppermute | solution.py:558
  28.1 32.2 %collective-permute-start.2 = (bf16[2,256,128]{2,1,0:T(8,128)(2,1)S(1)}, bf16[2,256,128]{2,1,0:T(8,128)(2,1)S(1)}, u32[]{:S(2)}, u32[]{:S(2)}) collective-permute-start(bf16[2,256,128]{2,1,0:T(8,128)(2,1)S(1)} %pad_maximum_fusion.1), channel_id=1, source_target_pairs={{0,64},{64,0},{96,32},{1,65},{65,1},{97,33},{2,66},{66,2},{98,34},... | collective-permute-start | bytes 393224 | tf_op jit(solution)/shard_map/ppermute | solution.py:558
  31.1 31.9 %collective-permute-start.3 = (bf16[2,256,128]{2,1,0:T(8,128)(2,1)S(1)}, bf16[2,256,128]{2,1,0:T(8,128)(2,1)S(1)}, u32[]{:S(2)}, u32[]{:S(2)}) collective-permute-start(bf16[2,256,128]{2,1,0:T(8,128)(2,1)S(1)} %pad_maximum_fusion.2), channel_id=1, source_target_pairs={{32,64},{64,32},{96,0},{33,65},{65,33},{97,1},{34,66},{66,34},{98,... | collective-permute-start | bytes 393224 | tf_op jit(solution)/shard_map/ppermute | solution.py:558
  65.5 5.6 %collective-permute-start.4 = (bf16[64,176,128]{2,1,0:T(8,128)(2,1)}, bf16[64,176,128]{2,1,0:T(8,128)(2,1)}, u32[]{:S(2)}, u32[]{:S(2)}) collective-permute-start(bf16[64,176,128]{2,1,0:T(8,128)(2,1)} %all-to-all-done.rows_hbm), channel_id=1, source_target_pairs={{0,4},{4,0},{1,5},{5,1},{2,6},{6,2},{3,7},{7,3},{8,12},{12,8},{9,1... | collective-permute-start | bytes 8650760 | tf_op jit(solution)/shard_map/ppermute | solution.py:567
  66.6 8.8 %collective-permute-start.5 = (bf16[32,32,128]{2,1,0:T(8,128)(2,1)S(1)}, bf16[32,32,128]{2,1,0:T(8,128)(2,1)S(1)}, u32[]{:S(2)}, u32[]{:S(2)}) collective-permute-start(bf16[32,32,128]{2,1,0:T(8,128)(2,1)S(1)} %bitcast.19), channel_id=1, source_target_pairs={{0,8},{8,0},{1,9},{9,1},{2,10},{10,2},{3,11},{11,3},{4,12},{12,4},... | collective-permute-start | bytes 786440 | tf_op jit(solution)/shard_map/ppermute | solution.py:574
  107.9 9.3 %collective-permute-start.6 = (bf16[64,128,128]{2,1,0:T(8,128)(2,1)}, bf16[64,128,128]{2,1,0:T(8,128)(2,1)S(1)}, u32[]{:S(2)}, u32[]{:S(2)}) collective-permute-start(bf16[64,128,128]{2,1,0:T(8,128)(2,1)} %get-tuple-element.34), channel_id=1, source_target_pairs={{0,4},{4,0},{1,5},{5,1},{2,6},{6,2},{3,7},{7,3},{8,12},{12,8},{9,1... | collective-permute-start | bytes 6291464 | tf_op jit(solution)/shard_map/ppermute | solution.py:585
  108.0 9.2 %collective-permute-start.7 = (bf16[32,32,128]{2,1,0:T(8,128)(2,1)S(1)}, bf16[32,32,128]{2,1,0:T(8,128)(2,1)S(1)}, u32[]{:S(2)}, u32[]{:S(2)}) collective-permute-start(bf16[32,32,128]{2,1,0:T(8,128)(2,1)S(1)} %get-tuple-element.35), channel_id=1, source_target_pairs={{0,8},{8,0},{1,9},{9,1},{2,10},{10,2},{3,11},{11,3},{4,12},{12,4},... | collective-permute-start | bytes 786440 | tf_op jit(solution)/shard_map/ppermute | solution.py:586
  108.3 12.5 %collective-permute-start.8 = (bf16[4,256,128]{2,1,0:T(8,128)(2,1)S(1)}, bf16[4,256,128]{2,1,0:T(8,128)(2,1)S(1)}, u32[]{:S(2)}, u32[]{:S(2)}) collective-permute-start(bf16[4,256,128]{2,1,0:T(8,128)(2,1)S(1)} %get-tuple-element.37), channel_id=1, source_target_pairs={{0,16},{16,0},{1,17},{17,1},{2,18},{18,2},{3,19},{19,3},{4,20},{20... | collective-permute-start | bytes 786440 | tf_op jit(solution)/shard_map/ppermute | solution.py:587
  120.8 45.7 %all-to-all-start.1 = ((bf16[64,160,128]{2,1,0:T(8,128)(2,1)}), bf16[64,160,128]{2,1,0:T(8,128)(2,1)S(1)}, u32[]{:S(2)}, u32[]{:S(2)}) async-start(bf16[64,160,128]{2,1,0:T(8,128)(2,1)} %merge.1), calls=%async_computation.1 | async-start | bytes 5242880 | tf_op jit(solution)/shard_map/all_to_all | solution.py:607
  128.6 33.5 %collective-permute-start.9 = (bf16[2,256,128]{2,1,0:T(8,128)(2,1)S(1)}, bf16[2,256,128]{2,1,0:T(8,128)(2,1)S(1)}, u32[]{:S(2)}, u32[]{:S(2)}) collective-permute-start(bf16[2,256,128]{2,1,0:T(8,128)(2,1)S(1)} %pad_maximum_fusion.3), channel_id=1, source_target_pairs={{0,32},{32,0},{64,96},{1,33},{33,1},{65,97},{2,34},{34,2},{66,98},... | collective-permute-start | bytes 393224 | tf_op jit(solution)/shard_map/ppermute | solution.py:558
  132.1 33.1 %collective-permute-start.10 = (bf16[2,256,128]{2,1,0:T(8,128)(2,1)S(1)}, bf16[2,256,128]{2,1,0:T(8,128)(2,1)S(1)}, u32[]{:S(2)}, u32[]{:S(2)}) collective-permute-start(bf16[2,256,128]{2,1,0:T(8,128)(2,1)S(1)} %pad_maximum_fusion.4), channel_id=1, source_target_pairs={{0,64},{32,96},{64,0},{1,65},{33,97},{65,1},{2,66},{34,98},{66,2},... | collective-permute-start | bytes 393224 | tf_op jit(solution)/shard_map/ppermute | solution.py:558
  136.9 28.2 %collective-permute-start.11 = (bf16[2,256,128]{2,1,0:T(8,128)(2,1)S(1)}, bf16[2,256,128]{2,1,0:T(8,128)(2,1)S(1)}, u32[]{:S(2)}, u32[]{:S(2)}) collective-permute-start(bf16[2,256,128]{2,1,0:T(8,128)(2,1)S(1)} %pad_maximum_fusion.5), channel_id=1, source_target_pairs={{0,96},{32,64},{64,32},{1,97},{33,65},{65,33},{2,98},{34,66},{66,3... | collective-permute-start | bytes 393224 | tf_op jit(solution)/shard_map/ppermute | solution.py:558

commit v3 on v2

--- a/solution.py
+++ b/solution.py
@@ -78,13 +78,12 @@
         rows_ref[dest, 2 * HALF : Q_AT] = held
 
 
-def pack_grad_kernel(info_ref, g_ref, keep_ref, swap_ref):
+def pack_grad_kernel(info_ref, g_ref, *grad_refs):
     x, yh = info_ref[2], info_ref[3]
-    for d in range(NX):
+    for d, ref in enumerate(grad_refs):
         first = jnp.minimum(x ^ d, SLOTS // NYH - 1) * NYH
-        for ref, side in ((keep_ref, yh), (swap_ref, 1 - yh)):
-            start = pl.multiple_of((first + side) * HD, HD)
-            ref[d] = g_ref[:, pl.ds(start, HD)]
+        for n, side in enumerate((yh, 1 - yh)):
+            ref[n] = g_ref[:, pl.ds(pl.multiple_of((first + side) * HD, HD), HD)]
 
 
 def dot(a, b):
@@ -93,13 +92,14 @@
 
 def attention_kernel(
     info_ref,
+    near_ref,
     lists_ref,
     bias_ref,
     rows_hbm,
     other_hbm,
     lower_hbm,
-    grad_keep_hbm,
     grad_came_hbm,
+    grad_0_hbm,
     grad_1_hbm,
     grad_2_hbm,
     grad_3_hbm,
@@ -158,9 +158,9 @@
 
     rows_in = copies(rows_hbm, rows_ref, rows_sem, ROWS)
     other_in = copies(other_hbm, other_ref, other_sem, Q_AT)
-    grad_pieces = [(grad_keep_hbm.at[0], grad_came_hbm.at[0])]
-    for ref in (grad_1_hbm, grad_2_hbm, grad_3_hbm):
-        grad_pieces.append((ref.at[0], ref.at[1]))
+    grad_pieces = []
+    for d, ref in enumerate((grad_0_hbm, grad_1_hbm, grad_2_hbm, grad_3_hbm)):
+        grad_pieces.append((ref.at[0], grad_came_hbm.at[d]))
     grads_in = []
     att_out = []
     for d, pieces in enumerate(grad_pieces):
@@ -204,7 +204,7 @@
                 fill(k * (part // 4) + m, base, ref)
                 return 0
 
-            lax.fori_loop(0, part // 4, fill_one, 0)
+            lax.fori_loop(0, part // 4, fill_one, 0, unroll=2)
     lower_in.wait()
     for copy in grads_in:
         copy.wait()
@@ -232,10 +232,11 @@
 
     def listed(i, j):
         _, half, quad = place(i)
-        n = lists_ref[quad * 4 + 2 + half, j]
-        far = ((n // 2) % 2 != core).astype(jnp.int32)
-        line = far * NB + (n // 4) * 4 + 2 + n % 2
-        return far * (NB // 2) + (n // 4) * 2 + n % 2, line
+        return near_ref[quad * 2 + half, j]
+
+    def chain_at(i, j):
+        _, half, quad = place(i)
+        return lists_ref[near_ref[quad * 2 + half, NBR + j], NBR]
 
     class Scores:
         def __init__(self, i, parity):
@@ -247,8 +248,8 @@
             self.peak = jnp.full((8, BS), -jnp.inf, F32)
 
         def step(self, j):
-            slot, line = listed(self.i, j)
-            shift = jnp.where(lists_ref[line, NBR] != self.chain, bias, 0.0)
+            slot = listed(self.i, j)
+            shift = jnp.where(chain_at(self.i, j) != self.chain, bias, 0.0)
             both = dot(kv[slot], self.into)
             score = both[:, :BS] * (SCALE * LOG2E) + (mask[slot] + shift)
             scores[j] = score
@@ -270,7 +271,7 @@
             row = jnp.exp2(scores[j] - self.peak)
             weights[j] = row
             self.total = self.total + jnp.sum(row.reshape(BS // 8, 8, BS), axis=0)
-            self.held.append((row.astype(BF16), vt[listed(self.i, j)[0]]))
+            self.held.append((row.astype(BF16), vt[listed(self.i, j)]))
             if j % 2:
                 (r0, v0), (r1, v1) = self.held
                 self.held = []
@@ -298,7 +299,7 @@
             self.held = []
 
         def step(self, j):
-            slot, _ = listed(self.i, j)
+            slot = listed(self.i, j)
             probs = weights[j] * self.inverse
             dscore = (probs * (self.dprob[j] - self.delta)).astype(BF16)
             both = jnp.concatenate([dscore, probs.astype(BF16)], axis=1)
@@ -419,7 +420,38 @@
         copy.wait()
 
 
-def unpack_kernel(info_ref, rows_hbm, dq_ref, dk_ref, dv_ref, rows_ref, sems):
+def join(info_ref, pieces, out_hbm, sems, act):
+    x, yh = info_ref[2], info_ref[3]
+    for d, pair in enumerate(pieces):
+        first = (x ^ d) * NYH
+
+        @pl.when(first < SLOTS)
+        def _(d=d, pair=pair, first=first):
+            for n, side in enumerate((yh, 1 - yh)):
+                lane = pl.ds(pl.multiple_of((first + side) * HD, HD), HD)
+                act(pltpu.make_async_copy(pair[n], out_hbm.at[:, lane], sems.at[d * 2 + n]))
+
+
+def unpack_kernel(
+    info_ref,
+    rows_hbm,
+    keep_hbm,
+    came_hbm,
+    one_hbm,
+    two_hbm,
+    three_hbm,
+    dq_ref,
+    dk_ref,
+    dv_ref,
+    att_hbm,
+    rows_ref,
+    sems,
+    att_sems,
+):
+    pieces = [(keep_hbm.at[0], came_hbm.at[0])]
+    for ref in (one_hbm, two_hbm, three_hbm):
+        pieces.append((ref.at[0], ref.at[1]))
+    join(info_ref, pieces, att_hbm, att_sems, lambda copy: copy.start())
     low = info_ref[1]
     each = NB // NX
     copies = [
@@ -444,26 +476,7 @@
                     part = slice(t * HALF, (t + 1) * HALF)
                     both = rows_ref[zero, part].astype(F32) + rows_ref[one, part].astype(F32)
                     ref[:, lane] = both.astype(BF16)
-
-
-def join_kernel(info_ref, keep_hbm, came_hbm, one_hbm, two_hbm, three_hbm, out_hbm, sems):
-    x, yh = info_ref[2], info_ref[3]
-    pieces = [(keep_hbm.at[0], came_hbm.at[0])]
-    for ref in (one_hbm, two_hbm, three_hbm):
-        pieces.append((ref.at[0], ref.at[1]))
-
-    def each(act):
-        for d, pair in enumerate(pieces):
-            first = (x ^ d) * NYH
-
-            @pl.when(first < SLOTS)
-            def _(d=d, pair=pair, first=first):
-                for n, side in enumerate((yh, 1 - yh)):
-                    lane = pl.ds(pl.multiple_of((first + side) * HD, HD), HD)
-                    act(pltpu.make_async_copy(pair[n], out_hbm.at[:, lane], sems.at[d * 2 + n]))
-
-    each(lambda copy: copy.start())
-    each(lambda copy: copy.wait())
+    join(info_ref, pieces, att_hbm, att_sems, lambda copy: copy.wait())
 
 
 def shape(dims, dtype):
@@ -484,7 +497,7 @@
             shape((NB, 2 * HALF, HD), BF16),
             shape((SIDES * NZ, QUARTER, HD), BF16),
         ),
-        in_specs=[SMEM, SMEM, SMEM] + [ANY] * 8,
+        in_specs=[SMEM] * 4 + [ANY] * 8,
         out_specs=(ANY,) * 5,
         scratch_shapes=[
             pltpu.VMEM((NB, ROWS, HD), BF16),
@@ -541,29 +554,29 @@
         compiler_params=FULL,
         name="pack",
     )(info, chain_of_block, queries, keys, values, key_valid.reshape(2, BS), neighbours)
-    four = shape((NX, 2 * BS, HD), BF16)
-    keep, sent = pl.pallas_call(
+    packed, out_grad = lax.optimization_barrier((packed, out_grad))
+    rows = lax.all_to_all(packed, CHIPS, split_axis=0, concat_axis=0, tiled=True)
+    grads = pl.pallas_call(
         pack_grad_kernel,
-        out_shape=(four, four),
+        out_shape=(shape((2, 2 * BS, HD), BF16),) * NX,
         in_specs=[SMEM, VMEM],
-        out_specs=(VMEM, VMEM),
+        out_specs=(VMEM,) * NX,
         compiler_params=FULL,
         name="pack_grad",
     )(info, out_grad)
 
-    def along_x(kept, came, onward):
+    def along_x(pieces, onward):
         moved = []
-        for d in range(1, NX):
+        for d, piece in enumerate(pieces, 1):
             pairs = [(i, i ^ d) for i in range(NX) if (i ^ d if onward else i) < SLOTS // NYH]
-            moved.append(lax.ppermute(jnp.stack([kept[d], came[d]]), "x", pairs))
+            moved.append(lax.ppermute(piece, "x", pairs))
         return moved
 
-    came = lax.ppermute(sent, "yh", swap)
-    packed, keep, came = lax.optimization_barrier((packed, keep, came))
-    rows = lax.all_to_all(packed, CHIPS, split_axis=0, concat_axis=0, tiled=True)
-    grads = along_x(keep, came, True)
-    rows, grads = lax.optimization_barrier((rows, grads))
-    grads = [keep, came] + grads
+    moved = along_x(grads[1:], True)
+    rows, moved = lax.optimization_barrier((rows, moved))
+    grads = [grads[0]] + moved
+    came = lax.ppermute(jnp.stack([piece[1] for piece in grads]), "yh", swap)
+    grads = [came] + grads
     other = lax.ppermute(rows, "c", swap)
     theirs = lax.dynamic_index_in_dim(
         rows.reshape(SIDES, NYL, NZ, ROWS, HD)[:, :, :, Q_AT:],
@@ -572,15 +585,16 @@
         keepdims=False,
     )
     lower = lax.ppermute(theirs.reshape(SIDES * NZ, QUARTER, HD), "yl", swap)
-    lists = jnp.stack(
-        [
-            rows.reshape(NB // NZ, NZ, ROWS, HD)[:, 0, 2 * HALF : 2 * HALF + 4],
-            other.reshape(NB // NZ, NZ, ROWS, HD)[:, 0, 2 * HALF : 2 * HALF + 4],
-        ]
-    )
-    lists = lists.astype(jnp.int32).reshape(2 * NB, HD)
-
-    att_keep, att_swap, back, far, lower = attend(info, lists, chain_bias, rows, other, lower, *grads)
+    mine = rows.reshape(NB // NZ, NZ, ROWS, HD)[:, 0, 2 * HALF : 2 * HALF + 4]
+    far = other.reshape(NB // NZ, NZ, ROWS, HD)[:, 0, 2 * HALF : 2 * HALF + 4]
+    lists = jnp.stack([mine, far]).astype(jnp.int32).reshape(2 * NB, HD)
+    block = mine[:, 2:, :NBR].astype(jnp.int32)
+    away = (block // 2 % 2 != lax.axis_index("c")).astype(jnp.int32)
+    there = block // 4
+    slots = away * (NB // 2) + there * 2 + block % 2
+    lines = away * NB + there * 4 + 2 + block % 2
+    near = jnp.concatenate([slots, lines], axis=-1).reshape(NB // 2, 2 * NBR)
+    att_keep, att_swap, back, far, lower = attend(info, near, lists, chain_bias, rows, other, lower, *grads)
 
     came = lax.ppermute(far, "c", swap)
     lower_came = lax.ppermute(lower, "yl", swap)
@@ -605,29 +619,21 @@
     )(info, back, came, lower_came)
     back, att_keep, att_came = lax.optimization_barrier((back, att_keep, att_came))
     back = lax.all_to_all(back, CHIPS, split_axis=0, concat_axis=0, tiled=True)
-    moved = along_x(att_keep, att_came, False)
-    attended = pl.pallas_call(
-        join_kernel,
-        out_shape=shape((2 * BS, SLOTS * HD), BF16),
-        in_specs=[SMEM] + [ANY] * 5,
-        out_specs=ANY,
-        scratch_shapes=[pltpu.SemaphoreType.DMA((SIDES,))],
-        compiler_params=PARAMS,
-        name="join",
-    )(info, att_keep, att_came, *moved)
+    moved = along_x([jnp.stack([att_keep[d], att_came[d]]) for d in range(1, NX)], False)
     flat = shape((HALF, NZ * SLOTS * HD), BF16)
-    dq, dk, dv = pl.pallas_call(
+    dq, dk, dv, attended = pl.pallas_call(
         unpack_kernel,
-        out_shape=(flat, flat, flat),
-        in_specs=[SMEM, ANY],
-        out_specs=(VMEM,) * 3,
+        out_shape=(flat, flat, flat, shape((2 * BS, SLOTS * HD), BF16)),
+        in_specs=[SMEM] + [ANY] * 6,
+        out_specs=(VMEM, VMEM, VMEM, ANY),
         scratch_shapes=[
             pltpu.VMEM((NB, BACK, HD), BF16),
             pltpu.SemaphoreType.DMA((SLOTS // NYH,)),
+            pltpu.SemaphoreType.DMA((SIDES,)),
         ],
         compiler_params=PARAMS,
         name="unpack",
-    )(info, back)
+    )(info, back, att_keep, att_came, *moved)
     return attended, dq, dk, dv
 
 

time: 170 us -> 167 us (0.982)
  waiting for transfers between devices: 80 us -> 76.6 us
  Pallas kernels: 45 us -> 42.2 us
  starting transfers between devices: 39.6 us -> 42 us
    ppermute x1, waiting for transfers between devices: 8.54 us -> 5.19 us  [body(): lower_came = lax.ppermute(lower, 'yl', swap)]
    ppermute x1, waiting for transfers between devices: 0.29 us -> 3.64 us  [body(): att_came = lax.ppermute(att_swap, 'yh', swap)]
    ppermute x1, waiting for transfers between devices: 3.64 us -> 0.66 us  [body(): other = lax.ppermute(rows, 'c', swap)]
    ppermute x1, starting transfers between devices: 0.29 us -> 3.24 us  [body(): att_came = lax.ppermute(att_swap, 'yh', swap)]
    ppermute x7, starting transfers between devices: 19.4 us -> 17.3 us  [the longest x6 17.2 us: along_x(): moved.append(lax.ppermute(piece, 'x', pairs))]
    pallas_call x3 -> x2, Pallas kernels: 5.66 us -> 4.44 us  [the longest x1 2.54 us: body(): pl.pallas_call(unpack_kernel, out_shape=(flat, flat, flat, shape((2 * BS,...]
  transfers between devices with their start and end apart: 14 -> 14, of which waited for: 11 -> 11; matrix products, arithmetic and copies ran while one was open for 2% -> 2% of each run, Pallas kernels for 5% -> 3%
where the time goes in v3:
time: 167 us; the launch traced here: 166 us
  waiting for transfers between devices  76.6 us (46%)
  Pallas kernels  42.2 us (25%)
  starting transfers between devices  42 us (25%)
  local copies, waits for them, and re-layouts  3.55 us (2%)
    ppermute x6, waiting for transfers between devices, along_x(): moved.append(lax.ppermute(piece, 'x', pairs))  56.6 us
    pallas_call x1, Pallas kernels, attend(): pl.pallas_call(attention_kernel, out_shape=(four, four, shape((NB, BACK,...  30.8 us
    ppermute x6, starting transfers between devices, along_x(): moved.append(lax.ppermute(piece, 'x', pairs))  17.2 us
    all_to_all x1, starting transfers between devices, body(): lax.all_to_all(packed, CHIPS, split_axis=0, concat_axis=0, tiled=True)  11.6 us
    all_to_all x1, starting transfers between devices, body(): back = lax.all_to_all(back, CHIPS, split_axis=0, concat_axis=0, tiled=True)  7.35 us
    ppermute x1, waiting for transfers between devices, body(): lower_came = lax.ppermute(lower, 'yl', swap)  5.19 us
    ppermute x1, waiting for transfers between devices, body(): came = lax.ppermute(jnp.stack([piece[1] for piece in grads]), 'yh', swap)  5.17 us
    ppermute x1, waiting for transfers between devices, body(): att_came = lax.ppermute(att_swap, 'yh', swap)  3.64 us
  transfers between devices with their start and end apart: 14, of which 11 were waited for; matrix products, arithmetic and copies ran while one was open for 2% of the time, Pallas kernels for 3%

profile of v3, /device:TPU:8, one launch (start us, length us, event | category | flops | bytes accessed | tf_op | source)
XLA Modules:
  0.0 166.3 jit_solution(10271896365916249164)
XLA Ops:
  0.6 0.7 pad_add_fusion.1.info_ref
  1.3 3.5 %pack.1 = bf16[64,176,128]{2,1,0:T(8,128)(2,1)} custom-call(s32[4]{0:T(128)} %pad_add_fusion.1.info_ref, s32[2]{0:T(128)} %chain_ref.1, bf16[64,3072]{1,0:T(8,128)(2,1)} %q_ref.1, bf16[64,3072]{1,0:T(8,128)(2,1)} %k_ref.1, bf16[64,3072]{1,0:T(8,128)(2,1)} %v_ref.1, s32[2,128]{1,0:T(2,128)} %bitcast.26, s32[2,16]{1,0:T(2,128)} %near_ref.1), custom_call_target="tpu_custom_call" | custom-call | tf_op jit(solution)/shard_map/pack/pallas_call | solution.py:539
  4.8 11.6 %all-to-all-start = ((bf16[64,176,128]{2,1,0:T(8,128)(2,1)}), bf16[64,176,128]{2,1,0:T(8,128)(2,1)}, u32[]{:S(2)}, u32[]{:S(2)}) async-start(bf16[64,176,128]{2,1,0:T(8,128)(2,1)} %pack.1), calls=%async_computation | async-start | bytes 5767168 | tf_op jit(solution)/shard_map/all_to_all | solution.py:558
  16.4 1.9 %pack_grad.1 = (bf16[2,256,128]{2,1,0:T(8,128)(2,1)}, bf16[2,256,128]{2,1,0:T(8,128)(2,1)}, bf16[2,256,128]{2,1,0:T(8,128)(2,1)}, bf16[2,256,128]{2,1,0:T(8,128)(2,1)}) custom-call(s32[4]{0:T(128)} %pad_add_fusion.1.info_ref, bf16[256,768]{1,0:T(8,128)(2,1)} %g_ref), custom_call_target="tpu_custom_call" | custom-call | tf_op jit(solution)/shard_map/pack_grad/pallas_call | solution.py:559
  18.3 3.5 %collective-permute-start = (bf16[2,256,128]{2,1,0:T(8,128)(2,1)}, bf16[2,256,128]{2,1,0:T(8,128)(2,1)S(1)}, u32[]{:S(2)}, u32[]{:S(2)}) collective-permute-start(bf16[2,256,128]{2,1,0:T(8,128)(2,1)} %get-tuple-element.28), channel_id=1, source_target_pairs={{0,32},{32,0},{96,64},{1,33},{33,1},{97,65},{2,34},{34,2},{98,66},... | collective-permute-start | bytes 393224 | tf_op jit(solution)/shard_map/ppermute | solution.py:572
  21.8 2.9 %collective-permute-start.1 = (bf16[2,256,128]{2,1,0:T(8,128)(2,1)}, bf16[2,256,128]{2,1,0:T(8,128)(2,1)S(1)}, u32[]{:S(2)}, u32[]{:S(2)}) collective-permute-start(bf16[2,256,128]{2,1,0:T(8,128)(2,1)} %get-tuple-element.29), channel_id=1, source_target_pairs={{0,64},{64,0},{96,32},{1,65},{65,1},{97,33},{2,66},{66,2},{98,34},... | collective-permute-start | bytes 393224 | tf_op jit(solution)/shard_map/ppermute | solution.py:572
  24.7 1.3 collective-permute-start.2
  26.0 26.1 %collective-permute-done.grad_1_hbm = bf16[2,256,128]{2,1,0:T(8,128)(2,1)S(1)} collective-permute-done((bf16[2,256,128]{2,1,0:T(8,128)(2,1)}, bf16[2,256,128]{2,1,0:T(8,128)(2,1)S(1)}, u32[]{:S(2)}, u32[]{:S(2)}) %collective-permute-start) | collective-permute-done | bytes 131104 | tf_op jit(solution)/shard_map/ppermute | solution.py:572
  52.1 1.2 collective-permute-done.1.grad_2_hbm
  53.3 2.3 %collective-permute-done.2.grad_3_hbm = bf16[2,256,128]{2,1,0:T(8,128)(2,1)S(1)} collective-permute-done((bf16[2,256,128]{2,1,0:T(8,128)(2,1)}, bf16[2,256,128]{2,1,0:T(8,128)(2,1)S(1)}, u32[]{:S(2)}, u32[]{:S(2)}) %collective-permute-start.2) | collective-permute-done | bytes 131104 | tf_op jit(solution)/shard_map/ppermute | solution.py:572
  55.6 2.1 %all-to-all-done.rows_hbm = bf16[64,176,128]{2,1,0:T(8,128)(2,1)} async-done(((bf16[64,176,128]{2,1,0:T(8,128)(2,1)}), bf16[64,176,128]{2,1,0:T(8,128)(2,1)}, u32[]{:S(2)}, u32[]{:S(2)}) %all-to-all-start) | async-done | bytes 2883616 | tf_op jit(solution)/shard_map/all_to_all | solution.py:558
  57.7 0.8 slice.46
  58.7 1.1 slice.59
  59.9 1.7 %collective-permute-start.4 = (bf16[32,32,128]{2,1,0:T(8,128)(2,1)S(1)}, bf16[32,32,128]{2,1,0:T(8,128)(2,1)S(1)}, u32[]{:S(2)}, u32[]{:S(2)}) collective-permute-start(bf16[32,32,128]{2,1,0:T(8,128)(2,1)S(1)} %bitcast.24), channel_id=1, source_target_pairs={{0,8},{8,0},{1,9},{9,1},{2,10},{10,2},{3,11},{11,3},{4,12},{12,4},... | collective-permute-start | bytes 786440 | tf_op jit(solution)/shard_map/ppermute | solution.py:587
  61.6 0.8 slice_bitcast_fusion.2
  62.7 0.7 collective-permute-done.3.other_hbm
  63.3 0.8 slice_bitcast_fusion
  64.1 5.2 %collective-permute-done.5.grad_came_hbm = bf16[4,256,128]{2,1,0:T(8,128)(2,1)S(1)} collective-permute-done((bf16[4,256,128]{2,1,0:T(8,128)(2,1)S(1)}, bf16[4,256,128]{2,1,0:T(8,128)(2,1)S(1)}, u32[]{:S(2)}, u32[]{:S(2)}) %collective-permute-start.5) | collective-permute-done | bytes 262176 | tf_op jit(solution)/shard_map/ppermute | solution.py:578
  69.3 3.3 %collective-permute-done.4.lower_hbm = bf16[32,32,128]{2,1,0:T(8,128)(2,1)S(1)} collective-permute-done((bf16[32,32,128]{2,1,0:T(8,128)(2,1)S(1)}, bf16[32,32,128]{2,1,0:T(8,128)(2,1)S(1)}, u32[]{:S(2)}, u32[]{:S(2)}) %collective-permute-start.4) | collective-permute-done | bytes 262176 | tf_op jit(solution)/shard_map/ppermute | solution.py:587
  72.7 30.8 %attention.1 = (bf16[4,256,128]{2,1,0:T(8,128)(2,1)S(1)}, bf16[4,256,128]{2,1,0:T(8,128)(2,1)S(1)}, bf16[64,160,128]{2,1,0:T(8,128)(2,1)}, bf16[64,128,128]{2,1,0:T(8,128)(2,1)S(1)}, bf16[32,32,128]{2,1,0:T(8,128)(2,1)S(1)}) custom-call(s32[4]{0:T(128)S(1)} %copy-done.1, s32[32,32]{1,0:T(8,128)S(1)} %bitcast.23, s32[128,128]{1,0:T(8,128)S(1)} %convert.1.lists_ref, ...), custom_call_target="tpu_custom_call" | custom-call | tf_op jit(solution)/shard_map/attention/pallas_call | solution.py:491
  103.6 0.8 collective-permute-start.7
  104.4 3.2 %collective-permute-start.8 = (bf16[4,256,128]{2,1,0:T(8,128)(2,1)S(1)}, bf16[4,256,128]{2,1,0:T(8,128)(2,1)S(1)}, u32[]{:S(2)}, u32[]{:S(2)}) collective-permute-start(bf16[4,256,128]{2,1,0:T(8,128)(2,1)S(1)} %get-tuple-element.40), channel_id=1, source_target_pairs={{0,16},{16,0},{1,17},{17,1},{2,18},{18,2},{3,19},{19,3},{4,20},{20... | collective-permute-start | bytes 786440 | tf_op jit(solution)/shard_map/ppermute | solution.py:601
  107.6 5.2 %collective-permute-done.7.lower_hbm = bf16[32,32,128]{2,1,0:T(8,128)(2,1)S(1)} collective-permute-done((bf16[32,32,128]{2,1,0:T(8,128)(2,1)S(1)}, bf16[32,32,128]{2,1,0:T(8,128)(2,1)S(1)}, u32[]{:S(2)}, u32[]{:S(2)}) %collective-permute-start.7) | collective-permute-done | bytes 262176 | tf_op jit(solution)/shard_map/ppermute | solution.py:600
  112.8 3.4 %merge.1 = bf16[64,160,128]{2,1,0:T(8,128)(2,1)} custom-call(s32[4]{0:T(128)S(1)} %copy-done.1, bf16[64,160,128]{2,1,0:T(8,128)(2,1)} %get-tuple-element.36.back_hbm, bf16[64,128,128]{2,1,0:T(8,128)(2,1)S(1)} %collective-permute-done.6.came_hbm, bf16[32,32,128]{2,1,0:T(8,128)(2,1)S(1)} %collective-permute-done.7.lower_hbm), custom_call_target="tpu_custom_call", output_to_operand_aliasing={{}: (1, {})} | custom-call | tf_op jit(solution)/shard_map/merge/pallas_call | solution.py:603
  116.2 3.6 %collective-permute-done.8.came_hbm = bf16[4,256,128]{2,1,0:T(8,128)(2,1)S(1)} collective-permute-done((bf16[4,256,128]{2,1,0:T(8,128)(2,1)S(1)}, bf16[4,256,128]{2,1,0:T(8,128)(2,1)S(1)}, u32[]{:S(2)}, u32[]{:S(2)}) %collective-permute-start.8) | collective-permute-done | bytes 262176 | tf_op jit(solution)/shard_map/ppermute | solution.py:601
  119.8 7.4 %all-to-all-start.1 = ((bf16[64,160,128]{2,1,0:T(8,128)(2,1)}), bf16[64,160,128]{2,1,0:T(8,128)(2,1)S(1)}, u32[]{:S(2)}, u32[]{:S(2)}) async-start(bf16[64,160,128]{2,1,0:T(8,128)(2,1)} %merge.1), calls=%async_computation.1 | async-start | bytes 5242880 | tf_op jit(solution)/shard_map/all_to_all | solution.py:621
  127.3 3.4 %collective-permute-start.9 = (bf16[2,256,128]{2,1,0:T(8,128)(2,1)S(1)}, bf16[2,256,128]{2,1,0:T(8,128)(2,1)S(1)}, u32[]{:S(2)}, u32[]{:S(2)}) collective-permute-start(bf16[2,256,128]{2,1,0:T(8,128)(2,1)S(1)} %pad_maximum_fusion.1), channel_id=1, source_target_pairs={{0,32},{32,0},{64,96},{1,33},{33,1},{65,97},{2,34},{34,2},{66,98},... | collective-permute-start | bytes 393224 | tf_op jit(solution)/shard_map/ppermute | solution.py:572
  130.7 4.8 %collective-permute-start.10 = (bf16[2,256,128]{2,1,0:T(8,128)(2,1)S(1)}, bf16[2,256,128]{2,1,0:T(8,128)(2,1)S(1)}, u32[]{:S(2)}, u32[]{:S(2)}) collective-permute-start(bf16[2,256,128]{2,1,0:T(8,128)(2,1)S(1)} %pad_maximum_fusion.2), channel_id=1, source_target_pairs={{0,64},{32,96},{64,0},{1,65},{33,97},{65,1},{2,66},{34,98},{66,2},... | collective-permute-start | bytes 393224 | tf_op jit(solution)/shard_map/ppermute | solution.py:572
  135.5 1.3 collective-permute-start.11
  136.8 23.9 %collective-permute-done.9.one_hbm = bf16[2,256,128]{2,1,0:T(8,128)(2,1)S(1)} collective-permute-done((bf16[2,256,128]{2,1,0:T(8,128)(2,1)S(1)}, bf16[2,256,128]{2,1,0:T(8,128)(2,1)S(1)}, u32[]{:S(2)}, u32[]{:S(2)}) %collective-permute-start.9) | collective-permute-done | bytes 131104 | tf_op jit(solution)/shard_map/ppermute | solution.py:572
  160.7 3.0 %collective-permute-done.10.two_hbm = bf16[2,256,128]{2,1,0:T(8,128)(2,1)S(1)} collective-permute-done((bf16[2,256,128]{2,1,0:T(8,128)(2,1)S(1)}, bf16[2,256,128]{2,1,0:T(8,128)(2,1)S(1)}, u32[]{:S(2)}, u32[]{:S(2)}) %collective-permute-start.10) | collective-permute-done | bytes 131104 | tf_op jit(solution)/shard_map/ppermute | solution.py:572
  163.8 2.5 %unpack.1 = (bf16[64,3072]{1,0:T(8,128)(2,1)}, bf16[64,3072]{1,0:T(8,128)(2,1)}, bf16[64,3072]{1,0:T(8,128)(2,1)}, bf16[256,768]{1,0:T(8,128)(2,1)}) custom-call(s32[4]{0:T(128)S(1)} %copy-done.1, bf16[64,160,128]{2,1,0:T(8,128)(2,1)S(1)} %all-to-all-done.1.rows_hbm, bf16[4,256,128]{2,1,0:T(8,128)(2,1)S(1)} %get-tuple-element.42.keep_hbm, ...), custom_call_target="tpu_custom_call" | custom-call | tf_op jit(solution)/shard_map/unpack/pallas_call | solution.py:624
  (26 shorter events, 0.7 us)
Async XLA Ops:
  4.8 52.9 %all-to-all-start = ((bf16[64,176,128]{2,1,0:T(8,128)(2,1)}), bf16[64,176,128]{2,1,0:T(8,128)(2,1)}, u32[]{:S(2)}, u32[]{:S(2)}) async-start(bf16[64,176,128]{2,1,0:T(8,128)(2,1)} %pack.1), calls=%async_computation | async-start | bytes 5767168 | tf_op jit(solution)/shard_map/all_to_all | solution.py:558
  16.4 56.3 %copy-start.1 = (s32[4]{0:T(128)S(1)}, s32[4]{0:T(128)}, u32[]{:S(2)}) copy-start(s32[4]{0:T(128)} %pad_add_fusion.1.info_ref) | copy-start | bytes 52
  16.4 56.3 %copy-start.2 = (f32[6]{0:T(128)S(1)}, f32[6]{0:T(128)}, u32[]{:S(2)}) copy-start(f32[6]{0:T(128)} %bias_ref.1) | copy-start | bytes 76
  18.3 54.4 %copy-start = (bf16[2,256,128]{2,1,0:T(8,128)(2,1)S(1)}, bf16[2,256,128]{2,1,0:T(8,128)(2,1)}, u32[]{:S(2)}) copy-start(bf16[2,256,128]{2,1,0:T(8,128)(2,1)} %get-tuple-element.32.grad_0_hbm) | copy-start | bytes 393220
  18.3 33.8 %collective-permute-start = (bf16[2,256,128]{2,1,0:T(8,128)(2,1)}, bf16[2,256,128]{2,1,0:T(8,128)(2,1)S(1)}, u32[]{:S(2)}, u32[]{:S(2)}) collective-permute-start(bf16[2,256,128]{2,1,0:T(8,128)(2,1)} %get-tuple-element.28), channel_id=1, source_target_pairs={{0,32},{32,0},{96,64},{1,33},{33,1},{97,65},{2,34},{34,2},{98,66},... | collective-permute-start | bytes 393224 | tf_op jit(solution)/shard_map/ppermute | solution.py:572
  21.8 31.5 %collective-permute-start.1 = (bf16[2,256,128]{2,1,0:T(8,128)(2,1)}, bf16[2,256,128]{2,1,0:T(8,128)(2,1)S(1)}, u32[]{:S(2)}, u32[]{:S(2)}) collective-permute-start(bf16[2,256,128]{2,1,0:T(8,128)(2,1)} %get-tuple-element.29), channel_id=1, source_target_pairs={{0,64},{64,0},{96,32},{1,65},{65,1},{97,33},{2,66},{66,2},{98,34},... | collective-permute-start | bytes 393224 | tf_op jit(solution)/shard_map/ppermute | solution.py:572
  24.7 30.9 %collective-permute-start.2 = (bf16[2,256,128]{2,1,0:T(8,128)(2,1)}, bf16[2,256,128]{2,1,0:T(8,128)(2,1)S(1)}, u32[]{:S(2)}, u32[]{:S(2)}) collective-permute-start(bf16[2,256,128]{2,1,0:T(8,128)(2,1)} %get-tuple-element.30), channel_id=1, source_target_pairs={{32,64},{64,32},{96,0},{33,65},{65,33},{97,1},{34,66},{66,34},{98,... | collective-permute-start | bytes 393224 | tf_op jit(solution)/shard_map/ppermute | solution.py:572
  57.7 5.6 %collective-permute-start.3 = (bf16[64,176,128]{2,1,0:T(8,128)(2,1)}, bf16[64,176,128]{2,1,0:T(8,128)(2,1)}, u32[]{:S(2)}, u32[]{:S(2)}) collective-permute-start(bf16[64,176,128]{2,1,0:T(8,128)(2,1)} %all-to-all-done.rows_hbm), channel_id=1, source_target_pairs={{0,4},{4,0},{1,5},{5,1},{2,6},{6,2},{3,7},{7,3},{8,12},{12,8},{9,1... | collective-permute-start | bytes 8650760 | tf_op jit(solution)/shard_map/ppermute | solution.py:580
  58.6 10.7 %collective-permute-start.5 = (bf16[4,256,128]{2,1,0:T(8,128)(2,1)S(1)}, bf16[4,256,128]{2,1,0:T(8,128)(2,1)S(1)}, u32[]{:S(2)}, u32[]{:S(2)}) collective-permute-start(bf16[4,256,128]{2,1,0:T(8,128)(2,1)S(1)} %pad_maximum_fusion), channel_id=1, source_target_pairs={{0,16},{16,0},{1,17},{17,1},{2,18},{18,2},{3,19},{19,3},{4,20},{20... | collective-permute-start | bytes 786440 | tf_op jit(solution)/shard_map/ppermute | solution.py:578
  59.9 12.8 %collective-permute-start.4 = (bf16[32,32,128]{2,1,0:T(8,128)(2,1)S(1)}, bf16[32,32,128]{2,1,0:T(8,128)(2,1)S(1)}, u32[]{:S(2)}, u32[]{:S(2)}) collective-permute-start(bf16[32,32,128]{2,1,0:T(8,128)(2,1)S(1)} %bitcast.24), channel_id=1, source_target_pairs={{0,8},{8,0},{1,9},{9,1},{2,10},{10,2},{3,11},{11,3},{4,12},{12,4},... | collective-permute-start | bytes 786440 | tf_op jit(solution)/shard_map/ppermute | solution.py:587
  103.5 9.3 %collective-permute-start.6 = (bf16[64,128,128]{2,1,0:T(8,128)(2,1)S(1)}, bf16[64,128,128]{2,1,0:T(8,128)(2,1)S(1)}, u32[]{:S(2)}, u32[]{:S(2)}) collective-permute-start(bf16[64,128,128]{2,1,0:T(8,128)(2,1)S(1)} %get-tuple-element.37), channel_id=1, source_target_pairs={{0,4},{4,0},{1,5},{5,1},{2,6},{6,2},{3,7},{7,3},{8,12},{12,8},{9,1... | collective-permute-start | bytes 6291464 | tf_op jit(solution)/shard_map/ppermute | solution.py:599
  103.6 9.2 %collective-permute-start.7 = (bf16[32,32,128]{2,1,0:T(8,128)(2,1)S(1)}, bf16[32,32,128]{2,1,0:T(8,128)(2,1)S(1)}, u32[]{:S(2)}, u32[]{:S(2)}) collective-permute-start(bf16[32,32,128]{2,1,0:T(8,128)(2,1)S(1)} %get-tuple-element.38), channel_id=1, source_target_pairs={{0,8},{8,0},{1,9},{9,1},{2,10},{10,2},{3,11},{11,3},{4,12},{12,4},... | collective-permute-start | bytes 786440 | tf_op jit(solution)/shard_map/ppermute | solution.py:600
  104.4 15.5 %collective-permute-start.8 = (bf16[4,256,128]{2,1,0:T(8,128)(2,1)S(1)}, bf16[4,256,128]{2,1,0:T(8,128)(2,1)S(1)}, u32[]{:S(2)}, u32[]{:S(2)}) collective-permute-start(bf16[4,256,128]{2,1,0:T(8,128)(2,1)S(1)} %get-tuple-element.40), channel_id=1, source_target_pairs={{0,16},{16,0},{1,17},{17,1},{2,18},{18,2},{3,19},{19,3},{4,20},{20... | collective-permute-start | bytes 786440 | tf_op jit(solution)/shard_map/ppermute | solution.py:601
  119.8 43.9 %all-to-all-start.1 = ((bf16[64,160,128]{2,1,0:T(8,128)(2,1)}), bf16[64,160,128]{2,1,0:T(8,128)(2,1)S(1)}, u32[]{:S(2)}, u32[]{:S(2)}) async-start(bf16[64,160,128]{2,1,0:T(8,128)(2,1)} %merge.1), calls=%async_computation.1 | async-start | bytes 5242880 | tf_op jit(solution)/shard_map/all_to_all | solution.py:621
  127.3 33.5 %collective-permute-start.9 = (bf16[2,256,128]{2,1,0:T(8,128)(2,1)S(1)}, bf16[2,256,128]{2,1,0:T(8,128)(2,1)S(1)}, u32[]{:S(2)}, u32[]{:S(2)}) collective-permute-start(bf16[2,256,128]{2,1,0:T(8,128)(2,1)S(1)} %pad_maximum_fusion.1), channel_id=1, source_target_pairs={{0,32},{32,0},{64,96},{1,33},{33,1},{65,97},{2,34},{34,2},{66,98},... | collective-permute-start | bytes 393224 | tf_op jit(solution)/shard_map/ppermute | solution.py:572
  130.7 33.1 %collective-permute-start.10 = (bf16[2,256,128]{2,1,0:T(8,128)(2,1)S(1)}, bf16[2,256,128]{2,1,0:T(8,128)(2,1)S(1)}, u32[]{:S(2)}, u32[]{:S(2)}) collective-permute-start(bf16[2,256,128]{2,1,0:T(8,128)(2,1)S(1)} %pad_maximum_fusion.2), channel_id=1, source_target_pairs={{0,64},{32,96},{64,0},{1,65},{33,97},{65,1},{2,66},{34,98},{66,2},... | collective-permute-start | bytes 393224 | tf_op jit(solution)/shard_map/ppermute | solution.py:572
  135.5 28.3 %collective-permute-start.11 = (bf16[2,256,128]{2,1,0:T(8,128)(2,1)S(1)}, bf16[2,256,128]{2,1,0:T(8,128)(2,1)S(1)}, u32[]{:S(2)}, u32[]{:S(2)}) collective-permute-start(bf16[2,256,128]{2,1,0:T(8,128)(2,1)S(1)} %pad_maximum_fusion.3), channel_id=1, source_target_pairs={{0,96},{32,64},{64,32},{1,97},{33,65},{65,33},{2,98},{34,66},{66,3... | collective-permute-start | bytes 393224 | tf_op jit(solution)/shard_map/ppermute | solution.py:572

commit v4 on v3

--- a/solution.py
+++ b/solution.py
@@ -25,7 +25,7 @@
 SCALE = 1.0 / math.sqrt(HD)
 LOG2E = math.log2(math.e)
 CHIPS = ("x", "yh", "yl", "z")
-PARTS = 4
+PARTS = 8
 ANY = pl.BlockSpec(memory_space=pl.ANY)
 VMEM = pl.BlockSpec(memory_space=pltpu.VMEM)
 SMEM = pl.BlockSpec(memory_space=pltpu.SMEM)
@@ -598,6 +598,7 @@
 
     came = lax.ppermute(far, "c", swap)
     lower_came = lax.ppermute(lower, "yl", swap)
+    att_swap, came = lax.optimization_barrier((att_swap, came))
     att_came = lax.ppermute(att_swap, "yh", swap)
     sems = pltpu.SemaphoreType.DMA((PARTS,))
     back = pl.pallas_call(

time: 167 us -> 168 us (level)
  waiting for transfers between devices: 76.6 us -> 78.5 us
    ppermute x1, waiting for transfers between devices: 0.01 us -> 3.37 us  [body(): came = lax.ppermute(far, 'c', swap)]
    ppermute x1, waiting for transfers between devices: 5.19 us -> 3.15 us  [body(): lower_came = lax.ppermute(lower, 'yl', swap)]
    ppermute x1, starting transfers between devices: 3.24 us -> 1.43 us  [body(): att_came = lax.ppermute(att_swap, 'yh', swap)]
  transfers between devices with their start and end apart: 14 -> 14, of which waited for: 11 -> 12; matrix products, arithmetic and copies ran while one was open for 2% -> 2% of each run, Pallas kernels for 3% -> 3%
where the time goes in v4:
time: 168 us; the launch traced here: 167 us
  waiting for transfers between devices  78.5 us (47%)
  Pallas kernels  42.5 us (25%)
  starting transfers between devices  40.4 us (24%)
  local copies, waits for them, and re-layouts  3.55 us (2%)
    ppermute x6, waiting for transfers between devices, along_x(): moved.append(lax.ppermute(piece, 'x', pairs))  56.6 us
    pallas_call x1, Pallas kernels, attend(): pl.pallas_call(attention_kernel, out_shape=(four, four, shape((NB, BACK,...  31.2 us
    ppermute x6, starting transfers between devices, along_x(): moved.append(lax.ppermute(piece, 'x', pairs))  17.2 us
    all_to_all x1, starting transfers between devices, body(): lax.all_to_all(packed, CHIPS, split_axis=0, concat_axis=0, tiled=True)  11.6 us
    all_to_all x1, starting transfers between devices, body(): back = lax.all_to_all(back, CHIPS, split_axis=0, concat_axis=0, tiled=True)  7.34 us
    ppermute x1, waiting for transfers between devices, body(): came = lax.ppermute(jnp.stack([piece[1] for piece in grads]), 'yh', swap)  5.17 us
    ppermute x1, waiting for transfers between devices, body(): att_came = lax.ppermute(att_swap, 'yh', swap)  4.18 us
    pallas_call x1, Pallas kernels, body(): pl.pallas_call(pack_kernel, grid=(NX,), out_shape=shape((NB, ROWS, HD), B...  3.51 us
  transfers between devices with their start and end apart: 14, of which 12 were waited for; matrix products, arithmetic and copies ran while one was open for 2% of the time, Pallas kernels for 3%

profile of v4, /device:TPU:8, one launch (start us, length us, event | category | flops | bytes accessed | tf_op | source)
XLA Modules:
  0.0 167.0 jit_solution(17626040340037702479)
XLA Ops:
  1.3 3.5 %pack.1 = bf16[64,176,128]{2,1,0:T(8,128)(2,1)} custom-call(s32[4]{0:T(128)} %pad_add_fusion.1.info_ref, s32[2]{0:T(128)} %chain_ref.1, bf16[64,3072]{1,0:T(8,128)(2,1)} %q_ref.1, bf16[64,3072]{1,0:T(8,128)(2,1)} %k_ref.1, bf16[64,3072]{1,0:T(8,128)(2,1)} %v_ref.1, s32[2,128]{1,0:T(2,128)} %bitcast.26, s32[2,16]{1,0:T(2,128)} %near_ref.1), custom_call_target="tpu_custom_call" | custom-call | tf_op jit(solution)/shard_map/pack/pallas_call | solution.py:539
  4.8 11.6 %all-to-all-start = ((bf16[64,176,128]{2,1,0:T(8,128)(2,1)}), bf16[64,176,128]{2,1,0:T(8,128)(2,1)}, u32[]{:S(2)}, u32[]{:S(2)}) async-start(bf16[64,176,128]{2,1,0:T(8,128)(2,1)} %pack.1), calls=%async_computation | async-start | bytes 5767168 | tf_op jit(solution)/shard_map/all_to_all | solution.py:558
  16.4 1.9 %pack_grad.1 = (bf16[2,256,128]{2,1,0:T(8,128)(2,1)}, bf16[2,256,128]{2,1,0:T(8,128)(2,1)}, bf16[2,256,128]{2,1,0:T(8,128)(2,1)}, bf16[2,256,128]{2,1,0:T(8,128)(2,1)}) custom-call(s32[4]{0:T(128)} %pad_add_fusion.1.info_ref, bf16[256,768]{1,0:T(8,128)(2,1)} %g_ref), custom_call_target="tpu_custom_call" | custom-call | tf_op jit(solution)/shard_map/pack_grad/pallas_call | solution.py:559
  18.3 3.5 %collective-permute-start = (bf16[2,256,128]{2,1,0:T(8,128)(2,1)}, bf16[2,256,128]{2,1,0:T(8,128)(2,1)S(1)}, u32[]{:S(2)}, u32[]{:S(2)}) collective-permute-start(bf16[2,256,128]{2,1,0:T(8,128)(2,1)} %get-tuple-element.30), channel_id=1, source_target_pairs={{0,32},{32,0},{96,64},{1,33},{33,1},{97,65},{2,34},{34,2},{98,66},... | collective-permute-start | bytes 393224 | tf_op jit(solution)/shard_map/ppermute | solution.py:572
  21.8 2.9 %collective-permute-start.1 = (bf16[2,256,128]{2,1,0:T(8,128)(2,1)}, bf16[2,256,128]{2,1,0:T(8,128)(2,1)S(1)}, u32[]{:S(2)}, u32[]{:S(2)}) collective-permute-start(bf16[2,256,128]{2,1,0:T(8,128)(2,1)} %get-tuple-element.31), channel_id=1, source_target_pairs={{0,64},{64,0},{96,32},{1,65},{65,1},{97,33},{2,66},{66,2},{98,34},... | collective-permute-start | bytes 393224 | tf_op jit(solution)/shard_map/ppermute | solution.py:572
  24.7 1.3 collective-permute-start.2
  26.0 26.1 %collective-permute-done.grad_1_hbm = bf16[2,256,128]{2,1,0:T(8,128)(2,1)S(1)} collective-permute-done((bf16[2,256,128]{2,1,0:T(8,128)(2,1)}, bf16[2,256,128]{2,1,0:T(8,128)(2,1)S(1)}, u32[]{:S(2)}, u32[]{:S(2)}) %collective-permute-start) | collective-permute-done | bytes 131104 | tf_op jit(solution)/shard_map/ppermute | solution.py:572
  52.1 1.2 collective-permute-done.1.grad_2_hbm
  53.3 2.3 %collective-permute-done.2.grad_3_hbm = bf16[2,256,128]{2,1,0:T(8,128)(2,1)S(1)} collective-permute-done((bf16[2,256,128]{2,1,0:T(8,128)(2,1)}, bf16[2,256,128]{2,1,0:T(8,128)(2,1)S(1)}, u32[]{:S(2)}, u32[]{:S(2)}) %collective-permute-start.2) | collective-permute-done | bytes 131104 | tf_op jit(solution)/shard_map/ppermute | solution.py:572
  55.6 2.1 %all-to-all-done.rows_hbm = bf16[64,176,128]{2,1,0:T(8,128)(2,1)} async-done(((bf16[64,176,128]{2,1,0:T(8,128)(2,1)}), bf16[64,176,128]{2,1,0:T(8,128)(2,1)}, u32[]{:S(2)}, u32[]{:S(2)}) %all-to-all-start) | async-done | bytes 2883616 | tf_op jit(solution)/shard_map/all_to_all | solution.py:558
  57.7 0.8 slice.46
  58.7 1.1 slice.59
  59.9 1.7 %collective-permute-start.4 = (bf16[32,32,128]{2,1,0:T(8,128)(2,1)S(1)}, bf16[32,32,128]{2,1,0:T(8,128)(2,1)S(1)}, u32[]{:S(2)}, u32[]{:S(2)}) collective-permute-start(bf16[32,32,128]{2,1,0:T(8,128)(2,1)S(1)} %bitcast.24), channel_id=1, source_target_pairs={{0,8},{8,0},{1,9},{9,1},{2,10},{10,2},{3,11},{11,3},{4,12},{12,4},... | collective-permute-start | bytes 786440 | tf_op jit(solution)/shard_map/ppermute | solution.py:587
  61.6 0.8 slice_bitcast_fusion.2
  62.7 0.7 collective-permute-done.3.other_hbm
  63.3 0.8 slice_bitcast_fusion
  64.1 5.2 %collective-permute-done.5.grad_came_hbm = bf16[4,256,128]{2,1,0:T(8,128)(2,1)S(1)} collective-permute-done((bf16[4,256,128]{2,1,0:T(8,128)(2,1)S(1)}, bf16[4,256,128]{2,1,0:T(8,128)(2,1)S(1)}, u32[]{:S(2)}, u32[]{:S(2)}) %collective-permute-start.5) | collective-permute-done | bytes 262176 | tf_op jit(solution)/shard_map/ppermute | solution.py:578
  69.3 3.3 %collective-permute-done.4.lower_hbm = bf16[32,32,128]{2,1,0:T(8,128)(2,1)S(1)} collective-permute-done((bf16[32,32,128]{2,1,0:T(8,128)(2,1)S(1)}, bf16[32,32,128]{2,1,0:T(8,128)(2,1)S(1)}, u32[]{:S(2)}, u32[]{:S(2)}) %collective-permute-start.4) | collective-permute-done | bytes 262176 | tf_op jit(solution)/shard_map/ppermute | solution.py:587
  72.7 31.2 %attention.1 = (bf16[4,256,128]{2,1,0:T(8,128)(2,1)S(1)}, bf16[4,256,128]{2,1,0:T(8,128)(2,1)S(1)}, bf16[64,160,128]{2,1,0:T(8,128)(2,1)}, bf16[64,128,128]{2,1,0:T(8,128)(2,1)S(1)}, bf16[32,32,128]{2,1,0:T(8,128)(2,1)S(1)}) custom-call(s32[4]{0:T(128)S(1)} %copy-done.1, s32[32,32]{1,0:T(8,128)S(1)} %bitcast.23, s32[128,128]{1,0:T(8,128)S(1)} %convert.1.lists_ref, ...), custom_call_target="tpu_custom_call" | custom-call | tf_op jit(solution)/shard_map/attention/pallas_call | solution.py:491
  104.2 0.8 collective-permute-start.7
  104.9 3.4 %collective-permute-done.6.came_hbm = bf16[64,128,128]{2,1,0:T(8,128)(2,1)S(1)} collective-permute-done((bf16[64,128,128]{2,1,0:T(8,128)(2,1)S(1)}, bf16[64,128,128]{2,1,0:T(8,128)(2,1)S(1)}, u32[]{:S(2)}, u32[]{:S(2)}) %collective-permute-start.6) | collective-permute-done | bytes 2097184 | tf_op jit(solution)/shard_map/ppermute | solution.py:599
  108.3 1.4 collective-permute-start.8
  109.7 3.1 %collective-permute-done.7.lower_hbm = bf16[32,32,128]{2,1,0:T(8,128)(2,1)S(1)} collective-permute-done((bf16[32,32,128]{2,1,0:T(8,128)(2,1)S(1)}, bf16[32,32,128]{2,1,0:T(8,128)(2,1)S(1)}, u32[]{:S(2)}, u32[]{:S(2)}) %collective-permute-start.7) | collective-permute-done | bytes 262176 | tf_op jit(solution)/shard_map/ppermute | solution.py:600
  112.9 3.3 %merge.1 = bf16[64,160,128]{2,1,0:T(8,128)(2,1)} custom-call(s32[4]{0:T(128)S(1)} %copy-done.1, bf16[64,160,128]{2,1,0:T(8,128)(2,1)} %get-tuple-element.38.back_hbm, bf16[64,128,128]{2,1,0:T(8,128)(2,1)S(1)} %collective-permute-done.6.came_hbm, bf16[32,32,128]{2,1,0:T(8,128)(2,1)S(1)} %collective-permute-done.7.lower_hbm), custom_call_target="tpu_custom_call", output_to_operand_aliasing={{}: (1, {})} | custom-call | tf_op jit(solution)/shard_map/merge/pallas_call | solution.py:604
  116.2 4.2 %collective-permute-done.8.came_hbm = bf16[4,256,128]{2,1,0:T(8,128)(2,1)S(1)} collective-permute-done((bf16[4,256,128]{2,1,0:T(8,128)(2,1)S(1)}, bf16[4,256,128]{2,1,0:T(8,128)(2,1)S(1)}, u32[]{:S(2)}, u32[]{:S(2)}) %collective-permute-start.8) | collective-permute-done | bytes 262176 | tf_op jit(solution)/shard_map/ppermute | solution.py:602
  120.4 7.3 %all-to-all-start.1 = ((bf16[64,160,128]{2,1,0:T(8,128)(2,1)}), bf16[64,160,128]{2,1,0:T(8,128)(2,1)S(1)}, u32[]{:S(2)}, u32[]{:S(2)}) async-start(bf16[64,160,128]{2,1,0:T(8,128)(2,1)} %merge.1), calls=%async_computation.1 | async-start | bytes 5242880 | tf_op jit(solution)/shard_map/all_to_all | solution.py:622
  127.8 3.4 %collective-permute-start.9 = (bf16[2,256,128]{2,1,0:T(8,128)(2,1)S(1)}, bf16[2,256,128]{2,1,0:T(8,128)(2,1)S(1)}, u32[]{:S(2)}, u32[]{:S(2)}) collective-permute-start(bf16[2,256,128]{2,1,0:T(8,128)(2,1)S(1)} %pad_maximum_fusion.1), channel_id=1, source_target_pairs={{0,32},{32,0},{64,96},{1,33},{33,1},{65,97},{2,34},{34,2},{66,98},... | collective-permute-start | bytes 393224 | tf_op jit(solution)/shard_map/ppermute | solution.py:572
  131.2 4.8 %collective-permute-start.10 = (bf16[2,256,128]{2,1,0:T(8,128)(2,1)S(1)}, bf16[2,256,128]{2,1,0:T(8,128)(2,1)S(1)}, u32[]{:S(2)}, u32[]{:S(2)}) collective-permute-start(bf16[2,256,128]{2,1,0:T(8,128)(2,1)S(1)} %pad_maximum_fusion.2), channel_id=1, source_target_pairs={{0,64},{32,96},{64,0},{1,65},{33,97},{65,1},{2,66},{34,98},{66,2},... | collective-permute-start | bytes 393224 | tf_op jit(solution)/shard_map/ppermute | solution.py:572
  136.1 1.3 collective-permute-start.11
  137.4 23.9 %collective-permute-done.9.one_hbm = bf16[2,256,128]{2,1,0:T(8,128)(2,1)S(1)} collective-permute-done((bf16[2,256,128]{2,1,0:T(8,128)(2,1)S(1)}, bf16[2,256,128]{2,1,0:T(8,128)(2,1)S(1)}, u32[]{:S(2)}, u32[]{:S(2)}) %collective-permute-start.9) | collective-permute-done | bytes 131104 | tf_op jit(solution)/shard_map/ppermute | solution.py:572
  161.3 3.0 %collective-permute-done.10.two_hbm = bf16[2,256,128]{2,1,0:T(8,128)(2,1)S(1)} collective-permute-done((bf16[2,256,128]{2,1,0:T(8,128)(2,1)S(1)}, bf16[2,256,128]{2,1,0:T(8,128)(2,1)S(1)}, u32[]{:S(2)}, u32[]{:S(2)}) %collective-permute-start.10) | collective-permute-done | bytes 131104 | tf_op jit(solution)/shard_map/ppermute | solution.py:572
  164.3 2.5 %unpack.1 = (bf16[64,3072]{1,0:T(8,128)(2,1)}, bf16[64,3072]{1,0:T(8,128)(2,1)}, bf16[64,3072]{1,0:T(8,128)(2,1)}, bf16[256,768]{1,0:T(8,128)(2,1)}) custom-call(s32[4]{0:T(128)S(1)} %copy-done.1, bf16[64,160,128]{2,1,0:T(8,128)(2,1)S(1)} %all-to-all-done.1.rows_hbm, bf16[4,256,128]{2,1,0:T(8,128)(2,1)S(1)} %get-tuple-element.46.keep_hbm, ...), custom_call_target="tpu_custom_call" | custom-call | tf_op jit(solution)/shard_map/unpack/pallas_call | solution.py:625
  (26 shorter events, 1.6 us)
Async XLA Ops:
  4.8 52.9 %all-to-all-start = ((bf16[64,176,128]{2,1,0:T(8,128)(2,1)}), bf16[64,176,128]{2,1,0:T(8,128)(2,1)}, u32[]{:S(2)}, u32[]{:S(2)}) async-start(bf16[64,176,128]{2,1,0:T(8,128)(2,1)} %pack.1), calls=%async_computation | async-start | bytes 5767168 | tf_op jit(solution)/shard_map/all_to_all | solution.py:558
  16.4 56.3 %copy-start.1 = (s32[4]{0:T(128)S(1)}, s32[4]{0:T(128)}, u32[]{:S(2)}) copy-start(s32[4]{0:T(128)} %pad_add_fusion.1.info_ref) | copy-start | bytes 52
  16.4 56.3 %copy-start.2 = (f32[6]{0:T(128)S(1)}, f32[6]{0:T(128)}, u32[]{:S(2)}) copy-start(f32[6]{0:T(128)} %bias_ref.1) | copy-start | bytes 76
  18.3 54.4 %copy-start = (bf16[2,256,128]{2,1,0:T(8,128)(2,1)S(1)}, bf16[2,256,128]{2,1,0:T(8,128)(2,1)}, u32[]{:S(2)}) copy-start(bf16[2,256,128]{2,1,0:T(8,128)(2,1)} %get-tuple-element.34.grad_0_hbm) | copy-start | bytes 393220
  18.3 33.8 %collective-permute-start = (bf16[2,256,128]{2,1,0:T(8,128)(2,1)}, bf16[2,256,128]{2,1,0:T(8,128)(2,1)S(1)}, u32[]{:S(2)}, u32[]{:S(2)}) collective-permute-start(bf16[2,256,128]{2,1,0:T(8,128)(2,1)} %get-tuple-element.30), channel_id=1, source_target_pairs={{0,32},{32,0},{96,64},{1,33},{33,1},{97,65},{2,34},{34,2},{98,66},... | collective-permute-start | bytes 393224 | tf_op jit(solution)/shard_map/ppermute | solution.py:572
  21.8 31.5 %collective-permute-start.1 = (bf16[2,256,128]{2,1,0:T(8,128)(2,1)}, bf16[2,256,128]{2,1,0:T(8,128)(2,1)S(1)}, u32[]{:S(2)}, u32[]{:S(2)}) collective-permute-start(bf16[2,256,128]{2,1,0:T(8,128)(2,1)} %get-tuple-element.31), channel_id=1, source_target_pairs={{0,64},{64,0},{96,32},{1,65},{65,1},{97,33},{2,66},{66,2},{98,34},... | collective-permute-start | bytes 393224 | tf_op jit(solution)/shard_map/ppermute | solution.py:572
  24.7 30.9 %collective-permute-start.2 = (bf16[2,256,128]{2,1,0:T(8,128)(2,1)}, bf16[2,256,128]{2,1,0:T(8,128)(2,1)S(1)}, u32[]{:S(2)}, u32[]{:S(2)}) collective-permute-start(bf16[2,256,128]{2,1,0:T(8,128)(2,1)} %get-tuple-element.32), channel_id=1, source_target_pairs={{32,64},{64,32},{96,0},{33,65},{65,33},{97,1},{34,66},{66,34},{98,... | collective-permute-start | bytes 393224 | tf_op jit(solution)/shard_map/ppermute | solution.py:572
  57.7 5.6 %collective-permute-start.3 = (bf16[64,176,128]{2,1,0:T(8,128)(2,1)}, bf16[64,176,128]{2,1,0:T(8,128)(2,1)}, u32[]{:S(2)}, u32[]{:S(2)}) collective-permute-start(bf16[64,176,128]{2,1,0:T(8,128)(2,1)} %all-to-all-done.rows_hbm), channel_id=1, source_target_pairs={{0,4},{4,0},{1,5},{5,1},{2,6},{6,2},{3,7},{7,3},{8,12},{12,8},{9,1... | collective-permute-start | bytes 8650760 | tf_op jit(solution)/shard_map/ppermute | solution.py:580
  58.6 10.7 %collective-permute-start.5 = (bf16[4,256,128]{2,1,0:T(8,128)(2,1)S(1)}, bf16[4,256,128]{2,1,0:T(8,128)(2,1)S(1)}, u32[]{:S(2)}, u32[]{:S(2)}) collective-permute-start(bf16[4,256,128]{2,1,0:T(8,128)(2,1)S(1)} %pad_maximum_fusion), channel_id=1, source_target_pairs={{0,16},{16,0},{1,17},{17,1},{2,18},{18,2},{3,19},{19,3},{4,20},{20... | collective-permute-start | bytes 786440 | tf_op jit(solution)/shard_map/ppermute | solution.py:578
  59.9 12.8 %collective-permute-start.4 = (bf16[32,32,128]{2,1,0:T(8,128)(2,1)S(1)}, bf16[32,32,128]{2,1,0:T(8,128)(2,1)S(1)}, u32[]{:S(2)}, u32[]{:S(2)}) collective-permute-start(bf16[32,32,128]{2,1,0:T(8,128)(2,1)S(1)} %bitcast.24), channel_id=1, source_target_pairs={{0,8},{8,0},{1,9},{9,1},{2,10},{10,2},{3,11},{11,3},{4,12},{12,4},... | collective-permute-start | bytes 786440 | tf_op jit(solution)/shard_map/ppermute | solution.py:587
  103.9 4.4 %collective-permute-start.6 = (bf16[64,128,128]{2,1,0:T(8,128)(2,1)S(1)}, bf16[64,128,128]{2,1,0:T(8,128)(2,1)S(1)}, u32[]{:S(2)}, u32[]{:S(2)}) collective-permute-start(bf16[64,128,128]{2,1,0:T(8,128)(2,1)S(1)} %get-tuple-element.40), channel_id=1, source_target_pairs={{0,4},{4,0},{1,5},{5,1},{2,6},{6,2},{3,7},{7,3},{8,12},{12,8},{9,1... | collective-permute-start | bytes 6291464 | tf_op jit(solution)/shard_map/ppermute | solution.py:599
  104.2 8.7 %collective-permute-start.7 = (bf16[32,32,128]{2,1,0:T(8,128)(2,1)S(1)}, bf16[32,32,128]{2,1,0:T(8,128)(2,1)S(1)}, u32[]{:S(2)}, u32[]{:S(2)}) collective-permute-start(bf16[32,32,128]{2,1,0:T(8,128)(2,1)S(1)} %get-tuple-element.42), channel_id=1, source_target_pairs={{0,8},{8,0},{1,9},{9,1},{2,10},{10,2},{3,11},{11,3},{4,12},{12,4},... | collective-permute-start | bytes 786440 | tf_op jit(solution)/shard_map/ppermute | solution.py:600
  108.3 12.1 %collective-permute-start.8 = (bf16[4,256,128]{2,1,0:T(8,128)(2,1)S(1)}, bf16[4,256,128]{2,1,0:T(8,128)(2,1)S(1)}, u32[]{:S(2)}, u32[]{:S(2)}) collective-permute-start(bf16[4,256,128]{2,1,0:T(8,128)(2,1)S(1)} %get-tuple-element.44), channel_id=1, source_target_pairs={{0,16},{16,0},{1,17},{17,1},{2,18},{18,2},{3,19},{19,3},{4,20},{20... | collective-permute-start | bytes 786440 | tf_op jit(solution)/shard_map/ppermute | solution.py:602
  120.4 43.9 %all-to-all-start.1 = ((bf16[64,160,128]{2,1,0:T(8,128)(2,1)}), bf16[64,160,128]{2,1,0:T(8,128)(2,1)S(1)}, u32[]{:S(2)}, u32[]{:S(2)}) async-start(bf16[64,160,128]{2,1,0:T(8,128)(2,1)} %merge.1), calls=%async_computation.1 | async-start | bytes 5242880 | tf_op jit(solution)/shard_map/all_to_all | solution.py:622
  127.8 33.5 %collective-permute-start.9 = (bf16[2,256,128]{2,1,0:T(8,128)(2,1)S(1)}, bf16[2,256,128]{2,1,0:T(8,128)(2,1)S(1)}, u32[]{:S(2)}, u32[]{:S(2)}) collective-permute-start(bf16[2,256,128]{2,1,0:T(8,128)(2,1)S(1)} %pad_maximum_fusion.1), channel_id=1, source_target_pairs={{0,32},{32,0},{64,96},{1,33},{33,1},{65,97},{2,34},{34,2},{66,98},... | collective-permute-start | bytes 393224 | tf_op jit(solution)/shard_map/ppermute | solution.py:572
  131.2 33.1 %collective-permute-start.10 = (bf16[2,256,128]{2,1,0:T(8,128)(2,1)S(1)}, bf16[2,256,128]{2,1,0:T(8,128)(2,1)S(1)}, u32[]{:S(2)}, u32[]{:S(2)}) collective-permute-start(bf16[2,256,128]{2,1,0:T(8,128)(2,1)S(1)} %pad_maximum_fusion.2), channel_id=1, source_target_pairs={{0,64},{32,96},{64,0},{1,65},{33,97},{65,1},{2,66},{34,98},{66,2},... | collective-permute-start | bytes 393224 | tf_op jit(solution)/shard_map/ppermute | solution.py:572
  136.1 28.3 %collective-permute-start.11 = (bf16[2,256,128]{2,1,0:T(8,128)(2,1)S(1)}, bf16[2,256,128]{2,1,0:T(8,128)(2,1)S(1)}, u32[]{:S(2)}, u32[]{:S(2)}) collective-permute-start(bf16[2,256,128]{2,1,0:T(8,128)(2,1)S(1)} %pad_maximum_fusion.3), channel_id=1, source_target_pairs={{0,96},{32,64},{64,32},{1,97},{33,65},{65,33},{2,98},{34,66},{66,3... | collective-permute-start | bytes 393224 | tf_op jit(solution)/shard_map/ppermute | solution.py:572

commit v5 on v3

--- a/solution.py
+++ b/solution.py
@@ -181,6 +181,8 @@
         return grad_ref[i // 2, pl.ds(start, BS)]
 
     def fill(quad, base, ref):
+        row = lax.broadcasted_iota(jnp.int32, (BS, BS), 0)
+        same = row == lax.broadcasted_iota(jnp.int32, (BS, BS), 1)
         lines = ref[quad * 4, 2 * HALF : Q_AT].astype(F32)
         for half in range(2):
             src = quad * 4 + half * 2
@@ -193,8 +195,9 @@
             kt[slot] = k_block.T
             vt[slot] = v_block.T
             dkv[slot] = jnp.zeros((BS, 2 * HD), F32)
-            shown = jnp.where(lines[half : half + 1] == 1.0, 0.0, -jnp.inf)
-            mask[slot] = jnp.broadcast_to(shown, (BS, BS)).T
+            spread = jnp.where(same, jnp.broadcast_to(lines[half : half + 1], (BS, BS)), 0.0)
+            shown = dot(spread.astype(BF16), jnp.ones((BS, BS), BF16))
+            mask[slot] = jnp.where(shown == 1.0, 0.0, -jnp.inf)
 
     for base, ref, waits in ((0, rows_ref, rows_in), (NB // 2, other_ref, other_in)):
         for k, copy in enumerate(waits):

time: 167 us -> 167 us (level)
  no operation moved by 1% of the time
where the time goes in v5:
time: 167 us; the launch traced here: 166 us
  waiting for transfers between devices  76.6 us (46%)
  Pallas kernels  42.2 us (25%)
  starting transfers between devices  42 us (25%)
  local copies, waits for them, and re-layouts  3.55 us (2%)
    ppermute x6, waiting for transfers between devices, along_x(): moved.append(lax.ppermute(piece, 'x', pairs))  56.6 us
    pallas_call x1, Pallas kernels, attend(): pl.pallas_call(attention_kernel, out_shape=(four, four, shape((NB, BACK,...  30.9 us
    ppermute x6, starting transfers between devices, along_x(): moved.append(lax.ppermute(piece, 'x', pairs))  17.2 us
    all_to_all x1, starting transfers between devices, body(): lax.all_to_all(packed, CHIPS, split_axis=0, concat_axis=0, tiled=True)  11.6 us
    all_to_all x1, starting transfers between devices, body(): back = lax.all_to_all(back, CHIPS, split_axis=0, concat_axis=0, tiled=True)  7.35 us
    ppermute x1, waiting for transfers between devices, body(): lower_came = lax.ppermute(lower, 'yl', swap)  5.19 us
    ppermute x1, waiting for transfers between devices, body(): came = lax.ppermute(jnp.stack([piece[1] for piece in grads]), 'yh', swap)  5.17 us
    ppermute x1, waiting for transfers between devices, body(): att_came = lax.ppermute(att_swap, 'yh', swap)  3.64 us
  transfers between devices with their start and end apart: 14, of which 11 were waited for; matrix products, arithmetic and copies ran while one was open for 2% of the time, Pallas kernels for 3%

profile of v5, /device:TPU:8, one launch (start us, length us, event | category | flops | bytes accessed | tf_op | source)
XLA Modules:
  0.0 166.4 jit_solution(8013852587882138881)
XLA Ops:
  0.6 0.7 pad_add_fusion.1.info_ref
  1.3 3.5 %pack.1 = bf16[64,176,128]{2,1,0:T(8,128)(2,1)} custom-call(s32[4]{0:T(128)} %pad_add_fusion.1.info_ref, s32[2]{0:T(128)} %chain_ref.1, bf16[64,3072]{1,0:T(8,128)(2,1)} %q_ref.1, bf16[64,3072]{1,0:T(8,128)(2,1)} %k_ref.1, bf16[64,3072]{1,0:T(8,128)(2,1)} %v_ref.1, s32[2,128]{1,0:T(2,128)} %bitcast.26, s32[2,16]{1,0:T(2,128)} %near_ref.1), custom_call_target="tpu_custom_call" | custom-call | tf_op jit(solution)/shard_map/pack/pallas_call | solution.py:542
  4.8 11.6 %all-to-all-start = ((bf16[64,176,128]{2,1,0:T(8,128)(2,1)}), bf16[64,176,128]{2,1,0:T(8,128)(2,1)}, u32[]{:S(2)}, u32[]{:S(2)}) async-start(bf16[64,176,128]{2,1,0:T(8,128)(2,1)} %pack.1), calls=%async_computation | async-start | bytes 5767168 | tf_op jit(solution)/shard_map/all_to_all | solution.py:561
  16.4 1.9 %pack_grad.1 = (bf16[2,256,128]{2,1,0:T(8,128)(2,1)}, bf16[2,256,128]{2,1,0:T(8,128)(2,1)}, bf16[2,256,128]{2,1,0:T(8,128)(2,1)}, bf16[2,256,128]{2,1,0:T(8,128)(2,1)}) custom-call(s32[4]{0:T(128)} %pad_add_fusion.1.info_ref, bf16[256,768]{1,0:T(8,128)(2,1)} %g_ref), custom_call_target="tpu_custom_call" | custom-call | tf_op jit(solution)/shard_map/pack_grad/pallas_call | solution.py:562
  18.3 3.5 %collective-permute-start = (bf16[2,256,128]{2,1,0:T(8,128)(2,1)}, bf16[2,256,128]{2,1,0:T(8,128)(2,1)S(1)}, u32[]{:S(2)}, u32[]{:S(2)}) collective-permute-start(bf16[2,256,128]{2,1,0:T(8,128)(2,1)} %get-tuple-element.28), channel_id=1, source_target_pairs={{0,32},{32,0},{96,64},{1,33},{33,1},{97,65},{2,34},{34,2},{98,66},... | collective-permute-start | bytes 393224 | tf_op jit(solution)/shard_map/ppermute | solution.py:575
  21.8 2.9 %collective-permute-start.1 = (bf16[2,256,128]{2,1,0:T(8,128)(2,1)}, bf16[2,256,128]{2,1,0:T(8,128)(2,1)S(1)}, u32[]{:S(2)}, u32[]{:S(2)}) collective-permute-start(bf16[2,256,128]{2,1,0:T(8,128)(2,1)} %get-tuple-element.29), channel_id=1, source_target_pairs={{0,64},{64,0},{96,32},{1,65},{65,1},{97,33},{2,66},{66,2},{98,34},... | collective-permute-start | bytes 393224 | tf_op jit(solution)/shard_map/ppermute | solution.py:575
  24.7 1.3 collective-permute-start.2
  26.0 26.1 %collective-permute-done.grad_1_hbm = bf16[2,256,128]{2,1,0:T(8,128)(2,1)S(1)} collective-permute-done((bf16[2,256,128]{2,1,0:T(8,128)(2,1)}, bf16[2,256,128]{2,1,0:T(8,128)(2,1)S(1)}, u32[]{:S(2)}, u32[]{:S(2)}) %collective-permute-start) | collective-permute-done | bytes 131104 | tf_op jit(solution)/shard_map/ppermute | solution.py:575
  52.1 1.2 collective-permute-done.1.grad_2_hbm
  53.3 2.3 %collective-permute-done.2.grad_3_hbm = bf16[2,256,128]{2,1,0:T(8,128)(2,1)S(1)} collective-permute-done((bf16[2,256,128]{2,1,0:T(8,128)(2,1)}, bf16[2,256,128]{2,1,0:T(8,128)(2,1)S(1)}, u32[]{:S(2)}, u32[]{:S(2)}) %collective-permute-start.2) | collective-permute-done | bytes 131104 | tf_op jit(solution)/shard_map/ppermute | solution.py:575
  55.6 2.1 %all-to-all-done.rows_hbm = bf16[64,176,128]{2,1,0:T(8,128)(2,1)} async-done(((bf16[64,176,128]{2,1,0:T(8,128)(2,1)}), bf16[64,176,128]{2,1,0:T(8,128)(2,1)}, u32[]{:S(2)}, u32[]{:S(2)}) %all-to-all-start) | async-done | bytes 2883616 | tf_op jit(solution)/shard_map/all_to_all | solution.py:561
  57.7 0.8 slice.46
  58.7 1.1 slice.59
  59.9 1.7 %collective-permute-start.4 = (bf16[32,32,128]{2,1,0:T(8,128)(2,1)S(1)}, bf16[32,32,128]{2,1,0:T(8,128)(2,1)S(1)}, u32[]{:S(2)}, u32[]{:S(2)}) collective-permute-start(bf16[32,32,128]{2,1,0:T(8,128)(2,1)S(1)} %bitcast.24), channel_id=1, source_target_pairs={{0,8},{8,0},{1,9},{9,1},{2,10},{10,2},{3,11},{11,3},{4,12},{12,4},... | collective-permute-start | bytes 786440 | tf_op jit(solution)/shard_map/ppermute | solution.py:590
  61.6 0.8 slice_bitcast_fusion.2
  62.7 0.7 collective-permute-done.3.other_hbm
  63.3 0.8 slice_bitcast_fusion
  64.1 5.2 %collective-permute-done.5.grad_came_hbm = bf16[4,256,128]{2,1,0:T(8,128)(2,1)S(1)} collective-permute-done((bf16[4,256,128]{2,1,0:T(8,128)(2,1)S(1)}, bf16[4,256,128]{2,1,0:T(8,128)(2,1)S(1)}, u32[]{:S(2)}, u32[]{:S(2)}) %collective-permute-start.5) | collective-permute-done | bytes 262176 | tf_op jit(solution)/shard_map/ppermute | solution.py:581
  69.3 3.3 %collective-permute-done.4.lower_hbm = bf16[32,32,128]{2,1,0:T(8,128)(2,1)S(1)} collective-permute-done((bf16[32,32,128]{2,1,0:T(8,128)(2,1)S(1)}, bf16[32,32,128]{2,1,0:T(8,128)(2,1)S(1)}, u32[]{:S(2)}, u32[]{:S(2)}) %collective-permute-start.4) | collective-permute-done | bytes 262176 | tf_op jit(solution)/shard_map/ppermute | solution.py:590
  72.7 30.9 %attention.1 = (bf16[4,256,128]{2,1,0:T(8,128)(2,1)S(1)}, bf16[4,256,128]{2,1,0:T(8,128)(2,1)S(1)}, bf16[64,160,128]{2,1,0:T(8,128)(2,1)}, bf16[64,128,128]{2,1,0:T(8,128)(2,1)S(1)}, bf16[32,32,128]{2,1,0:T(8,128)(2,1)S(1)}) custom-call(s32[4]{0:T(128)S(1)} %copy-done.1, s32[32,32]{1,0:T(8,128)S(1)} %bitcast.23, s32[128,128]{1,0:T(8,128)S(1)} %convert.1.lists_ref, ...), custom_call_target="tpu_custom_call" | custom-call | tf_op jit(solution)/shard_map/attention/pallas_call | solution.py:494
  103.7 0.8 collective-permute-start.7
  104.4 3.2 %collective-permute-start.8 = (bf16[4,256,128]{2,1,0:T(8,128)(2,1)S(1)}, bf16[4,256,128]{2,1,0:T(8,128)(2,1)S(1)}, u32[]{:S(2)}, u32[]{:S(2)}) collective-permute-start(bf16[4,256,128]{2,1,0:T(8,128)(2,1)S(1)} %get-tuple-element.40), channel_id=1, source_target_pairs={{0,16},{16,0},{1,17},{17,1},{2,18},{18,2},{3,19},{19,3},{4,20},{20... | collective-permute-start | bytes 786440 | tf_op jit(solution)/shard_map/ppermute | solution.py:604
  107.7 5.2 %collective-permute-done.7.lower_hbm = bf16[32,32,128]{2,1,0:T(8,128)(2,1)S(1)} collective-permute-done((bf16[32,32,128]{2,1,0:T(8,128)(2,1)S(1)}, bf16[32,32,128]{2,1,0:T(8,128)(2,1)S(1)}, u32[]{:S(2)}, u32[]{:S(2)}) %collective-permute-start.7) | collective-permute-done | bytes 262176 | tf_op jit(solution)/shard_map/ppermute | solution.py:603
  112.9 3.4 %merge.1 = bf16[64,160,128]{2,1,0:T(8,128)(2,1)} custom-call(s32[4]{0:T(128)S(1)} %copy-done.1, bf16[64,160,128]{2,1,0:T(8,128)(2,1)} %get-tuple-element.36.back_hbm, bf16[64,128,128]{2,1,0:T(8,128)(2,1)S(1)} %collective-permute-done.6.came_hbm, bf16[32,32,128]{2,1,0:T(8,128)(2,1)S(1)} %collective-permute-done.7.lower_hbm), custom_call_target="tpu_custom_call", output_to_operand_aliasing={{}: (1, {})} | custom-call | tf_op jit(solution)/shard_map/merge/pallas_call | solution.py:606
  116.2 3.6 %collective-permute-done.8.came_hbm = bf16[4,256,128]{2,1,0:T(8,128)(2,1)S(1)} collective-permute-done((bf16[4,256,128]{2,1,0:T(8,128)(2,1)S(1)}, bf16[4,256,128]{2,1,0:T(8,128)(2,1)S(1)}, u32[]{:S(2)}, u32[]{:S(2)}) %collective-permute-start.8) | collective-permute-done | bytes 262176 | tf_op jit(solution)/shard_map/ppermute | solution.py:604
  119.9 7.4 %all-to-all-start.1 = ((bf16[64,160,128]{2,1,0:T(8,128)(2,1)}), bf16[64,160,128]{2,1,0:T(8,128)(2,1)S(1)}, u32[]{:S(2)}, u32[]{:S(2)}) async-start(bf16[64,160,128]{2,1,0:T(8,128)(2,1)} %merge.1), calls=%async_computation.1 | async-start | bytes 5242880 | tf_op jit(solution)/shard_map/all_to_all | solution.py:624
  127.3 3.4 %collective-permute-start.9 = (bf16[2,256,128]{2,1,0:T(8,128)(2,1)S(1)}, bf16[2,256,128]{2,1,0:T(8,128)(2,1)S(1)}, u32[]{:S(2)}, u32[]{:S(2)}) collective-permute-start(bf16[2,256,128]{2,1,0:T(8,128)(2,1)S(1)} %pad_maximum_fusion.1), channel_id=1, source_target_pairs={{0,32},{32,0},{64,96},{1,33},{33,1},{65,97},{2,34},{34,2},{66,98},... | collective-permute-start | bytes 393224 | tf_op jit(solution)/shard_map/ppermute | solution.py:575
  130.7 4.8 %collective-permute-start.10 = (bf16[2,256,128]{2,1,0:T(8,128)(2,1)S(1)}, bf16[2,256,128]{2,1,0:T(8,128)(2,1)S(1)}, u32[]{:S(2)}, u32[]{:S(2)}) collective-permute-start(bf16[2,256,128]{2,1,0:T(8,128)(2,1)S(1)} %pad_maximum_fusion.2), channel_id=1, source_target_pairs={{0,64},{32,96},{64,0},{1,65},{33,97},{65,1},{2,66},{34,98},{66,2},... | collective-permute-start | bytes 393224 | tf_op jit(solution)/shard_map/ppermute | solution.py:575
  135.6 1.3 collective-permute-start.11
  136.9 23.9 %collective-permute-done.9.one_hbm = bf16[2,256,128]{2,1,0:T(8,128)(2,1)S(1)} collective-permute-done((bf16[2,256,128]{2,1,0:T(8,128)(2,1)S(1)}, bf16[2,256,128]{2,1,0:T(8,128)(2,1)S(1)}, u32[]{:S(2)}, u32[]{:S(2)}) %collective-permute-start.9) | collective-permute-done | bytes 131104 | tf_op jit(solution)/shard_map/ppermute | solution.py:575
  160.8 3.0 %collective-permute-done.10.two_hbm = bf16[2,256,128]{2,1,0:T(8,128)(2,1)S(1)} collective-permute-done((bf16[2,256,128]{2,1,0:T(8,128)(2,1)S(1)}, bf16[2,256,128]{2,1,0:T(8,128)(2,1)S(1)}, u32[]{:S(2)}, u32[]{:S(2)}) %collective-permute-start.10) | collective-permute-done | bytes 131104 | tf_op jit(solution)/shard_map/ppermute | solution.py:575
  163.8 2.5 %unpack.1 = (bf16[64,3072]{1,0:T(8,128)(2,1)}, bf16[64,3072]{1,0:T(8,128)(2,1)}, bf16[64,3072]{1,0:T(8,128)(2,1)}, bf16[256,768]{1,0:T(8,128)(2,1)}) custom-call(s32[4]{0:T(128)S(1)} %copy-done.1, bf16[64,160,128]{2,1,0:T(8,128)(2,1)S(1)} %all-to-all-done.1.rows_hbm, bf16[4,256,128]{2,1,0:T(8,128)(2,1)S(1)} %get-tuple-element.42.keep_hbm, ...), custom_call_target="tpu_custom_call" | custom-call | tf_op jit(solution)/shard_map/unpack/pallas_call | solution.py:627
  (26 shorter events, 0.7 us)
Async XLA Ops:
  4.8 52.9 %all-to-all-start = ((bf16[64,176,128]{2,1,0:T(8,128)(2,1)}), bf16[64,176,128]{2,1,0:T(8,128)(2,1)}, u32[]{:S(2)}, u32[]{:S(2)}) async-start(bf16[64,176,128]{2,1,0:T(8,128)(2,1)} %pack.1), calls=%async_computation | async-start | bytes 5767168 | tf_op jit(solution)/shard_map/all_to_all | solution.py:561
  16.4 56.3 %copy-start.1 = (s32[4]{0:T(128)S(1)}, s32[4]{0:T(128)}, u32[]{:S(2)}) copy-start(s32[4]{0:T(128)} %pad_add_fusion.1.info_ref) | copy-start | bytes 52
  16.4 56.3 %copy-start.2 = (f32[6]{0:T(128)S(1)}, f32[6]{0:T(128)}, u32[]{:S(2)}) copy-start(f32[6]{0:T(128)} %bias_ref.1) | copy-start | bytes 76
  18.3 54.4 %copy-start = (bf16[2,256,128]{2,1,0:T(8,128)(2,1)S(1)}, bf16[2,256,128]{2,1,0:T(8,128)(2,1)}, u32[]{:S(2)}) copy-start(bf16[2,256,128]{2,1,0:T(8,128)(2,1)} %get-tuple-element.32.grad_0_hbm) | copy-start | bytes 393220
  18.3 33.8 %collective-permute-start = (bf16[2,256,128]{2,1,0:T(8,128)(2,1)}, bf16[2,256,128]{2,1,0:T(8,128)(2,1)S(1)}, u32[]{:S(2)}, u32[]{:S(2)}) collective-permute-start(bf16[2,256,128]{2,1,0:T(8,128)(2,1)} %get-tuple-element.28), channel_id=1, source_target_pairs={{0,32},{32,0},{96,64},{1,33},{33,1},{97,65},{2,34},{34,2},{98,66},... | collective-permute-start | bytes 393224 | tf_op jit(solution)/shard_map/ppermute | solution.py:575
  21.8 31.5 %collective-permute-start.1 = (bf16[2,256,128]{2,1,0:T(8,128)(2,1)}, bf16[2,256,128]{2,1,0:T(8,128)(2,1)S(1)}, u32[]{:S(2)}, u32[]{:S(2)}) collective-permute-start(bf16[2,256,128]{2,1,0:T(8,128)(2,1)} %get-tuple-element.29), channel_id=1, source_target_pairs={{0,64},{64,0},{96,32},{1,65},{65,1},{97,33},{2,66},{66,2},{98,34},... | collective-permute-start | bytes 393224 | tf_op jit(solution)/shard_map/ppermute | solution.py:575
  24.7 30.9 %collective-permute-start.2 = (bf16[2,256,128]{2,1,0:T(8,128)(2,1)}, bf16[2,256,128]{2,1,0:T(8,128)(2,1)S(1)}, u32[]{:S(2)}, u32[]{:S(2)}) collective-permute-start(bf16[2,256,128]{2,1,0:T(8,128)(2,1)} %get-tuple-element.30), channel_id=1, source_target_pairs={{32,64},{64,32},{96,0},{33,65},{65,33},{97,1},{34,66},{66,34},{98,... | collective-permute-start | bytes 393224 | tf_op jit(solution)/shard_map/ppermute | solution.py:575
  57.7 5.6 %collective-permute-start.3 = (bf16[64,176,128]{2,1,0:T(8,128)(2,1)}, bf16[64,176,128]{2,1,0:T(8,128)(2,1)}, u32[]{:S(2)}, u32[]{:S(2)}) collective-permute-start(bf16[64,176,128]{2,1,0:T(8,128)(2,1)} %all-to-all-done.rows_hbm), channel_id=1, source_target_pairs={{0,4},{4,0},{1,5},{5,1},{2,6},{6,2},{3,7},{7,3},{8,12},{12,8},{9,1... | collective-permute-start | bytes 8650760 | tf_op jit(solution)/shard_map/ppermute | solution.py:583
  58.6 10.7 %collective-permute-start.5 = (bf16[4,256,128]{2,1,0:T(8,128)(2,1)S(1)}, bf16[4,256,128]{2,1,0:T(8,128)(2,1)S(1)}, u32[]{:S(2)}, u32[]{:S(2)}) collective-permute-start(bf16[4,256,128]{2,1,0:T(8,128)(2,1)S(1)} %pad_maximum_fusion), channel_id=1, source_target_pairs={{0,16},{16,0},{1,17},{17,1},{2,18},{18,2},{3,19},{19,3},{4,20},{20... | collective-permute-start | bytes 786440 | tf_op jit(solution)/shard_map/ppermute | solution.py:581
  59.9 12.8 %collective-permute-start.4 = (bf16[32,32,128]{2,1,0:T(8,128)(2,1)S(1)}, bf16[32,32,128]{2,1,0:T(8,128)(2,1)S(1)}, u32[]{:S(2)}, u32[]{:S(2)}) collective-permute-start(bf16[32,32,128]{2,1,0:T(8,128)(2,1)S(1)} %bitcast.24), channel_id=1, source_target_pairs={{0,8},{8,0},{1,9},{9,1},{2,10},{10,2},{3,11},{11,3},{4,12},{12,4},... | collective-permute-start | bytes 786440 | tf_op jit(solution)/shard_map/ppermute | solution.py:590
  103.6 9.3 %collective-permute-start.6 = (bf16[64,128,128]{2,1,0:T(8,128)(2,1)S(1)}, bf16[64,128,128]{2,1,0:T(8,128)(2,1)S(1)}, u32[]{:S(2)}, u32[]{:S(2)}) collective-permute-start(bf16[64,128,128]{2,1,0:T(8,128)(2,1)S(1)} %get-tuple-element.37), channel_id=1, source_target_pairs={{0,4},{4,0},{1,5},{5,1},{2,6},{6,2},{3,7},{7,3},{8,12},{12,8},{9,1... | collective-permute-start | bytes 6291464 | tf_op jit(solution)/shard_map/ppermute | solution.py:602
  103.7 9.2 %collective-permute-start.7 = (bf16[32,32,128]{2,1,0:T(8,128)(2,1)S(1)}, bf16[32,32,128]{2,1,0:T(8,128)(2,1)S(1)}, u32[]{:S(2)}, u32[]{:S(2)}) collective-permute-start(bf16[32,32,128]{2,1,0:T(8,128)(2,1)S(1)} %get-tuple-element.38), channel_id=1, source_target_pairs={{0,8},{8,0},{1,9},{9,1},{2,10},{10,2},{3,11},{11,3},{4,12},{12,4},... | collective-permute-start | bytes 786440 | tf_op jit(solution)/shard_map/ppermute | solution.py:603
  104.4 15.5 %collective-permute-start.8 = (bf16[4,256,128]{2,1,0:T(8,128)(2,1)S(1)}, bf16[4,256,128]{2,1,0:T(8,128)(2,1)S(1)}, u32[]{:S(2)}, u32[]{:S(2)}) collective-permute-start(bf16[4,256,128]{2,1,0:T(8,128)(2,1)S(1)} %get-tuple-element.40), channel_id=1, source_target_pairs={{0,16},{16,0},{1,17},{17,1},{2,18},{18,2},{3,19},{19,3},{4,20},{20... | collective-permute-start | bytes 786440 | tf_op jit(solution)/shard_map/ppermute | solution.py:604
  119.9 43.9 %all-to-all-start.1 = ((bf16[64,160,128]{2,1,0:T(8,128)(2,1)}), bf16[64,160,128]{2,1,0:T(8,128)(2,1)S(1)}, u32[]{:S(2)}, u32[]{:S(2)}) async-start(bf16[64,160,128]{2,1,0:T(8,128)(2,1)} %merge.1), calls=%async_computation.1 | async-start | bytes 5242880 | tf_op jit(solution)/shard_map/all_to_all | solution.py:624
  127.3 33.5 %collective-permute-start.9 = (bf16[2,256,128]{2,1,0:T(8,128)(2,1)S(1)}, bf16[2,256,128]{2,1,0:T(8,128)(2,1)S(1)}, u32[]{:S(2)}, u32[]{:S(2)}) collective-permute-start(bf16[2,256,128]{2,1,0:T(8,128)(2,1)S(1)} %pad_maximum_fusion.1), channel_id=1, source_target_pairs={{0,32},{32,0},{64,96},{1,33},{33,1},{65,97},{2,34},{34,2},{66,98},... | collective-permute-start | bytes 393224 | tf_op jit(solution)/shard_map/ppermute | solution.py:575
  130.7 33.1 %collective-permute-start.10 = (bf16[2,256,128]{2,1,0:T(8,128)(2,1)S(1)}, bf16[2,256,128]{2,1,0:T(8,128)(2,1)S(1)}, u32[]{:S(2)}, u32[]{:S(2)}) collective-permute-start(bf16[2,256,128]{2,1,0:T(8,128)(2,1)S(1)} %pad_maximum_fusion.2), channel_id=1, source_target_pairs={{0,64},{32,96},{64,0},{1,65},{33,97},{65,1},{2,66},{34,98},{66,2},... | collective-permute-start | bytes 393224 | tf_op jit(solution)/shard_map/ppermute | solution.py:575
  135.6 28.3 %collective-permute-start.11 = (bf16[2,256,128]{2,1,0:T(8,128)(2,1)S(1)}, bf16[2,256,128]{2,1,0:T(8,128)(2,1)S(1)}, u32[]{:S(2)}, u32[]{:S(2)}) collective-permute-start(bf16[2,256,128]{2,1,0:T(8,128)(2,1)S(1)} %pad_maximum_fusion.3), channel_id=1, source_target_pairs={{0,96},{32,64},{64,32},{1,97},{33,65},{65,33},{2,98},{34,66},{66,3... | collective-permute-start | bytes 393224 | tf_op jit(solution)/shard_map/ppermute | solution.py:575
